TPU v7x, 256 devices: a whole 4x4x8 slice. The times are simulated.
256 devices in a mesh: dp: 16 (over x_hi, y, core), shard: 16 (over x_lo, z).
Axes of the slice: x: 4 (x_hi: 2, x_lo: 2; x = x_hi * 2 + x_lo), y: 4, z: 8, core: 2. Of those that a mesh axis runs over, the one named last changes fastest.
Arguments:
- tokens: bfloat16 [40960, 16384], P(('dp', 'shard')), may hold values from -24 to 24
- rotated_key_gradient: bfloat16 [40960, 512], P(('dp', 'shard')), may hold values from -6 to 6
- document_numbers: int32 [16, 2560], P('dp', 'shard'), may hold values from 0 to 15, never falling along the last dimension, each value on 1 to 640 neighbouring positions
- frozen_base_levels: bfloat16 [16384, 512], P('shard'), may hold values from -1 to 1
- first_level_scales: bfloat16 [256, 512], P('shard'), may hold values from 0.5 to 2
- second_level_scales: float32 [1, 512], replicated, may hold values from 0.01 to 0.03
- adapter_down_matrix: bfloat16 [16384, 64], P('shard'), may hold values from -0.046875 to 0.046875
- adapter_up_matrix: bfloat16 [64, 512], replicated, may hold values from -0.75 to 0.75
Outputs:
- grad_tokens: bfloat16 [40960, 16384], P(('dp', 'shard'))
- grad_down: float32 [16384, 64], P('shard')
- grad_up: float32 [64, 512], replicated
Inputs may be any that keep to these rules, and one draw needn't show every extreme that they name: `document_numbers`: along each packed sequence the ids never fall; every id of 0 to 15 appears, each on at most 640 consecutive places, and some id on exactly that many.
All inputs are finite; a program needn't handle non-finite values.
Results may differ from a plain program's by a relative error of at most 0.0056.
Values may be sent and summed in bfloat16 or wider, within the bound.
No kernel may reach another device: no remote copies, remote signals or barrier semaphores. Data moves between devices by JAX's collectives and lax.ppermute only.
A program may use at most 128 MiB of HBM per device.

v0:
```python
import jax
import jax.numpy as jnp
from jax import lax
from jax.sharding import PartitionSpec as P

HEAD = 128
ADAPTER_RANK = 64
BLOCK = 64
SGROUP = 256
SEGS = 16


rope_base = 500000.0


def prefix(array, axis, combine, identity):
    length, position = (lax.axis_size(axis), lax.axis_index(axis))
    everything = lax.all_gather(array, axis)
    start = jnp.broadcast_to(jnp.asarray(identity, array.dtype), array.shape)

    def step(k, before):
        reached = k < position
        new = combine(before, everything[k])
        return jnp.where(reached, new, before)

    return lax.fori_loop(0, length, step, start)


def unrotate(input_gradients, position):
    token_row_list = input_gradients.shape[0]
    shaped = input_gradients.astype(jnp.float32).reshape(token_row_list, -1, HEAD)
    half = HEAD // 2
    freqs = rope_base ** (-jnp.arange(half, dtype=jnp.float32) * 2.0 / HEAD)
    angle = position.astype(jnp.float32)[:, None, None] * freqs[None, None, :]
    cosine = jnp.cos(angle)
    sine = jnp.sin(angle)
    first = shaped[..., :half]
    second = shaped[..., half:]
    out_first = first * cosine + second * sine
    out_second = second * cosine - first * sine
    return (
        jnp.concatenate([out_first, out_second], -1)
        .reshape(token_row_list, -1)
        .astype(jnp.bfloat16)
    )


def add_counts(earlier, later):
    return earlier + later


def dequantize(weight_levels, scales_one, second_level_scales):
    token_row_list = weight_levels.shape[0]
    blocks = token_row_list // BLOCK
    scaled = (
        weight_levels.astype(jnp.float32).reshape(blocks, BLOCK, -1)
        * scales_one.astype(jnp.float32)[:, None, :]
    )
    group_index = jnp.arange(blocks, dtype=jnp.int32) // SGROUP
    picker = (
        group_index[:, None] == jnp.arange(second_level_scales.shape[0], dtype=jnp.int32)[None, :]
    ).astype(jnp.float32)
    per_block = jnp.dot(picker, second_level_scales, precision=lax.Precision.HIGHEST)
    return (scaled * per_block[:, None, :]).reshape(token_row_list, -1).astype(jnp.bfloat16)


def on_device(
    tokens,
    rotated_key_gradient,
    document_numbers,
    frozen_base_levels,
    first_level_scales,
    second_level_scales,
    adapter_down_matrix,
    adapter_up_matrix,
):
    adapter_scale = 16.0 / ADAPTER_RANK
    token_row_list = tokens.shape[0]
    all_tokens = token_row_list * lax.axis_size("dp") * lax.axis_size("shard")
    segment_row = document_numbers[0]
    marks = jnp.arange(SEGS, dtype=jnp.int32)
    onehot = (segment_row[:, None] == marks[None, :]).astype(jnp.int32)
    local_counts = jnp.sum(onehot, axis=0)
    lower_counts = prefix(local_counts, "shard", add_counts, jnp.zeros_like(local_counts))
    counts = lower_counts + local_counts
    before = jnp.cumsum(counts) - counts
    first = jnp.sum(onehot * before[None, :], axis=-1)
    position = (
        lax.axis_index("shard") * token_row_list
        + jnp.arange(token_row_list, dtype=jnp.int32)
        - first
    )
    input_gradients = unrotate(rotated_key_gradient, position)
    reduced_gradient = jnp.dot(
        input_gradients, adapter_up_matrix.T, preferred_element_type=jnp.float32
    ).astype(jnp.bfloat16)
    weight_levels = lax.all_gather(frozen_base_levels, "shard", axis=0, tiled=True)
    scales_one = lax.all_gather(first_level_scales, "shard", axis=0, tiled=True)
    adapter_token_rows = lax.all_gather(adapter_down_matrix, "shard", axis=0, tiled=True)
    weight = dequantize(weight_levels, scales_one, second_level_scales)
    frozen_base_term = jnp.einsum(
        "tk,dk->td", input_gradients, weight, preferred_element_type=jnp.float32
    )
    adapter_term = jnp.einsum(
        "nh,sh->ns", reduced_gradient, adapter_token_rows, preferred_element_type=jnp.float32
    )
    feature_columns = frozen_base_term + adapter_scale * adapter_term
    inputs = tokens
    lowered = jnp.dot(inputs, adapter_token_rows, preferred_element_type=jnp.float32)
    feature_columns, lowered = (feature_columns, lowered)
    grad_tokens = feature_columns.astype(jnp.bfloat16)
    reduced_tokens = lowered.astype(jnp.bfloat16)
    inputs = tokens
    down_sequence = lax.psum_scatter(
        jnp.einsum("td,tr->dr", inputs, reduced_gradient, preferred_element_type=jnp.float32),
        "shard",
        scatter_dimension=0,
        tiled=True,
    )
    up_local = jnp.einsum(
        "tr,tk->rk", reduced_tokens, input_gradients, preferred_element_type=jnp.float32
    )
    down_sum = lax.psum(down_sequence, "dp")
    up_sum = lax.psum(up_local, ("dp", "shard"))
    factor = adapter_scale / jnp.sqrt(jnp.float32(all_tokens))
    return (grad_tokens, factor * down_sum, factor * up_sum)


def solution(mesh):
    in_specs = (
        P(("dp", "shard"), None),
        P(("dp", "shard"), None),
        P("dp", "shard"),
        P("shard", None),
        P("shard", None),
        P(),
        P("shard", None),
        P(),
    )
    out_specs = (P(("dp", "shard"), None), P("shard", None), P())
    return jax.shard_map(
        on_device, mesh=mesh, in_specs=in_specs, out_specs=out_specs, check_vma=False
    )
```

profile of v0, /device:TPU:1, one launch (start us, length us, event | category | flops | bytes accessed | tf_op | source)
XLA Modules:
  0.0 785.4 jit_solution(16017803261360904684)
XLA Ops:
  7.2 0.0 copy-start
  7.2 0.0 all-gather.6.cloned.1.call-start
  7.2 0.7 all-gather.6.cloned.1.call-update
  7.9 0.0 reduce-scatter.2.cloned.1.call-start
  8.0 1.0 reshape.132
  9.0 0.8 convert_reduce_fusion
  9.8 1.3 dynamic-slice
  11.7 0.2 dynamic-update-slice
  12.0 16.7 %all-reduce = s32[256]{0:T(256)S(1)} all-reduce(s32[256]{0:T(256)S(1)} %dynamic-update-slice), channel_id=2, replica_groups=mesh['dp'=16,'shard'=16] {'shard'}, use_global_device_ids=true, to_apply=%add | all-reduce | flops 256 | bytes 2048
  28.6 0.1 reshape.133
  28.7 0.6 while.14
  29.4 0.1 copy.13
  29.5 0.1 reduce
  29.6 0.8 select_reduce_fusion
  30.4 0.4 multiply_cosine_fusion
  30.8 0.3 add_convert_fusion
  31.1 0.2 pad_maximum_fusion
  31.4 0.0 copy-done
  31.4 0.2 convolution_convert_fusion.1
  31.5 5.4 convolution_bitcast_fusion
  36.9 0.0 reduce-scatter.2.cloned.1.call-update
  37.0 0.0 copy-start.2
  37.0 0.0 copy-start.3
  37.0 0.0 all-reduce.6.cloned.1.call-start
  37.0 38.9 %all-gather.6.cloned.1.call-done = bf16[16384,64]{0,1:T(8,128)(2,1)} async-done(((bf16[1024,64]{0,1:T(8,128)(2,1)}), bf16[16384,64]{0,1:T(8,128)(2,1)}) %all-gather.6.cloned.1.call-update) | async-done | bytes 2097168 | tf_op jit(solution)/shard_map/all_gather | solution.py:99
  75.9 5.8 fusion.3
  81.8 0.0 all-reduce.6.cloned.1.call-update
  81.8 0.0 all-reduce.4.cloned.1.call-start
  81.9 73.2 %reduce-scatter.2.cloned.1.call-done = f32[1024,64]{0,1:T(8,128)} async-done(((f32[16384,64]{0,1:T(8,128)}), f32[1024,64]{0,1:T(8,128)}) %reduce-scatter.2.cloned.1.call-update) | async-done | bytes 262160 | tf_op jit(solution)/shard_map/reduce_scatter | solution.py:114
  155.1 0.0 all-reduce.4.cloned.1.call-update
  155.1 0.0 all-gather.4.cloned.1.call-start
  155.2 0.5 all-gather.4.cloned.1.call-update
  155.7 0.0 copy-done.2
  155.7 25.9 %all_gather.18 = bf16[256,512]{1,0:T(8,128)(2,1)S(1)} all-gather(bf16[16,512]{1,0:T(8,128)(2,1)S(1)} %copy-done.2), channel_id=1, replica_groups=mesh['dp'=16,'shard'=16] {'shard'}, dimensions={0}, use_global_device_ids=true | all-gather | bytes 278528 | tf_op jit(solution)/shard_map/all_gather | solution.py:98
  181.6 0.1 convert_element_type.38
  181.7 0.0 copy-done.3
  181.7 0.1 broadcast_multiply_fusion
  181.8 227.7 %all-reduce.6.cloned.1.call-done = f32[64,512]{1,0:T(8,128)} async-done(((f32[64,512]{1,0:T(8,128)}), f32[64,512]{1,0:T(8,128)}) %all-reduce.6.cloned.1.call-update) | async-done | bytes 131088 | tf_op jit(solution)/shard_map/psum | solution.py:124
  409.5 1.6 broadcast_multiply_fusion.2
  411.1 141.0 %all-reduce.4.cloned.1.call-done = f32[1024,64]{0,1:T(8,128)} async-done(((f32[1024,64]{0,1:T(8,128)}), f32[1024,64]{0,1:T(8,128)}) %all-reduce.4.cloned.1.call-update) | async-done | bytes 262160 | tf_op jit(solution)/shard_map/psum | solution.py:123
  552.1 1.7 broadcast_multiply_fusion.1
  553.8 186.5 %all-gather.4.cloned.1.call-done = bf16[16384,512]{1,0:T(8,128)(2,1)} async-done(((bf16[1024,512]{1,0:T(8,128)(2,1)}), bf16[16384,512]{1,0:T(8,128)(2,1)}) %all-gather.4.cloned.1.call-update) | async-done | bytes 16777232 | tf_op jit(solution)/shard_map/all_gather | solution.py:97
  740.3 15.2 %fusion = bf16[16384,512]{1,0:T(8,128)(2,1)} fusion(bf16[16384,512]{1,0:T(8,128)(2,1)} %all-gather.4.cloned.1.call-done, f32[256,512]{1,0:T(8,128)S(1)} %broadcast_multiply_fusion, f32[256,512]{1,0:T(8,128)S(1)} %convert_element_type.38), kind=kLoop, calls=%fused_computation.3 | loop fusion | flops 33554432 | bytes 34603008 | tf_op jit(solution)/shard_map/convert_element_type | solution.py:64
  755.5 0.0 copy-start.1
  755.5 15.5 %fusion.6 = f32[160,16384]{1,0:T(8,128)} fusion(bf16[16384,512]{1,0:T(8,128)(2,1)} %fusion, bf16[20,8,4,128]{3,2,1,0:T(4,128)(2,1)S(1)} %bitcast.36), kind=kOutput, calls=%fused_computation.17 | convolution fusion | flops 2684354560 | bytes 27426816 | tf_op jit(solution)/shard_map/tk,dk->td/dot_general | solution.py:101
  771.0 0.0 copy-done.1
  771.0 7.9 %fusion.2 = bf16[160,16384]{1,0:T(8,128)(2,1)} fusion(f32[160,16384]{1,0:T(8,128)} %fusion.6, bf16[160,64]{0,1:T(8,128)(2,1)S(1)} %convolution_convert_fusion.1, bf16[16384,64]{0,1:T(8,128)(2,1)S(1)} %copy-done.1), kind=kOutput, calls=%fused_computation.7 | convolution fusion | flops 343408640 | bytes 17846272 | tf_op jit(solution)/shard_map/nh,sh->ns/dot_general | solution.py:104
  (24 shorter events, 0.4 us)
Async XLA Ops:
  7.2 24.2 %copy-start = (bf16[64,512]{1,0:T(8,128)(2,1)S(1)}, bf16[64,512]{1,0:T(8,128)(2,1)}, u32[]{:S(2)}) copy-start(bf16[64,512]{1,0:T(8,128)(2,1)} %param.17) | copy-start | bytes 196612
  7.2 68.8 %all-gather.6.cloned.1.call-start = ((), (), s32[]{:S(2)}) async-start(), calls=%async_computation.2 | async-start | bytes 2228224 | tf_op jit(solution)/shard_map/all_gather | solution.py:99
  7.9 147.2 %reduce-scatter.2.cloned.1.call-start = ((), (), s32[]{:S(2)}) async-start(), calls=%async_computation.3 | async-start | bytes 4456448 | tf_op jit(solution)/shard_map/reduce_scatter | solution.py:114
  37.0 118.8 %copy-start.2 = (bf16[16,512]{1,0:T(8,128)(2,1)S(1)}, bf16[16,512]{1,0:T(8,128)(2,1)}, u32[]{:S(2)}) copy-start(bf16[16,512]{1,0:T(8,128)(2,1)} %param.14) | copy-start | bytes 49156
  37.0 144.7 %copy-start.3 = (f32[1,512]{1,0:T(1,128)S(1)}, f32[1,512]{1,0:T(1,128)}, u32[]{:S(2)}) copy-start(f32[1,512]{1,0:T(1,128)} %param.15) | copy-start | bytes 6148
  37.0 372.5 %all-reduce.6.cloned.1.call-start = ((), (), s32[]{:S(2)}) async-start(), calls=%async_computation.5 | async-start | bytes 262144 | tf_op jit(solution)/shard_map/psum | solution.py:124
  81.8 470.3 %all-reduce.4.cloned.1.call-start = ((), (), s32[]{:S(2)}) async-start(), calls=%async_computation.4 | async-start | bytes 524288 | tf_op jit(solution)/shard_map/psum | solution.py:123
  155.1 585.2 %all-gather.4.cloned.1.call-start = ((), (), s32[]{:S(2)}) async-start(), calls=%async_computation.1 | async-start | bytes 17825792 | tf_op jit(solution)/shard_map/all_gather | solution.py:97
  755.5 15.5 %copy-start.1 = (bf16[16384,64]{0,1:T(8,128)(2,1)S(1)}, bf16[16384,64]{0,1:T(8,128)(2,1)}, u32[]{:S(2)}) copy-start(bf16[16384,64]{0,1:T(8,128)(2,1)} %all-gather.6.cloned.1.call-done) | copy-start | bytes 6291460
Sparse Core Ops, SparseCore 0:
  9.8 66.0 all-gather.5
  79.1 76.0 reduce-scatter.1
  161.2 248.2 all-reduce.5
  412.0 140.0 all-reduce.3
  553.9 186.3 all-gather.3
where the time goes:
time: 786 us; the launch traced here: 785 us
  waiting for transfers between devices  669 us (85%)
  blocking collectives  42.6 us (5%)
  matrix products  34.8 us (4%)
  other arithmetic  21.6 us (3%)
  between operations  14.6 us (2%)
    psum x1, waiting for transfers between devices, on_device(): up_sum = lax.psum(up_local, ('dp', 'shard'))  228 us
    all_gather x1, waiting for transfers between devices, on_device(): lax.all_gather(frozen_base_levels, 'shard', axis=0, tiled=True)  187 us
    psum x1, waiting for transfers between devices, on_device(): down_sum = lax.psum(down_sequence, 'dp')  141 us
    reduce_scatter x1, waiting for transfers between devices, on_device(): lax.psum_scatter(jnp.einsum('td,tr->dr', inputs, reduced_gradient, prefer...  73.2 us
    all_gather x1, waiting for transfers between devices, on_device(): lax.all_gather(adapter_down_matrix, 'shard', axis=0, tiled=True)  38.9 us
    all_gather x1, blocking collectives, on_device(): scales_one = lax.all_gather(first_level_scales, 'shard', axis=0, tiled=True)  25.9 us
    unnamed x1, blocking collectives  16.7 us
  transfers between devices with their start and end apart: 5, of which 5 were waited for; matrix products, arithmetic and copies ran while one was open for 3% of the time, Pallas kernels for 0%

commit v1 on v0

v1 whole, which is shorter than its diff:
```python
import functools

import jax
import jax.numpy as jnp
from jax import lax
from jax.experimental import pallas as pl
from jax.experimental.pallas import tpu as pltpu
from jax.sharding import Mesh, PartitionSpec as P

HEAD = 128
RANK = 64
BLOCK = 64
WIDTH = 16384
KEYS = 512
ROWS = 160
SHARDS = 16
NZ = 8
HALF = 512
QUART = 256
ROPE_BASE = 500000.0
SCALE = 16.0 / RANK
TOKENS = 40960

BF = jnp.bfloat16
F32 = jnp.float32

X_AXES = ("xh", "c", "xl")
SHARD_AXES = ("xl", "z")
DP_AXES = ("xh", "y", "c")


def params(mib):
    return pltpu.CompilerParams(vmem_limit_bytes=mib * 1024 * 1024)


def dot(a, b, ca, cb):
    return lax.dot_general(a, b, (((ca,), (cb,)), ((), ())), preferred_element_type=F32)


def weight_kernel(idx, levels, scales, second, down, up, out):
    base = dot(down[...], up[...], 1, 0) * SCALE
    for j in range(HALF // BLOCK):
        rows = slice(j * BLOCK, (j + 1) * BLOCK)
        first = scales[j : j + 1, :].astype(F32)
        scaled = (levels[rows, :].astype(F32) * first) * second[...]
        out[rows, :] = (scaled + base[rows, :]).astype(BF)


def local_weight(idx, levels, scales, second, down, up):
    return pl.pallas_call(
        weight_kernel,
        grid_spec=pltpu.PrefetchScalarGridSpec(
            num_scalar_prefetch=1,
            grid=(1,),
            in_specs=[
                pl.BlockSpec((HALF, KEYS), lambda i, s: (s[0], 0)),
                pl.BlockSpec((HALF // BLOCK, KEYS), lambda i, s: (s[0], 0)),
                pl.BlockSpec((1, KEYS), lambda i, s: (0, 0)),
                pl.BlockSpec((HALF, RANK), lambda i, s: (s[0], 0)),
                pl.BlockSpec((RANK, KEYS), lambda i, s: (0, 0)),
            ],
            out_specs=pl.BlockSpec((HALF, KEYS), lambda i, s: (0, 0)),
        ),
        out_shape=jax.ShapeDtypeStruct((HALF, KEYS), BF),
        compiler_params=params(16),
        cost_estimate=pl.CostEstimate(flops=2 * HALF * RANK * KEYS, bytes_accessed=2 << 20, transcendentals=0),
        name="weight",
    )(idx, levels, scales, second, down, up)


def grads_kernel(idx, everyone, own, rotated, freqs, up, grads, low):
    mine = own[...]
    count = jnp.zeros((ROWS, QUART), F32)
    for k in range(SHARDS):
        row = everyone[k, RANK : RANK + 1, :].astype(F32)
        count = count + jnp.where(row < mine, 1.0, 0.0)
    first = jnp.sum(count, axis=1, keepdims=True)
    place = lax.broadcasted_iota(jnp.int32, (ROWS, 1), 0) + idx[3] * ROWS
    position = place.astype(F32) - first
    angle = position * freqs[...]
    cosine = jnp.cos(angle)
    lane = lax.broadcasted_iota(jnp.int32, (ROWS, HEAD), 1)
    sine = jnp.where(lane < HEAD // 2, 1.0, -1.0) * jnp.sin(angle)
    for h in range(KEYS // HEAD):
        cols = slice(h * HEAD, (h + 1) * HEAD)
        g = rotated[:, cols].astype(F32)
        grads[:, cols] = (g * cosine + pltpu.roll(g, HEAD // 2, 1) * sine).astype(BF)
    low[...] = dot(up[...], grads[...], 1, 1).astype(BF)


def make_grads(idx, everyone, own, rotated, freqs, up):
    full = lambda shape: pl.BlockSpec(shape, lambda i, s: (0,) * len(shape))
    return pl.pallas_call(
        grads_kernel,
        grid_spec=pltpu.PrefetchScalarGridSpec(
            num_scalar_prefetch=1,
            grid=(1,),
            in_specs=[
                full(everyone.shape),
                full((ROWS, 1)),
                full((ROWS, KEYS)),
                full((1, HEAD)),
                full((RANK, KEYS)),
            ],
            out_specs=[full((ROWS, KEYS)), full((RANK, ROWS))],
        ),
        out_shape=[jax.ShapeDtypeStruct((ROWS, KEYS), BF), jax.ShapeDtypeStruct((RANK, ROWS), BF)],
        compiler_params=params(16),
        cost_estimate=pl.CostEstimate(flops=2 * ROWS * RANK * KEYS, bytes_accessed=1 << 20, transcendentals=2 * ROWS * HEAD),
        name="grads",
    )(idx, everyone, own, rotated, freqs, up)


DOWN_STEPS = 4
DOWN_SHARDS = SHARDS // DOWN_STEPS


def down_kernel(idx, low, tokens, keep, send):
    c = idx[0]
    for k in range(DOWN_SHARDS):
        cols = slice(k * HALF, (k + 1) * HALF)
        mine = pl.multiple_of(k * 2 * HALF + c * HALF, HALF)
        other = pl.multiple_of(k * 2 * HALF + (1 - c) * HALF, HALF)
        send[:, cols] = dot(low[...], tokens[:, pl.ds(other, HALF)], 1, 0).astype(BF)
        keep[:, cols] = dot(low[...], tokens[:, pl.ds(mine, HALF)], 1, 0)


def down_part(idx, low, tokens):
    wide = DOWN_SHARDS * HALF
    return pl.pallas_call(
        down_kernel,
        grid_spec=pltpu.PrefetchScalarGridSpec(
            num_scalar_prefetch=1,
            grid=(DOWN_STEPS,),
            in_specs=[
                pl.BlockSpec((RANK, ROWS), lambda i, s: (0, 0)),
                pl.BlockSpec((ROWS, 2 * wide), lambda i, s: (0, i)),
            ],
            out_specs=[
                pl.BlockSpec((RANK, wide), lambda i, s: (0, i)),
                pl.BlockSpec((RANK, wide), lambda i, s: (0, i)),
            ],
        ),
        out_shape=[
            jax.ShapeDtypeStruct((RANK, WIDTH // 2), F32),
            jax.ShapeDtypeStruct((RANK, WIDTH // 2), BF),
        ],
        compiler_params=params(24),
        cost_estimate=pl.CostEstimate(flops=2 * ROWS * RANK * WIDTH, bytes_accessed=9 << 20, transcendentals=0),
        name="down",
    )(idx, low, tokens)


def up_kernel(idx, t0, t1, t2, t3, a0, a1, a2, a3, grads, keep, send, total):
    i = pl.program_id(0)

    @pl.when(i == 0)
    def _():
        total[...] = jnp.zeros_like(total)

    part = dot(t0[...], a0[0], 1, 1) + dot(t1[...], a1[0], 1, 1)
    total[...] += part + (dot(t2[...], a2[0], 1, 1) + dot(t3[...], a3[0], 1, 1))

    @pl.when(i == SHARDS - 1)
    def _():
        low = total[...].astype(BF)
        mine = pl.multiple_of(idx[0] * QUART, QUART)
        other = pl.multiple_of((1 - idx[0]) * QUART, QUART)
        keep[...] = dot(low, grads[:, pl.ds(mine, QUART)], 0, 0)
        send[...] = dot(low, grads[:, pl.ds(other, QUART)], 0, 0)


def up_part(idx, tokens, pieces, grads):
    def column(flip_c, flip_x):
        def at(i, s):
            c = s[0] if not flip_c else 1 - s[0]
            x = s[1] if not flip_x else 1 - s[1]
            return (0, i * 4 + c * 2 + x)

        return pl.BlockSpec((ROWS, QUART), at)

    piece = pl.BlockSpec((1, RANK, QUART), lambda i, s: (i, 0, 0))
    full = lambda shape: pl.BlockSpec(shape, lambda i, s: (0,) * len(shape))
    return pl.pallas_call(
        up_kernel,
        grid_spec=pltpu.PrefetchScalarGridSpec(
            num_scalar_prefetch=1,
            grid=(SHARDS,),
            in_specs=[column(0, 0), column(0, 1), column(1, 0), column(1, 1)]
            + [piece] * 4
            + [full((ROWS, KEYS))],
            out_specs=[full((RANK, QUART)), full((RANK, QUART))],
            scratch_shapes=[pltpu.VMEM((ROWS, RANK), F32)],
        ),
        out_shape=[jax.ShapeDtypeStruct((RANK, QUART), F32)] * 2,
        compiler_params=params(16),
        cost_estimate=pl.CostEstimate(flops=2 * ROWS * RANK * WIDTH, bytes_accessed=8 << 20, transcendentals=0),
        name="up",
    )(idx, tokens, tokens, tokens, tokens, *pieces, grads)


def block_kernel(n_weights, *refs):
    sources = refs[:4]
    weights = refs[4 : 4 + n_weights]
    outs = refs[4 + n_weights :]
    for source, out in zip(sources[::-1], outs[::-1]):
        at = 0
        for w in weights:
            wide = w.shape[0]
            out[:, at : at + wide] = dot(source[...], w[...], 1, 1).astype(BF)
            at += wide


def blocks(sources, weights):
    wide = sum(w.shape[0] for w in weights)
    return pl.pallas_call(
        functools.partial(block_kernel, len(weights)),
        out_shape=[jax.ShapeDtypeStruct((ROWS, wide), BF)] * 4,
        compiler_params=params(24),
        cost_estimate=pl.CostEstimate(
            flops=2 * 4 * ROWS * KEYS * wide, bytes_accessed=2 * wide * (KEYS + 4 * ROWS), transcendentals=0
        ),
        name="blocks",
    )(*sources, *weights)


def assemble_kernel(groups, idx, *refs):
    n = 4 * len(groups)
    pieces, out, sems = refs[:n], refs[n], refs[n + 1]
    c, x, z = idx[0], idx[2], idx[4]
    copies = []
    for g, offsets in enumerate(groups):
        for q in range(4):
            xl = x if q < 2 else 1 - x
            h = c if q % 2 == 0 else 1 - c
            for j, k in enumerate(offsets):
                zz = lax.rem(z + (k + NZ), NZ)
                col = pl.multiple_of(((xl * NZ + zz) * 2 + h) * HALF, HALF)
                copies.append(
                    pltpu.make_async_copy(
                        pieces[4 * g + q].at[:, pl.ds(j * HALF, HALF)],
                        out.at[:, pl.ds(col, HALF)],
                        sems.at[len(copies)],
                    )
                )
    for copy in copies:
        copy.start()
    for copy in copies:
        copy.wait()


def assemble(idx, groups, pieces):
    anywhere = pl.BlockSpec(memory_space=pl.ANY)
    return pl.pallas_call(
        functools.partial(assemble_kernel, groups),
        in_specs=[pl.BlockSpec(memory_space=pltpu.SMEM)] + [anywhere] * len(pieces),
        out_specs=anywhere,
        scratch_shapes=[pltpu.SemaphoreType.DMA((32,))],
        out_shape=jax.ShapeDtypeStruct((ROWS, WIDTH), BF),
        compiler_params=params(8),
        cost_estimate=pl.CostEstimate(flops=0, bytes_accessed=10 << 20, transcendentals=0),
        name="assemble",
    )(idx, *pieces)


def x_permutation(swap):
    at = lambda x, c: ((x // 2) * 2 + c) * 2 + x % 2
    pairs = []
    for x in range(4):
        for c in range(2):
            if (c ^ swap) == 0:
                pairs.append((at(x, c), at((x + 1) % 4, 0)))
            else:
                pairs.append((at(x, c), at((x - 1) % 4, 1)))
    return pairs


def inverse(pairs):
    return [(b, a) for a, b in pairs]


CORE = [(0, 1), (1, 0)]
RIGHT = [(i, (i + 1) % NZ) for i in range(NZ)]
LEFT = [(i, (i - 1) % NZ) for i in range(NZ)]


def on_device(tokens, rotated, documents, levels, scales, second, down, up):
    xh, y, c, xl, z = (lax.axis_index(a) for a in ("xh", "y", "c", "xl", "z"))
    idx = jnp.stack([c, xh, xl, xl * NZ + z, z]).astype(jnp.int32)

    weight = local_weight(idx, levels, scales, second, down, up)
    right = [weight]
    left = [weight]
    for step in range(3):
        right.append(lax.ppermute(right[-1], "z", RIGHT))
        left.append(lax.ppermute(left[-1], "z", LEFT))
    far = HALF // 2
    far_right = lax.ppermute(right[-1][:far], "z", RIGHT)
    far_left = lax.ppermute(left[-1][far:], "z", LEFT)

    quarter = lax.dynamic_slice(down, ((c * 2 + xh) * QUART, 0), (QUART, RANK)).T
    ids = jnp.pad(documents.astype(BF), ((0, 7), (0, QUART - ROWS)), constant_values=1000.0)
    packet = jnp.concatenate([quarter, ids], axis=0)
    packet = jnp.broadcast_to(packet[None], (SHARDS,) + packet.shape)
    everyone = lax.all_to_all(packet, SHARD_AXES, 0, 0, tiled=True)

    half = HEAD // 2
    freqs = ROPE_BASE ** (-jnp.arange(half, dtype=F32) * 2.0 / HEAD)
    freqs = jnp.concatenate([freqs, freqs])[None, :]
    own = documents.astype(F32).reshape(ROWS, 1)
    grads, low = make_grads(idx, everyone, own, rotated, freqs, up)

    there, across = x_permutation(0), x_permutation(1)
    sources = [
        grads,
        lax.ppermute(grads, "c", CORE),
        lax.ppermute(grads, X_AXES, there),
        lax.ppermute(grads, X_AXES, across),
    ]

    keep, send = down_part(idx, low, tokens)
    total = keep + lax.ppermute(send, "c", CORE).astype(F32)
    total = total.reshape(4, RANK // 4, WIDTH // 2)
    mine = lax.dynamic_index_in_dim(total, y, 0, keepdims=False)
    for d in (1, 3, 2):
        out = lax.dynamic_index_in_dim(total, (y + d) % 4, 0, keepdims=False).astype(BF)
        mine = mine + lax.ppermute(out, "y", [(i, (i + d) % 4) for i in range(4)]).astype(F32)

    other_x = lax.ppermute(everyone, "xh", CORE)
    pieces = [everyone, other_x, lax.ppermute(everyone, "c", CORE), lax.ppermute(other_x, "c", CORE)]
    up_keep, up_send = up_part(idx, tokens, pieces, grads)
    up_total = (up_keep + lax.ppermute(up_send, "c", CORE)).reshape(4, RANK // 4, QUART)
    up_mine = lax.dynamic_index_in_dim(up_total, y, 0, keepdims=False)
    for d in (1, 3, 2):
        out = lax.dynamic_index_in_dim(up_total, (y + d) % 4, 0, keepdims=False)
        up_mine = up_mine + lax.ppermute(out, "y", [(i, (i + d) % 4) for i in range(4)])

    slabs = mine.reshape(RANK // 4, SHARDS, HALF).transpose(1, 0, 2)
    slabs = jnp.concatenate([slabs, jnp.broadcast_to(up_mine[None], (SHARDS,) + up_mine.shape)], axis=2)
    slabs = jnp.sum(lax.all_to_all(slabs, SHARD_AXES, 0, 0, tiled=True), axis=0)
    slabs = jnp.broadcast_to(slabs[None], (16,) + slabs.shape)
    slabs = lax.all_to_all(slabs, DP_AXES, 0, 0, tiled=True)
    slabs = slabs.reshape(2, 4, 2, RANK // 4, HALF + QUART)
    factor = SCALE / jnp.sqrt(jnp.float32(TOKENS))
    slabs = factor * (slabs[0] + slabs[1])
    grad_down = slabs[..., :HALF].transpose(1, 3, 0, 2).reshape(2 * HALF, RANK)
    grad_up = slabs[..., HALF:].transpose(0, 2, 1, 3).reshape(RANK, KEYS)

    groups = ((0, -1, 1), (-2, 2, -3, 3), (4,))
    parts = (
        (right[0], right[1], left[1]),
        (right[2], left[2], right[3], left[3]),
        (far_right, far_left),
    )
    filled = []
    for part in parts:
        o, p, a, b = blocks(sources, part)
        filled += [
            o,
            lax.ppermute(p, "c", CORE),
            lax.ppermute(a, X_AXES, inverse(there)),
            lax.ppermute(b, X_AXES, inverse(across)),
        ]
    grad_tokens = assemble(idx, groups, filled)
    return grad_tokens, grad_down, grad_up


def solution(mesh):
    fine = Mesh(mesh.devices.reshape(2, 4, 2, 2, 8), ("xh", "y", "c", "xl", "z"))
    everything = DP_AXES + SHARD_AXES
    in_specs = (
        P(everything, None),
        P(everything, None),
        P(DP_AXES, SHARD_AXES),
        P(SHARD_AXES, None),
        P(SHARD_AXES, None),
        P(),
        P(SHARD_AXES, None),
        P(),
    )
    out_specs = (P(everything, None), P(SHARD_AXES, None), P())
    return jax.shard_map(on_device, mesh=fine, in_specs=in_specs, out_specs=out_specs, check_vma=False)
```

time: 786 us -> 194 us (0.25)
  waiting for transfers between devices: 669 us -> 80.6 us
  starting transfers between devices: 0.2 us -> 62.3 us
  blocking collectives: 42.6 us -> 0 us
  matrix products: 34.8 us -> 0 us
  Pallas kernels: 0 us -> 22.5 us
  local copies, waits for them, and re-layouts: 2.72 us -> 21 us
  other arithmetic: 21.6 us -> 6.13 us
  between operations: 14.6 us -> 1.02 us
    psum x2 -> x0, waiting for transfers between devices: 369 us -> none  [the longest x1 228 us: on_device(): up_sum = lax.psum(up_local, ('dp', 'shard'))]
    all_gather x2 -> x0, waiting for transfers between devices: 225 us -> none  [the longest x1 187 us: on_device(): lax.all_gather(frozen_base_levels, 'shard', axis=0, tiled=True)]
    reduce_scatter x1 -> x0, waiting for transfers between devices: 73.2 us -> none  [on_device(): lax.psum_scatter(jnp.einsum('td,tr->dr', inputs, reduced_gradient, prefer...]
    ppermute x0 -> x31, waiting for transfers between devices: none -> 65.8 us  [the longest x3 26.3 us: on_device(): left.append(lax.ppermute(left[-1], 'z', LEFT))]
    ppermute x0 -> x31, starting transfers between devices: none -> 42.2 us  [the longest x3 8.11 us: on_device(): left.append(lax.ppermute(left[-1], 'z', LEFT))]
    dot_general x5 -> x0, matrix products: 34.8 us -> none  [the longest x1 15.5 us: on_device(): jnp.einsum('tk,dk->td', input_gradients, weight, preferred_element_type=j...]
    all_gather x1 -> x0, blocking collectives: 25.9 us -> none  [on_device(): scales_one = lax.all_gather(first_level_scales, 'shard', axis=0, tiled=True)]
    pallas_call x0 -> x8, Pallas kernels: none -> 22.5 us  [the longest x3 7.64 us: blocks(): pl.pallas_call(functools.partial(block_kernel, len(weights)), out_shape=[...]
  transfers between devices with their start and end apart: 5 -> 34, of which waited for: 5 -> 11; matrix products, arithmetic and copies ran while one was open for 3% -> 5% of each run, Pallas kernels for 0% -> 6%
where the time goes in v1:
time: 194 us
  waiting for transfers between devices  80.6 us (42%)
  starting transfers between devices  62.3 us (32%)
  Pallas kernels  22.5 us (12%)
  local copies, waits for them, and re-layouts  21 us (11%)
  other arithmetic  6.13 us (3%)
    ppermute x3, waiting for transfers between devices, on_device(): left.append(lax.ppermute(left[-1], 'z', LEFT))  26.3 us
    all_to_all x1, waiting for transfers between devices, on_device(): everyone = lax.all_to_all(packet, SHARD_AXES, 0, 0, tiled=True)  14.8 us
    unnamed x48, local copies, waits for them, and re-layouts  14.3 us
    ppermute x1, waiting for transfers between devices, on_device(): other_x = lax.ppermute(everyone, 'xh', CORE)  13.7 us
    ppermute x3, waiting for transfers between devices, on_device(): lax.ppermute(a, X_AXES, inverse(there))  13.5 us
    all_to_all x1, starting transfers between devices, on_device(): everyone = lax.all_to_all(packet, SHARD_AXES, 0, 0, tiled=True)  10 us
    ppermute x3, starting transfers between devices, on_device(): left.append(lax.ppermute(left[-1], 'z', LEFT))  8.11 us
    pallas_call x3, Pallas kernels, blocks(): pl.pallas_call(functools.partial(block_kernel, len(weights)), out_shape=[...  7.64 us
  transfers between devices with their start and end apart: 34, of which 11 were waited for; matrix products, arithmetic and copies ran while one was open for 5% of the time, Pallas kernels for 6%

profile of v1, /device:TPU:1, one launch (start us, length us, event | category | flops | bytes accessed | tf_op | source)
XLA Modules:
  0.0 193.6 jit_solution(15267246254195166864)
XLA Ops:
  0.7 0.8 convert_bitcast_fusion
  1.4 0.8 dynamic-slice_bitcast_fusion
  2.2 0.9 broadcast_in_dim.8
  3.0 10.0 %all-to-all-start = ((bf16[16,72,256]{2,1,0:T(8,128)(2,1)}), bf16[16,72,256]{2,1,0:T(8,128)(2,1)S(1)}, u32[]{:S(2)}, u32[]{:S(2)}) async-start(bf16[16,72,256]{2,1,0:T(8,128)(2,1)} %broadcast_in_dim.8), calls=%async_computation | async-start | bytes 1179648 | tf_op jit(solution)/shard_map/all_to_all | solution.py:305
  13.4 14.8 %all-to-all-done.everyone.a0 = bf16[16,72,256]{2,1,0:T(8,128)(2,1)S(1)} async-done(((bf16[16,72,256]{2,1,0:T(8,128)(2,1)}), bf16[16,72,256]{2,1,0:T(8,128)(2,1)S(1)}, u32[]{:S(2)}, u32[]{:S(2)}) %all-to-all-start) | async-done | bytes 589856 | tf_op jit(solution)/shard_map/all_to_all | solution.py:305
  28.2 1.4 grads.1
  29.6 2.5 %copy-done = bf16[160,16384]{1,0:T(8,128)(2,1)S(1)} copy-done((bf16[160,16384]{1,0:T(8,128)(2,1)S(1)}, bf16[160,16384]{1,0:T(8,128)(2,1)}, u32[]{:S(2)}) %copy-start) | copy-done | bytes 5242904
  32.1 3.4 %down.2 = (f32[64,8192]{1,0:T(8,128)S(1)}, bf16[64,8192]{1,0:T(8,128)(2,1)}) custom-call(s32[5]{0:T(128)S(1)} %stack.23.idx, bf16[64,160]{1,0:T(8,128)(2,1)S(1)} %get-tuple-element.34.low, bf16[160,16384]{1,0:T(8,128)(2,1)S(1)} %copy-done), custom_call_target="tpu_custom_call" | custom-call | flops 335544320 | bytes 9437184 | tf_op jit(solution)/shard_map/down/pallas_call | solution.py:130
  35.4 2.8 %collective-permute-start.20 = (bf16[64,8192]{1,0:T(8,128)(2,1)}, bf16[64,8192]{1,0:T(8,128)(2,1)}, u32[]{:S(2)}, u32[]{:S(2)}) collective-permute-start(bf16[64,8192]{1,0:T(8,128)(2,1)} %get-tuple-element.36), channel_id=1, source_target_pairs={{0,16},{16,0},{1,17},{17,1},{2,18},{18,2},{3,19},{19,3},{4,20},{20... | collective-permute-start | bytes 3145736 | tf_op jit(solution)/shard_map/ppermute | solution.py:322
  38.2 2.4 %collective-permute-start.24 = (bf16[16,72,256]{2,1,0:T(8,128)(2,1)S(1)}, bf16[16,72,256]{2,1,0:T(8,128)(2,1)S(1)}, u32[]{:S(2)}, u32[]{:S(2)}) collective-permute-start(bf16[16,72,256]{2,1,0:T(8,128)(2,1)S(1)} %all-to-all-done.everyone.a0), channel_id=1, source_target_pairs={{0,128},{128,0},{1,129},{129,1},{2,130},{130,2},{3,131},{131,3},{4... | collective-permute-start | bytes 1769480 | tf_op jit(solution)/shard_map/ppermute | solution.py:329
  40.9 13.7 %collective-permute-done.24.a1 = bf16[16,72,256]{2,1,0:T(8,128)(2,1)S(1)} collective-permute-done((bf16[16,72,256]{2,1,0:T(8,128)(2,1)S(1)}, bf16[16,72,256]{2,1,0:T(8,128)(2,1)S(1)}, u32[]{:S(2)}, u32[]{:S(2)}) %collective-permute-start.24) | collective-permute-done | bytes 589856 | tf_op jit(solution)/shard_map/ppermute | solution.py:329
  54.7 0.8 collective-permute-start.26
  55.5 1.5 convert_add_fusion
  57.1 3.1 %copy-done.1 = bf16[160,16384]{1,0:T(8,128)(2,1)S(1)} copy-done((bf16[160,16384]{1,0:T(8,128)(2,1)S(1)}, bf16[160,16384]{1,0:T(8,128)(2,1)}, u32[]{:S(2)}) %copy-start.1) | copy-done | bytes 5242904
  60.2 6.1 %up.5 = (f32[64,256]{1,0:T(8,128)S(1)}, f32[64,256]{1,0:T(8,128)S(1)}) custom-call(s32[5]{0:T(128)S(1)} %stack.23.idx, bf16[160,16384]{1,0:T(8,128)(2,1)S(1)} %copy-done.1, bf16[160,16384]{1,0:T(8,128)(2,1)S(1)} %copy-done.1, bf16[160,16384]{1,0:T(8,128)(2,1)S(1)} %copy-done.1, bf16[160,16384]{1,0:T(8,128)(2,1)S(1)} %copy-done.1, ...), custom_call_target="tpu_custom_call" | custom-call | flops 335544320 | bytes 8388608 | tf_op jit(solution)/shard_map/up/pallas_call | solution.py:184
  66.5 0.8 fusion.3
  67.3 1.3 collective-permute-start.21
  68.6 2.6 %collective-permute-start.23 = (bf16[16,8192]{1,0:T(8,128)(2,1)S(1)}, bf16[16,8192]{1,0:T(8,128)(2,1)}, u32[]{:S(2)}, u32[]{:S(2)}) collective-permute-start(bf16[16,8192]{1,0:T(8,128)(2,1)S(1)} %get-tuple-element.40), channel_id=1, source_target_pairs={{0,64},{32,96},{64,0},{96,32},{1,65},{33,97},{65,1},{97,33},{2,66}... | collective-permute-start | bytes 786440 | tf_op jit(solution)/shard_map/ppermute | solution.py:327
  71.2 1.1 collective-permute-start.22
  72.8 0.8 collective-permute-start.30
  73.6 6.4 %collective-permute-done.28 = f32[16,256]{1,0:T(8,128)S(1)} collective-permute-done((f32[16,256]{1,0:T(8,128)S(1)}, f32[16,256]{1,0:T(8,128)S(1)}, u32[]{:S(2)}, u32[]{:S(2)}) %collective-permute-start.28) | collective-permute-done | bytes 16416 | tf_op jit(solution)/shard_map/ppermute | solution.py:336
  80.0 3.7 %collective-permute-start.29 = (f32[16,256]{1,0:T(8,128)S(1)}, f32[16,256]{1,0:T(8,128)S(1)}, u32[]{:S(2)}, u32[]{:S(2)}) collective-permute-start(f32[16,256]{1,0:T(8,128)S(1)} %get-tuple-element.44), channel_id=1, source_target_pairs={{0,96},{32,0},{64,32},{96,64},{1,97},{33,1},{65,33},{97,65},{2,98}... | collective-permute-start | bytes 49160 | tf_op jit(solution)/shard_map/ppermute | solution.py:336
  83.9 0.8 weight.1.refs_4_
  84.7 2.3 %collective-permute-start.4 = (bf16[512,512]{1,0:T(8,128)(2,1)S(1)}, bf16[512,512]{1,0:T(8,128)(2,1)S(1)}, u32[]{:S(2)}, u32[]{:S(2)}) collective-permute-start(bf16[512,512]{1,0:T(8,128)(2,1)S(1)} %weight.1.refs_4_), channel_id=1, source_target_pairs={{0,7},{1,0},{2,1},{3,2},{4,3},{5,4},{6,5},{7,6},{8,15},{9,8},{10,9... | collective-permute-start | bytes 1572872 | tf_op jit(solution)/shard_map/ppermute | solution.py:296
  87.1 1.4 fusion.1
  88.9 1.3 copy.24
  90.3 4.9 %all-to-all-start.1 = ((f32[16,16,768]{2,1,0:T(8,128)}), f32[16,16,768]{2,1,0:T(8,128)}, u32[]{:S(2)}, u32[]{:S(2)}) async-start(f32[16,16,768]{2,1,0:T(8,128)} %copy.24), calls=%async_computation.1 | async-start | bytes 1572864 | tf_op jit(solution)/shard_map/all_to_all | solution.py:340
  95.2 1.4 collective-permute-done.4.refs_6_
  96.6 3.4 %collective-permute-start.9 = (bf16[512,512]{1,0:T(8,128)(2,1)S(1)}, bf16[512,512]{1,0:T(8,128)(2,1)S(1)}, u32[]{:S(2)}, u32[]{:S(2)}) collective-permute-start(bf16[512,512]{1,0:T(8,128)(2,1)S(1)} %collective-permute-done.4.refs_6_), channel_id=1, source_target_pairs={{0,7},{1,0},{2,1},{3,2},{4,3},{5,4},{6,5},{7,6},{8,15},{9,8},{10,9... | collective-permute-start | bytes 1572872 | tf_op jit(solution)/shard_map/ppermute | solution.py:296
  100.0 0.8 copy-done.9
  100.8 24.9 %collective-permute-done.9.refs_5_ = bf16[512,512]{1,0:T(8,128)(2,1)S(1)} collective-permute-done((bf16[512,512]{1,0:T(8,128)(2,1)S(1)}, bf16[512,512]{1,0:T(8,128)(2,1)S(1)}, u32[]{:S(2)}, u32[]{:S(2)}) %collective-permute-start.9) | collective-permute-done | bytes 524320 | tf_op jit(solution)/shard_map/ppermute | solution.py:296
  125.7 2.4 %collective-permute-start.11 = (bf16[512,512]{1,0:T(8,128)(2,1)S(1)}, bf16[512,512]{1,0:T(8,128)(2,1)S(1)}, u32[]{:S(2)}, u32[]{:S(2)}) collective-permute-start(bf16[512,512]{1,0:T(8,128)(2,1)S(1)} %collective-permute-done.9.refs_5_), channel_id=1, source_target_pairs={{0,7},{1,0},{2,1},{3,2},{4,3},{5,4},{6,5},{7,6},{8,15},{9,8},{10,9... | collective-permute-start | bytes 1572872 | tf_op jit(solution)/shard_map/ppermute | solution.py:296
  128.1 3.6 %collective-permute-start.2 = (bf16[160,512]{1,0:T(8,128)(2,1)S(1)}, bf16[160,512]{1,0:T(8,128)(2,1)S(1)}, u32[]{:S(2)}, u32[]{:S(2)}) collective-permute-start(bf16[160,512]{1,0:T(8,128)(2,1)S(1)} %get-tuple-element.21.refs_0_.grads), channel_id=1, source_target_pairs={{0,152},{16,8},{8,16},{24,128},{128,24},{144,136},{136,144},{152,0... | collective-permute-start | bytes 491528 | tf_op jit(solution)/shard_map/ppermute | solution.py:318
  131.7 1.9 %collective-permute-start.1 = (bf16[160,512]{1,0:T(8,128)(2,1)S(1)}, bf16[160,512]{1,0:T(8,128)(2,1)S(1)}, u32[]{:S(2)}, u32[]{:S(2)}) collective-permute-start(bf16[160,512]{1,0:T(8,128)(2,1)S(1)} %get-tuple-element.21.refs_0_.grads), channel_id=1, source_target_pairs={{0,8},{16,152},{8,128},{24,16},{128,136},{144,24},{136,0},{152,144... | collective-permute-start | bytes 491528 | tf_op jit(solution)/shard_map/ppermute | solution.py:317
  133.7 1.9 collective-permute-done.2.refs_3_
  135.6 1.2 collective-permute-done.1.refs_2_
  136.8 1.1 copy-done.10
  137.9 3.0 %blocks.3 = (bf16[160,1536]{1,0:T(8,128)(2,1)S(1)}, bf16[160,1536]{1,0:T(8,128)(2,1)}, bf16[160,1536]{1,0:T(8,128)(2,1)}, bf16[160,1536]{1,0:T(8,128)(2,1)}) custom-call(bf16[160,512]{1,0:T(8,128)(2,1)S(1)} %get-tuple-element.21.refs_0_.grads, bf16[160,512]{1,0:T(8,128)(2,1)S(1)} %collective-permute-done.refs_1_, ...), custom_call_target="tpu_custom_call" | custom-call | flops 1006632960 | bytes 3538944 | tf_op jit(solution)/shard_map/blocks/pallas_call | solution.py:216
  140.8 2.0 %collective-permute-start.5 = (bf16[160,1536]{1,0:T(8,128)(2,1)}, bf16[160,1536]{1,0:T(8,128)(2,1)S(1)}, u32[]{:S(2)}, u32[]{:S(2)}) collective-permute-start(bf16[160,1536]{1,0:T(8,128)(2,1)} %get-tuple-element.23), channel_id=1, source_target_pairs={{0,16},{16,0},{1,17},{17,1},{2,18},{18,2},{3,19},{19,3},{4,20},{20... | collective-permute-start | bytes 1474568 | tf_op jit(solution)/shard_map/ppermute | solution.py:360
  142.9 0.7 slice.27
  143.6 2.9 %collective-permute-start.16 = (bf16[256,512]{1,0:T(8,128)(2,1)}, bf16[256,512]{1,0:T(8,128)(2,1)S(1)}, u32[]{:S(2)}, u32[]{:S(2)}) collective-permute-start(bf16[256,512]{1,0:T(8,128)(2,1)} %slice.27), channel_id=1, source_target_pairs={{0,7},{1,0},{2,1},{3,2},{4,3},{5,4},{6,5},{7,6},{8,15},{9,8},{10,9... | collective-permute-start | bytes 786440 | tf_op jit(solution)/shard_map/ppermute | solution.py:299
  146.6 0.7 slice.26
  147.3 1.9 collective-permute-start.7
  149.2 1.2 reduce_sum.9
  150.4 1.0 broadcast_in_dim.11
  151.3 5.2 %all-to-all-start.2 = ((f32[16,16,768]{2,1,0:T(8,128)}), f32[16,16,768]{2,1,0:T(8,128)}, u32[]{:S(2)}, u32[]{:S(2)}) async-start(f32[16,16,768]{2,1,0:T(8,128)} %broadcast_in_dim.11), calls=%async_computation.2 | async-start | bytes 1572864 | tf_op jit(solution)/shard_map/all_to_all | solution.py:342
  156.5 1.0 copy-done.8
  157.6 1.0 copy-done.12
  158.6 0.9 copy-done.14
  159.5 0.9 copy-done.17
  160.5 0.9 copy-done.19
  161.4 2.9 %blocks.4 = (bf16[160,2048]{1,0:T(8,128)(2,1)S(1)}, bf16[160,2048]{1,0:T(8,128)(2,1)S(1)}, bf16[160,2048]{1,0:T(8,128)(2,1)S(1)}, bf16[160,2048]{1,0:T(8,128)(2,1)S(1)}) custom-call(bf16[160,512]{1,0:T(8,128)(2,1)S(1)} %get-tuple-element.21.refs_0_.grads, bf16[160,512]{1,0:T(8,128)(2,1)S(1)} %copy-done.19, bf16[160,512]{1,0:T(8,128)(2,1)S(1)} %copy-done.17, ...), custom_call_target="tpu_custom_call" | custom-call | flops 1342177280 | bytes 4718592 | tf_op jit(solution)/shard_map/blocks/pallas_call | solution.py:216
  164.3 0.6 collective-permute-start.12
  164.9 1.7 collective-permute-start.14
  166.6 1.8 blocks.5
  168.4 1.4 collective-permute-start.17
  169.8 1.0 collective-permute-done.17.refs_9_
  170.9 1.5 collective-permute-start.19
  172.4 13.5 %collective-permute-done.18.refs_10_ = bf16[160,512]{1,0:T(8,128)(2,1)S(1)} collective-permute-done((bf16[160,512]{1,0:T(8,128)(2,1)S(1)}, bf16[160,512]{1,0:T(8,128)(2,1)S(1)}, u32[]{:S(2)}, u32[]{:S(2)}) %collective-permute-start.18) | collective-permute-done | bytes 163872 | tf_op jit(solution)/shard_map/ppermute | solution.py:361
  185.9 1.6 collective-permute-done.19.refs_11_
  187.5 3.2 %assemble.1 = bf16[160,16384]{1,0:T(8,128)(2,1)} custom-call(s32[5]{0:T(128)S(1)} %stack.23.idx, bf16[160,1536]{1,0:T(8,128)(2,1)S(1)} %get-tuple-element.22.refs_0_, bf16[160,1536]{1,0:T(8,128)(2,1)S(1)} %collective-permute-done.5.refs_1_, bf16[160,1536]{1,0:T(8,128)(2,1)S(1)} %collective-permute-done.6.refs_2_, ...), custom_call_target="tpu_custom_call" | custom-call | bytes 10485760 | tf_op jit(solution)/shard_map/assemble/pallas_call | solution.py:254
  190.6 1.2 fusion.2
  192.1 0.8 copy.28
  192.9 0.7 copy.29
  (86 shorter events, 2.4 us)
Async XLA Ops:
  0.6 27.5 %copy-start.3 = (bf16[64,512]{1,0:T(8,128)(2,1)S(1)}, bf16[64,512]{1,0:T(8,128)(2,1)}, u32[]{:S(2)}) copy-start(bf16[64,512]{1,0:T(8,128)(2,1)} %up.4) | copy-start | bytes 196612
  0.6 27.5 %copy-start.4 = (bf16[160,512]{1,0:T(8,128)(2,1)S(1)}, bf16[160,512]{1,0:T(8,128)(2,1)}, u32[]{:S(2)}) copy-start(bf16[160,512]{1,0:T(8,128)(2,1)} %rotated.1) | copy-start | bytes 491524
  3.0 25.1 %all-to-all-start = ((bf16[16,72,256]{2,1,0:T(8,128)(2,1)}), bf16[16,72,256]{2,1,0:T(8,128)(2,1)S(1)}, u32[]{:S(2)}, u32[]{:S(2)}) async-start(bf16[16,72,256]{2,1,0:T(8,128)(2,1)} %broadcast_in_dim.8), calls=%async_computation | async-start | bytes 1179648 | tf_op jit(solution)/shard_map/all_to_all | solution.py:305
  29.6 2.5 %copy-start = (bf16[160,16384]{1,0:T(8,128)(2,1)S(1)}, bf16[160,16384]{1,0:T(8,128)(2,1)}, u32[]{:S(2)}) copy-start(bf16[160,16384]{1,0:T(8,128)(2,1)} %t3.1) | copy-start | bytes 15728644
  35.4 20.0 %collective-permute-start.20 = (bf16[64,8192]{1,0:T(8,128)(2,1)}, bf16[64,8192]{1,0:T(8,128)(2,1)}, u32[]{:S(2)}, u32[]{:S(2)}) collective-permute-start(bf16[64,8192]{1,0:T(8,128)(2,1)} %get-tuple-element.36), channel_id=1, source_target_pairs={{0,16},{16,0},{1,17},{17,1},{2,18},{18,2},{3,19},{19,3},{4,20},{20... | collective-permute-start | bytes 3145736 | tf_op jit(solution)/shard_map/ppermute | solution.py:322
  38.2 16.5 %collective-permute-start.24 = (bf16[16,72,256]{2,1,0:T(8,128)(2,1)S(1)}, bf16[16,72,256]{2,1,0:T(8,128)(2,1)S(1)}, u32[]{:S(2)}, u32[]{:S(2)}) collective-permute-start(bf16[16,72,256]{2,1,0:T(8,128)(2,1)S(1)} %all-to-all-done.everyone.a0), channel_id=1, source_target_pairs={{0,128},{128,0},{1,129},{129,1},{2,130},{130,2},{3,131},{131,3},{4... | collective-permute-start | bytes 1769480 | tf_op jit(solution)/shard_map/ppermute | solution.py:329
  40.7 16.3 %collective-permute-start.25 = (bf16[16,72,256]{2,1,0:T(8,128)(2,1)S(1)}, bf16[16,72,256]{2,1,0:T(8,128)(2,1)S(1)}, u32[]{:S(2)}, u32[]{:S(2)}) collective-permute-start(bf16[16,72,256]{2,1,0:T(8,128)(2,1)S(1)} %all-to-all-done.everyone.a0), channel_id=1, source_target_pairs={{0,16},{16,0},{1,17},{17,1},{2,18},{18,2},{3,19},{19,3},{4,20},{20... | collective-permute-start | bytes 1769480 | tf_op jit(solution)/shard_map/ppermute | solution.py:330
  54.7 2.4 %collective-permute-start.26 = (bf16[16,72,256]{2,1,0:T(8,128)(2,1)S(1)}, bf16[16,72,256]{2,1,0:T(8,128)(2,1)S(1)}, u32[]{:S(2)}, u32[]{:S(2)}) collective-permute-start(bf16[16,72,256]{2,1,0:T(8,128)(2,1)S(1)} %collective-permute-done.24.a1), channel_id=1, source_target_pairs={{0,16},{16,0},{1,17},{17,1},{2,18},{18,2},{3,19},{19,3},{4,20},{20... | collective-permute-start | bytes 1769480 | tf_op jit(solution)/shard_map/ppermute | solution.py:330
  56.9 9.5 %copy-start.20 = (f32[64,8192]{1,0:T(8,128)}, f32[64,8192]{1,0:T(8,128)S(1)}, u32[]{:S(2)}) copy-start(f32[64,8192]{1,0:T(8,128)S(1)} %convert_add_fusion) | copy-start | bytes 6291460
  57.1 3.1 %copy-start.1 = (bf16[160,16384]{1,0:T(8,128)(2,1)S(1)}, bf16[160,16384]{1,0:T(8,128)(2,1)}, u32[]{:S(2)}) copy-start(bf16[160,16384]{1,0:T(8,128)(2,1)} %t3.1) | copy-start | bytes 15728644
  60.2 23.5 %copy-start.21 = (bf16[1024,64]{0,1:T(8,128)(2,1)S(1)}, bf16[1024,64]{0,1:T(8,128)(2,1)}, u32[]{:S(2)}) copy-start(bf16[1024,64]{0,1:T(8,128)(2,1)} %param.14) | copy-start | bytes 393220
  66.3 17.5 %copy-start.2 = (bf16[1024,512]{1,0:T(8,128)(2,1)S(1)}, bf16[1024,512]{1,0:T(8,128)(2,1)}, u32[]{:S(2)}) copy-start(bf16[1024,512]{1,0:T(8,128)(2,1)} %levels.1) | copy-start | bytes 3145732
  66.3 17.5 %copy-start.5 = (bf16[16,512]{1,0:T(8,128)(2,1)S(1)}, bf16[16,512]{1,0:T(8,128)(2,1)}, u32[]{:S(2)}) copy-start(bf16[16,512]{1,0:T(8,128)(2,1)} %scales.1) | copy-start | bytes 49156
  66.3 17.5 %copy-start.6 = (f32[1,512]{1,0:T(1,128)S(1)}, f32[1,512]{1,0:T(1,128)}, u32[]{:S(2)}) copy-start(f32[1,512]{1,0:T(1,128)} %second.1) | copy-start | bytes 6148
  66.4 5.9 %collective-permute-start.27 = (f32[64,256]{1,0:T(8,128)S(1)}, f32[64,256]{1,0:T(8,128)S(1)}, u32[]{:S(2)}, u32[]{:S(2)}) collective-permute-start(f32[64,256]{1,0:T(8,128)S(1)} %get-tuple-element.38), channel_id=1, source_target_pairs={{0,16},{16,0},{1,17},{17,1},{2,18},{18,2},{3,19},{19,3},{4,20},{20... | collective-permute-start | bytes 196616 | tf_op jit(solution)/shard_map/ppermute | solution.py:332
  67.3 19.8 %collective-permute-start.21 = (bf16[16,8192]{1,0:T(8,128)(2,1)}, bf16[16,8192]{1,0:T(8,128)(2,1)}, u32[]{:S(2)}, u32[]{:S(2)}) collective-permute-start(bf16[16,8192]{1,0:T(8,128)(2,1)} %get-tuple-element.39), channel_id=1, source_target_pairs={{0,32},{32,64},{64,96},{96,0},{1,33},{33,65},{65,97},{97,1},{2,34}... | collective-permute-start | bytes 786440 | tf_op jit(solution)/shard_map/ppermute | solution.py:327
  68.6 18.5 %collective-permute-start.23 = (bf16[16,8192]{1,0:T(8,128)(2,1)S(1)}, bf16[16,8192]{1,0:T(8,128)(2,1)}, u32[]{:S(2)}, u32[]{:S(2)}) collective-permute-start(bf16[16,8192]{1,0:T(8,128)(2,1)S(1)} %get-tuple-element.40), channel_id=1, source_target_pairs={{0,64},{32,96},{64,0},{96,32},{1,65},{33,97},{65,1},{97,33},{2,66}... | collective-permute-start | bytes 786440 | tf_op jit(solution)/shard_map/ppermute | solution.py:327
  71.2 15.9 %collective-permute-start.22 = (bf16[16,8192]{1,0:T(8,128)(2,1)S(1)}, bf16[16,8192]{1,0:T(8,128)(2,1)}, u32[]{:S(2)}, u32[]{:S(2)}) collective-permute-start(bf16[16,8192]{1,0:T(8,128)(2,1)S(1)} %get-tuple-element.41), channel_id=1, source_target_pairs={{0,96},{32,0},{64,32},{96,64},{1,97},{33,1},{65,33},{97,65},{2,98}... | collective-permute-start | bytes 786440 | tf_op jit(solution)/shard_map/ppermute | solution.py:327
  72.3 7.7 %collective-permute-start.28 = (f32[16,256]{1,0:T(8,128)S(1)}, f32[16,256]{1,0:T(8,128)S(1)}, u32[]{:S(2)}, u32[]{:S(2)}) collective-permute-start(f32[16,256]{1,0:T(8,128)S(1)} %get-tuple-element.42), channel_id=1, source_target_pairs={{0,32},{32,64},{64,96},{96,0},{1,33},{33,65},{65,97},{97,1},{2,34}... | collective-permute-start | bytes 49160 | tf_op jit(solution)/shard_map/ppermute | solution.py:336
  72.8 12.0 %collective-permute-start.30 = (f32[16,256]{1,0:T(8,128)S(1)}, f32[16,256]{1,0:T(8,128)S(1)}, u32[]{:S(2)}, u32[]{:S(2)}) collective-permute-start(f32[16,256]{1,0:T(8,128)S(1)} %get-tuple-element.43), channel_id=1, source_target_pairs={{0,64},{32,96},{64,0},{96,32},{1,65},{33,97},{65,1},{97,33},{2,66}... | collective-permute-start | bytes 49160 | tf_op jit(solution)/shard_map/ppermute | solution.py:336
  80.0 7.1 %collective-permute-start.29 = (f32[16,256]{1,0:T(8,128)S(1)}, f32[16,256]{1,0:T(8,128)S(1)}, u32[]{:S(2)}, u32[]{:S(2)}) collective-permute-start(f32[16,256]{1,0:T(8,128)S(1)} %get-tuple-element.44), channel_id=1, source_target_pairs={{0,96},{32,0},{64,32},{96,64},{1,97},{33,1},{65,33},{97,65},{2,98}... | collective-permute-start | bytes 49160 | tf_op jit(solution)/shard_map/ppermute | solution.py:336
  84.7 11.9 %collective-permute-start.4 = (bf16[512,512]{1,0:T(8,128)(2,1)S(1)}, bf16[512,512]{1,0:T(8,128)(2,1)S(1)}, u32[]{:S(2)}, u32[]{:S(2)}) collective-permute-start(bf16[512,512]{1,0:T(8,128)(2,1)S(1)} %weight.1.refs_4_), channel_id=1, source_target_pairs={{0,7},{1,0},{2,1},{3,2},{4,3},{5,4},{6,5},{7,6},{8,15},{9,8},{10,9... | collective-permute-start | bytes 1572872 | tf_op jit(solution)/shard_map/ppermute | solution.py:296
  87.1 12.9 %collective-permute-start.3 = (bf16[512,512]{1,0:T(8,128)(2,1)S(1)}, bf16[512,512]{1,0:T(8,128)(2,1)S(1)}, u32[]{:S(2)}, u32[]{:S(2)}) collective-permute-start(bf16[512,512]{1,0:T(8,128)(2,1)S(1)} %weight.1.refs_4_), channel_id=1, source_target_pairs={{0,1},{1,2},{2,3},{3,4},{4,5},{5,6},{6,7},{7,0},{8,9},{9,10},{10,1... | collective-permute-start | bytes 1572872 | tf_op jit(solution)/shard_map/ppermute | solution.py:295
  90.3 58.9 %all-to-all-start.1 = ((f32[16,16,768]{2,1,0:T(8,128)}), f32[16,16,768]{2,1,0:T(8,128)}, u32[]{:S(2)}, u32[]{:S(2)}) async-start(f32[16,16,768]{2,1,0:T(8,128)} %copy.24), calls=%async_computation.1 | async-start | bytes 1572864 | tf_op jit(solution)/shard_map/all_to_all | solution.py:340
  96.6 29.1 %collective-permute-start.9 = (bf16[512,512]{1,0:T(8,128)(2,1)S(1)}, bf16[512,512]{1,0:T(8,128)(2,1)S(1)}, u32[]{:S(2)}, u32[]{:S(2)}) collective-permute-start(bf16[512,512]{1,0:T(8,128)(2,1)S(1)} %collective-permute-done.4.refs_6_), channel_id=1, source_target_pairs={{0,7},{1,0},{2,1},{3,2},{4,3},{5,4},{6,5},{7,6},{8,15},{9,8},{10,9... | collective-permute-start | bytes 1572872 | tf_op jit(solution)/shard_map/ppermute | solution.py:296
  100.0 28.1 %collective-permute-start.8 = (bf16[512,512]{1,0:T(8,128)(2,1)S(1)}, bf16[512,512]{1,0:T(8,128)(2,1)S(1)}, u32[]{:S(2)}, u32[]{:S(2)}) collective-permute-start(bf16[512,512]{1,0:T(8,128)(2,1)S(1)} %collective-permute-done.3.refs_5_), channel_id=1, source_target_pairs={{0,1},{1,2},{2,3},{3,4},{4,5},{5,6},{6,7},{7,0},{8,9},{9,10},{10,1... | collective-permute-start | bytes 1572872 | tf_op jit(solution)/shard_map/ppermute | solution.py:295
  100.0 0.8 copy-start.9
  125.7 17.9 %copy-start.7 = (bf16[512,512]{1,0:T(8,128)(2,1)}, bf16[512,512]{1,0:T(8,128)(2,1)S(1)}, u32[]{:S(2)}) copy-start(bf16[512,512]{1,0:T(8,128)(2,1)S(1)} %collective-permute-done.9.refs_5_) | copy-start | bytes 1572868
  125.7 17.1 %collective-permute-start.11 = (bf16[512,512]{1,0:T(8,128)(2,1)S(1)}, bf16[512,512]{1,0:T(8,128)(2,1)S(1)}, u32[]{:S(2)}, u32[]{:S(2)}) collective-permute-start(bf16[512,512]{1,0:T(8,128)(2,1)S(1)} %collective-permute-done.9.refs_5_), channel_id=1, source_target_pairs={{0,7},{1,0},{2,1},{3,2},{4,3},{5,4},{6,5},{7,6},{8,15},{9,8},{10,9... | collective-permute-start | bytes 1572872 | tf_op jit(solution)/shard_map/ppermute | solution.py:296
  128.1 15.5 %copy-start.11 = (bf16[512,512]{1,0:T(8,128)(2,1)}, bf16[512,512]{1,0:T(8,128)(2,1)S(1)}, u32[]{:S(2)}) copy-start(bf16[512,512]{1,0:T(8,128)(2,1)S(1)} %collective-permute-done.8.refs_4_) | copy-start | bytes 1572868
  128.1 18.4 %collective-permute-start.10 = (bf16[512,512]{1,0:T(8,128)(2,1)S(1)}, bf16[512,512]{1,0:T(8,128)(2,1)S(1)}, u32[]{:S(2)}, u32[]{:S(2)}) collective-permute-start(bf16[512,512]{1,0:T(8,128)(2,1)S(1)} %collective-permute-done.8.refs_4_), channel_id=1, source_target_pairs={{0,1},{1,2},{2,3},{3,4},{4,5},{5,6},{6,7},{7,0},{8,9},{9,10},{10,1... | collective-permute-start | bytes 1572872 | tf_op jit(solution)/shard_map/ppermute | solution.py:295
  128.1 7.5 %collective-permute-start.2 = (bf16[160,512]{1,0:T(8,128)(2,1)S(1)}, bf16[160,512]{1,0:T(8,128)(2,1)S(1)}, u32[]{:S(2)}, u32[]{:S(2)}) collective-permute-start(bf16[160,512]{1,0:T(8,128)(2,1)S(1)} %get-tuple-element.21.refs_0_.grads), channel_id=1, source_target_pairs={{0,152},{16,8},{8,16},{24,128},{128,24},{144,136},{136,144},{152,0... | collective-permute-start | bytes 491528 | tf_op jit(solution)/shard_map/ppermute | solution.py:318
  131.7 5.1 %collective-permute-start.1 = (bf16[160,512]{1,0:T(8,128)(2,1)S(1)}, bf16[160,512]{1,0:T(8,128)(2,1)S(1)}, u32[]{:S(2)}, u32[]{:S(2)}) collective-permute-start(bf16[160,512]{1,0:T(8,128)(2,1)S(1)} %get-tuple-element.21.refs_0_.grads), channel_id=1, source_target_pairs={{0,8},{16,152},{8,128},{24,16},{128,136},{144,24},{136,0},{152,144... | collective-permute-start | bytes 491528 | tf_op jit(solution)/shard_map/ppermute | solution.py:317
  133.6 3.1 %collective-permute-start = (bf16[160,512]{1,0:T(8,128)(2,1)S(1)}, bf16[160,512]{1,0:T(8,128)(2,1)S(1)}, u32[]{:S(2)}, u32[]{:S(2)}) collective-permute-start(bf16[160,512]{1,0:T(8,128)(2,1)S(1)} %get-tuple-element.21.refs_0_.grads), channel_id=1, source_target_pairs={{0,16},{16,0},{1,17},{17,1},{2,18},{18,2},{3,19},{19,3},{4,20},{20... | collective-permute-start | bytes 491528 | tf_op jit(solution)/shard_map/ppermute | solution.py:316
  135.6 8.0 %copy-start.13 = (bf16[160,512]{1,0:T(8,128)(2,1)}, bf16[160,512]{1,0:T(8,128)(2,1)S(1)}, u32[]{:S(2)}) copy-start(bf16[160,512]{1,0:T(8,128)(2,1)S(1)} %collective-permute-done.2.refs_3_) | copy-start | bytes 491524
  136.8 6.8 %copy-start.16 = (bf16[160,512]{1,0:T(8,128)(2,1)}, bf16[160,512]{1,0:T(8,128)(2,1)S(1)}, u32[]{:S(2)}) copy-start(bf16[160,512]{1,0:T(8,128)(2,1)S(1)} %collective-permute-done.1.refs_2_) | copy-start | bytes 491524
  136.8 1.1 copy-start.10
  137.9 5.7 %copy-start.18 = (bf16[160,512]{1,0:T(8,128)(2,1)}, bf16[160,512]{1,0:T(8,128)(2,1)S(1)}, u32[]{:S(2)}) copy-start(bf16[160,512]{1,0:T(8,128)(2,1)S(1)} %collective-permute-done.refs_1_) | copy-start | bytes 491524
  140.8 23.5 %collective-permute-start.5 = (bf16[160,1536]{1,0:T(8,128)(2,1)}, bf16[160,1536]{1,0:T(8,128)(2,1)S(1)}, u32[]{:S(2)}, u32[]{:S(2)}) collective-permute-start(bf16[160,1536]{1,0:T(8,128)(2,1)} %get-tuple-element.23), channel_id=1, source_target_pairs={{0,16},{16,0},{1,17},{17,1},{2,18},{18,2},{3,19},{19,3},{4,20},{20... | collective-permute-start | bytes 1474568 | tf_op jit(solution)/shard_map/ppermute | solution.py:360
  143.6 21.3 %collective-permute-start.16 = (bf16[256,512]{1,0:T(8,128)(2,1)}, bf16[256,512]{1,0:T(8,128)(2,1)S(1)}, u32[]{:S(2)}, u32[]{:S(2)}) collective-permute-start(bf16[256,512]{1,0:T(8,128)(2,1)} %slice.27), channel_id=1, source_target_pairs={{0,7},{1,0},{2,1},{3,2},{4,3},{5,4},{6,5},{7,6},{8,15},{9,8},{10,9... | collective-permute-start | bytes 786440 | tf_op jit(solution)/shard_map/ppermute | solution.py:299
  147.3 17.6 %collective-permute-start.15 = (bf16[256,512]{1,0:T(8,128)(2,1)}, bf16[256,512]{1,0:T(8,128)(2,1)}, u32[]{:S(2)}, u32[]{:S(2)}) collective-permute-start(bf16[256,512]{1,0:T(8,128)(2,1)} %slice.26), channel_id=1, source_target_pairs={{0,1},{1,2},{2,3},{3,4},{4,5},{5,6},{6,7},{7,0},{8,9},{9,10},{10,1... | collective-permute-start | bytes 786440 | tf_op jit(solution)/shard_map/ppermute | solution.py:298
  147.3 21.1 %collective-permute-start.6 = (bf16[160,1536]{1,0:T(8,128)(2,1)}, bf16[160,1536]{1,0:T(8,128)(2,1)S(1)}, u32[]{:S(2)}, u32[]{:S(2)}) collective-permute-start(bf16[160,1536]{1,0:T(8,128)(2,1)} %get-tuple-element.24), channel_id=1, source_target_pairs={{8,0},{152,16},{128,8},{16,24},{136,128},{24,144},{0,136},{144,152... | collective-permute-start | bytes 1474568 | tf_op jit(solution)/shard_map/ppermute | solution.py:361
  147.3 22.6 %collective-permute-start.7 = (bf16[160,1536]{1,0:T(8,128)(2,1)}, bf16[160,1536]{1,0:T(8,128)(2,1)S(1)}, u32[]{:S(2)}, u32[]{:S(2)}) collective-permute-start(bf16[160,1536]{1,0:T(8,128)(2,1)} %get-tuple-element.25), channel_id=1, source_target_pairs={{152,0},{8,16},{16,8},{128,24},{24,128},{136,144},{144,136},{0,152... | collective-permute-start | bytes 1474568 | tf_op jit(solution)/shard_map/ppermute | solution.py:362
  151.3 39.3 %all-to-all-start.2 = ((f32[16,16,768]{2,1,0:T(8,128)}), f32[16,16,768]{2,1,0:T(8,128)}, u32[]{:S(2)}, u32[]{:S(2)}) async-start(f32[16,16,768]{2,1,0:T(8,128)} %broadcast_in_dim.11), calls=%async_computation.2 | async-start | bytes 1572864 | tf_op jit(solution)/shard_map/all_to_all | solution.py:342
  156.5 1.0 copy-start.8
  157.6 1.0 copy-start.12
  158.6 0.9 copy-start.14
  159.5 0.9 copy-start.17
  160.5 0.9 copy-start.19
  161.4 5.2 %copy-start.15 = (bf16[160,512]{1,0:T(8,128)(2,1)S(1)}, bf16[160,512]{1,0:T(8,128)(2,1)}, u32[]{:S(2)}) copy-start(bf16[160,512]{1,0:T(8,128)(2,1)} %copy-done.13) | copy-start | bytes 491524
  164.3 23.2 %collective-permute-start.12 = (bf16[160,2048]{1,0:T(8,128)(2,1)S(1)}, bf16[160,2048]{1,0:T(8,128)(2,1)S(1)}, u32[]{:S(2)}, u32[]{:S(2)}) collective-permute-start(bf16[160,2048]{1,0:T(8,128)(2,1)S(1)} %get-tuple-element.27), channel_id=1, source_target_pairs={{0,16},{16,0},{1,17},{17,1},{2,18},{18,2},{3,19},{19,3},{4,20},{20... | collective-permute-start | bytes 1966088 | tf_op jit(solution)/shard_map/ppermute | solution.py:360
  164.9 22.6 %collective-permute-start.13 = (bf16[160,2048]{1,0:T(8,128)(2,1)S(1)}, bf16[160,2048]{1,0:T(8,128)(2,1)S(1)}, u32[]{:S(2)}, u32[]{:S(2)}) collective-permute-start(bf16[160,2048]{1,0:T(8,128)(2,1)S(1)} %get-tuple-element.28), channel_id=1, source_target_pairs={{8,0},{152,16},{128,8},{16,24},{136,128},{24,144},{0,136},{144,152... | collective-permute-start | bytes 1966088 | tf_op jit(solution)/shard_map/ppermute | solution.py:361
  164.9 22.6 %collective-permute-start.14 = (bf16[160,2048]{1,0:T(8,128)(2,1)S(1)}, bf16[160,2048]{1,0:T(8,128)(2,1)S(1)}, u32[]{:S(2)}, u32[]{:S(2)}) collective-permute-start(bf16[160,2048]{1,0:T(8,128)(2,1)S(1)} %get-tuple-element.29), channel_id=1, source_target_pairs={{152,0},{8,16},{16,8},{128,24},{24,128},{136,144},{144,136},{0,152... | collective-permute-start | bytes 1966088 | tf_op jit(solution)/shard_map/ppermute | solution.py:362
  168.4 2.5 %collective-permute-start.17 = (bf16[160,512]{1,0:T(8,128)(2,1)S(1)}, bf16[160,512]{1,0:T(8,128)(2,1)S(1)}, u32[]{:S(2)}, u32[]{:S(2)}) collective-permute-start(bf16[160,512]{1,0:T(8,128)(2,1)S(1)} %get-tuple-element.31), channel_id=1, source_target_pairs={{0,16},{16,0},{1,17},{17,1},{2,18},{18,2},{3,19},{19,3},{4,20},{20... | collective-permute-start | bytes 491528 | tf_op jit(solution)/shard_map/ppermute | solution.py:360
  169.8 16.0 %collective-permute-start.18 = (bf16[160,512]{1,0:T(8,128)(2,1)S(1)}, bf16[160,512]{1,0:T(8,128)(2,1)S(1)}, u32[]{:S(2)}, u32[]{:S(2)}) collective-permute-start(bf16[160,512]{1,0:T(8,128)(2,1)S(1)} %get-tuple-element.32), channel_id=1, source_target_pairs={{8,0},{152,16},{128,8},{16,24},{136,128},{24,144},{0,136},{144,152... | collective-permute-start | bytes 491528 | tf_op jit(solution)/shard_map/ppermute | solution.py:361
  170.9 16.6 %collective-permute-start.19 = (bf16[160,512]{1,0:T(8,128)(2,1)S(1)}, bf16[160,512]{1,0:T(8,128)(2,1)S(1)}, u32[]{:S(2)}, u32[]{:S(2)}) collective-permute-start(bf16[160,512]{1,0:T(8,128)(2,1)S(1)} %get-tuple-element.33), channel_id=1, source_target_pairs={{152,0},{8,16},{16,8},{128,24},{24,128},{136,144},{144,136},{0,152... | collective-permute-start | bytes 491528 | tf_op jit(solution)/shard_map/ppermute | solution.py:362

commit v2 on v1

v2 whole, which is shorter than its diff:
```python
import functools

import jax
import jax.numpy as jnp
from jax import lax
from jax.experimental import pallas as pl
from jax.experimental.pallas import tpu as pltpu
from jax.sharding import Mesh, PartitionSpec as P

HEAD = 128
RANK = 64
BLOCK = 64
WIDTH = 16384
KEYS = 512
ROWS = 160
SHARDS = 16
NZ = 8
HALF = 512
PACKET = NZ * RANK + ROWS
IDS = 16
ROPE_BASE = 500000.0
SCALE = 16.0 / RANK
TOKENS = 40960

BF = jnp.bfloat16
F32 = jnp.float32

X_AXES = ("xh", "c", "xl")
SHARD_AXES = ("xl", "z")
DP_AXES = ("xh", "y", "c")


BRIEF = pl.CostEstimate(flops=1, bytes_accessed=1, transcendentals=0)


def params(mib):
    return pltpu.CompilerParams(vmem_limit_bytes=mib * 1024 * 1024)


def dot(a, b, ca, cb):
    return lax.dot_general(a, b, (((ca,), (cb,)), ((), ())), preferred_element_type=F32)


def weight_kernel(idx, levels, scales, second, down, up, ids, weight, packet):
    half = down[...]
    for k in range(NZ):
        packet[k, :RANK, :] = half
        packet[k, RANK:, :] = ids[...]
    scale = scales[...].astype(F32)
    n = HALF // BLOCK
    scale = jnp.where(idx[0] == 0, scale[:n], scale[n:])
    rows = []
    for j in range(n):
        level = levels[j * BLOCK : (j + 1) * BLOCK, :].astype(F32)
        rows.append((level * scale[j : j + 1]) * second[...])
    base = dot(up[...], half, 0, 0) * SCALE
    weight[...] = (jnp.concatenate(rows, axis=0).T + base).astype(BF)


def local_weight(idx, levels, scales, second, down, up, ids):
    full = lambda shape: pl.BlockSpec(shape, lambda i, s: (0,) * len(shape))
    return pl.pallas_call(
        weight_kernel,
        grid_spec=pltpu.PrefetchScalarGridSpec(
            num_scalar_prefetch=1,
            grid=(1,),
            in_specs=[
                pl.BlockSpec((HALF, KEYS), lambda i, s: (s[0], 0)),
                full(scales.shape),
                full((1, KEYS)),
                pl.BlockSpec((RANK, HALF), lambda i, s: (0, s[0])),
                full((RANK, KEYS)),
                full((IDS, HALF)),
            ],
            out_specs=[full((KEYS, HALF)), full((NZ, RANK + IDS, HALF))],
        ),
        out_shape=[
            jax.ShapeDtypeStruct((KEYS, HALF), BF),
            jax.ShapeDtypeStruct((NZ, RANK + IDS, HALF), BF),
        ],
        compiler_params=params(56),
        cost_estimate=BRIEF,
        name="weight",
    )(idx, levels, scales, second, down, up, ids)


def grads_kernel(idx, everyone, own, rotated, freqs, up, packet, low):
    mine = own[...]
    count = jnp.zeros((ROWS, HALF), F32)
    for k in range(NZ):
        packet[k * RANK : (k + 1) * RANK, :] = everyone[k, :RANK, :]
        row = everyone[k, RANK : RANK + 1, :].astype(F32)
        count = count + jnp.where(row < mine, 1.0, 0.0)
    first = jnp.sum(count, axis=1, keepdims=True)
    place = lax.broadcasted_iota(jnp.int32, (ROWS, 1), 0) + idx[3] * ROWS
    position = place.astype(F32) - first
    angle = position * freqs[...]
    cosine = jnp.cos(angle)
    lane = lax.broadcasted_iota(jnp.int32, (ROWS, HEAD), 1)
    sine = jnp.where(lane < HEAD // 2, 1.0, -1.0) * jnp.sin(angle)
    for h in range(KEYS // HEAD):
        cols = slice(h * HEAD, (h + 1) * HEAD)
        g = rotated[:, cols].astype(F32)
        packet[NZ * RANK :, cols] = (g * cosine + pltpu.roll(g, HEAD // 2, 1) * sine).astype(BF)
    low[...] = dot(up[...], packet[NZ * RANK :, :], 1, 1).astype(BF)


def make_grads(idx, everyone, own, rotated, freqs, up):
    full = lambda shape: pl.BlockSpec(shape, lambda i, s: (0,) * len(shape))
    return pl.pallas_call(
        grads_kernel,
        grid_spec=pltpu.PrefetchScalarGridSpec(
            num_scalar_prefetch=1,
            grid=(1,),
            in_specs=[
                full(everyone.shape),
                full((ROWS, 1)),
                full((ROWS, KEYS)),
                full((1, HEAD)),
                full((RANK, KEYS)),
            ],
            out_specs=[full((PACKET, KEYS)), full((RANK, ROWS))],
        ),
        out_shape=[jax.ShapeDtypeStruct((PACKET, KEYS), BF), jax.ShapeDtypeStruct((RANK, ROWS), BF)],
        compiler_params=params(56),
        cost_estimate=BRIEF,
        name="grads",
    )(idx, everyone, own, rotated, freqs, up)


CHUNKS = 8
WIDE = WIDTH // CHUNKS
STEP = WIDE // (2 * HALF)


def down_kernel(idx, low, tokens, keep, send, held, keep_held, send_held, sems):
    c = idx[0]
    loads = [
        pltpu.make_async_copy(tokens.at[:, pl.ds(i * WIDE, WIDE)], held.at[i], sems.at[i]) for i in range(CHUNKS)
    ]
    for load in loads:
        load.start()
    stores = []
    for i in range(CHUNKS):
        loads[i].wait()
        for k in range(STEP):
            at = (i * STEP + k) * HALF
            mine = pl.multiple_of(k * 2 * HALF + c * HALF, HALF)
            other = pl.multiple_of(k * 2 * HALF + (1 - c) * HALF, HALF)
            send_held[:, at : at + HALF] = dot(low[...], held[i, :, pl.ds(other, HALF)], 1, 0).astype(BF)
            keep_held[:, at : at + HALF] = dot(low[...], held[i, :, pl.ds(mine, HALF)], 1, 0)
        cols = pl.ds(i * STEP * HALF, STEP * HALF)
        stores.append(pltpu.make_async_copy(send_held.at[:, cols], send.at[:, cols], sems.at[CHUNKS + 2 * i]))
        stores.append(pltpu.make_async_copy(keep_held.at[:, cols], keep.at[:, cols], sems.at[CHUNKS + 2 * i + 1]))
        stores[-2].start()
        stores[-1].start()
    for store in stores:
        store.wait()


def down_part(idx, low, tokens):
    anywhere = pl.BlockSpec(memory_space=pl.ANY)
    return pl.pallas_call(
        down_kernel,
        in_specs=[pl.BlockSpec(memory_space=pltpu.SMEM), pl.BlockSpec(memory_space=pltpu.VMEM), anywhere],
        out_specs=[anywhere, anywhere],
        out_shape=[
            jax.ShapeDtypeStruct((RANK, WIDTH // 2), F32),
            jax.ShapeDtypeStruct((RANK, WIDTH // 2), BF),
        ],
        scratch_shapes=[
            pltpu.VMEM((CHUNKS, ROWS, WIDE), BF),
            pltpu.VMEM((RANK, WIDTH // 2), F32),
            pltpu.VMEM((RANK, WIDTH // 2), BF),
            pltpu.SemaphoreType.DMA((3 * CHUNKS,)),
        ],
        compiler_params=params(56),
        cost_estimate=BRIEF,
        name="down",
    )(idx, low, tokens)


def up_kernel(idx, tokens, p0, p1, p2, p3, out, held, lows, grads, sems):
    c, x = idx[0], idx[2]
    loads = []
    for i in range(CHUNKS):
        xl = x if i < CHUNKS // 2 else 1 - x
        at = pl.multiple_of(xl * (WIDTH // 2) + (i % (CHUNKS // 2)) * WIDE, WIDE)
        loads.append(pltpu.make_async_copy(tokens.at[:, pl.ds(at, WIDE)], held.at[i], sems.at[i]))
    pieces = [
        pltpu.make_async_copy(p.at[pl.ds(0, NZ * RANK), :], lows.at[k], sems.at[CHUNKS + k])
        for k, p in enumerate((p0, p1, p2, p3))
    ]
    last = pltpu.make_async_copy(p0.at[pl.ds(NZ * RANK, ROWS), :], grads, sems.at[CHUNKS + 4])
    for copy in pieces[:2] + loads[: CHUNKS // 2] + pieces[2:] + loads[CHUNKS // 2 :] + [last]:
        copy.start()
    total = jnp.zeros((ROWS, RANK), F32)
    for i in range(CHUNKS):
        first = 0 if i < CHUNKS // 2 else 2
        if i % (CHUNKS // 2) == 0:
            pieces[first].wait()
            pieces[first + 1].wait()
        loads[i].wait()
        for k in range(STEP):
            z = (i % (CHUNKS // 2)) * STEP + k
            rows = slice(z * RANK, (z + 1) * RANK)
            mine = pl.multiple_of(k * 2 * HALF + c * HALF, HALF)
            other = pl.multiple_of(k * 2 * HALF + (1 - c) * HALF, HALF)
            total = total + dot(held[i, :, pl.ds(mine, HALF)], lows[first, rows, :], 1, 1)
            total = total + dot(held[i, :, pl.ds(other, HALF)], lows[first + 1, rows, :], 1, 1)
    last.wait()
    out[...] = dot(total.astype(BF), grads[...], 0, 0)


def up_part(idx, tokens, packets):
    anywhere = pl.BlockSpec(memory_space=pl.ANY)
    return pl.pallas_call(
        up_kernel,
        in_specs=[pl.BlockSpec(memory_space=pltpu.SMEM)] + [anywhere] * 5,
        out_specs=pl.BlockSpec(memory_space=pltpu.VMEM),
        out_shape=jax.ShapeDtypeStruct((RANK, KEYS), F32),
        scratch_shapes=[
            pltpu.VMEM((CHUNKS, ROWS, WIDE), BF),
            pltpu.VMEM((4, NZ * RANK, HALF), BF),
            pltpu.VMEM((ROWS, KEYS), BF),
            pltpu.SemaphoreType.DMA((CHUNKS + 5,)),
        ],
        compiler_params=params(56),
        cost_estimate=BRIEF,
        name="up",
    )(idx, tokens, *packets)


def block_kernel(own, core, there, across, weight, out_own, out_core, out_there, out_across, rows):
    @pl.when(pl.program_id(0) == 0)
    def _():
        for k, source in enumerate((own, core, there, across)):
            rows[k * ROWS : (k + 1) * ROWS, :] = source[NZ * RANK :, :]

    product = dot(rows[...], weight[...], 1, 0).astype(BF)
    for k, out in enumerate((out_own, out_core, out_there, out_across)):
        out[...] = product[k * ROWS : (k + 1) * ROWS]


def blocks(sources, weight, start, count):
    source = pl.BlockSpec((PACKET, KEYS), lambda i: (0, 0))
    out = pl.BlockSpec((ROWS, HALF), lambda i: (0, i))
    return pl.pallas_call(
        block_kernel,
        grid=(count,),
        in_specs=[source] * 4 + [pl.BlockSpec((KEYS, HALF), lambda i: (start + i, 0))],
        out_specs=[out] * 4,
        out_shape=[jax.ShapeDtypeStruct((ROWS, count * HALF), BF)] * 4,
        scratch_shapes=[pltpu.VMEM((4 * ROWS, KEYS), BF)],
        compiler_params=params(56),
        cost_estimate=BRIEF,
        name="blocks",
    )(*sources, weight)


def assemble_kernel(start, count, idx, own, core, there, across, *rest):
    out, sems = rest[-2:]
    copies = []
    for k, piece in enumerate((own, core, there, across)):
        x = idx[2] if k < 2 else 1 - idx[2]
        h = idx[0] if k % 2 == 0 else 1 - idx[0]
        for j in range(count):
            col = pl.multiple_of(((x * NZ + start + j) * 2 + h) * HALF, HALF)
            copies.append(
                pltpu.make_async_copy(
                    piece.at[:, pl.ds(j * HALF, HALF)],
                    out.at[:, pl.ds(col, HALF)],
                    sems.at[len(copies)],
                )
            )
    for copy in copies:
        copy.start()
    for copy in copies:
        copy.wait()


def assemble(idx, pieces, start, count, before):
    anywhere = pl.BlockSpec(memory_space=pl.ANY)
    return pl.pallas_call(
        functools.partial(assemble_kernel, start, count),
        in_specs=[pl.BlockSpec(memory_space=pltpu.SMEM)]
        + [pl.BlockSpec(memory_space=pltpu.VMEM)] * 4
        + [anywhere] * len(before),
        out_specs=anywhere,
        scratch_shapes=[pltpu.SemaphoreType.DMA((4 * count,))],
        out_shape=jax.ShapeDtypeStruct((ROWS, WIDTH), BF),
        input_output_aliases={5: 0} if before else {},
        compiler_params=params(8),
        cost_estimate=BRIEF,
        name="assemble",
    )(idx, *pieces, *before)


def x_permutation(swap):
    at = lambda x, c: ((x // 2) * 2 + c) * 2 + x % 2
    pairs = []
    for x in range(4):
        for c in range(2):
            if (c ^ swap) == 0:
                pairs.append((at(x, c), at((x + 1) % 4, 0)))
            else:
                pairs.append((at(x, c), at((x - 1) % 4, 1)))
    return pairs


def inverse(pairs):
    return [(b, a) for a, b in pairs]


CORE = [(0, 1), (1, 0)]


def on_device(tokens, rotated, documents, levels, scales, second, down, up):
    xh, y, c, xl, z = (lax.axis_index(a) for a in ("xh", "y", "c", "xl", "z"))
    idx = jnp.stack([c, xh, xl, xl * NZ + z]).astype(jnp.int32)

    ids = jnp.pad(documents.astype(BF), ((0, 0), (0, HALF // 2 - ROWS)), constant_values=1000.0)
    ids = jnp.concatenate([ids, lax.ppermute(ids, "xl", CORE)], axis=1)
    ids = jnp.broadcast_to(ids, (IDS, HALF))

    weight, packet = local_weight(idx, levels, scales, second, down.T, up, ids)
    weight = lax.all_gather(weight, "z", tiled=True)
    everyone = lax.all_to_all(packet, "z", 0, 0, tiled=True)

    half = HEAD // 2
    freqs = ROPE_BASE ** (-jnp.arange(half, dtype=F32) * 2.0 / HEAD)
    freqs = jnp.concatenate([freqs, freqs])[None, :]
    own = documents.astype(F32).reshape(ROWS, 1)
    packet, low = make_grads(idx, everyone, own, rotated, freqs, up)

    there, across = x_permutation(0), x_permutation(1)
    packets = [
        packet,
        lax.ppermute(packet, "c", CORE),
        lax.ppermute(packet, X_AXES, there),
        lax.ppermute(packet, X_AXES, across),
    ]

    keep, send = down_part(idx, low, tokens)
    sent = [lax.ppermute(part, "c", CORE) for part in jnp.split(send, 2, axis=0)]
    total = keep + jnp.concatenate(sent, axis=0).astype(F32)
    total = total.reshape(4, RANK // 4, WIDTH // 2)
    mine = lax.dynamic_index_in_dim(total, y, 0, keepdims=False)
    for d in (1, 3, 2):
        out = lax.dynamic_index_in_dim(total, (y + d) % 4, 0, keepdims=False).astype(BF)
        mine = mine + lax.ppermute(out, "y", [(i, (i + d) % 4) for i in range(4)]).astype(F32)

    up_total = up_part(idx, tokens, packets).reshape(8, 8, KEYS)
    up_total = jnp.sum(lax.all_to_all(up_total, ("y", "c"), 0, 0, tiled=True), axis=0)

    slabs = mine.reshape(RANK // 4, SHARDS, HALF).transpose(1, 0, 2)
    up_total = jnp.broadcast_to(up_total[None], (SHARDS,) + up_total.shape)
    slabs = jnp.concatenate([slabs, up_total], axis=1).astype(BF)
    slabs = lax.all_to_all(slabs, SHARD_AXES, 0, 0, tiled=True)
    slabs = jnp.sum(slabs.astype(F32), axis=0).astype(BF)
    slabs = jnp.broadcast_to(slabs[None], (16,) + slabs.shape)
    slabs = lax.all_to_all(slabs, DP_AXES, 0, 0, tiled=True).astype(F32)
    slabs = slabs.reshape(2, 4, 2, RANK // 4 + 8, KEYS)
    factor = SCALE / jnp.sqrt(jnp.float32(TOKENS))
    slabs = factor * (slabs[0] + slabs[1])
    grad_down = slabs[:, :, : RANK // 4].transpose(1, 3, 0, 2).reshape(2 * HALF, RANK)
    grad_up = slabs[:, :, RANK // 4 :].reshape(RANK, KEYS)

    grad_tokens = []
    for start, count in ((0, 4), (4, 4)):
        o, p, a, b = blocks(packets, weight, start, count)
        pieces = [
            o,
            lax.ppermute(p, "c", CORE),
            lax.ppermute(a, X_AXES, inverse(there)),
            lax.ppermute(b, X_AXES, inverse(across)),
        ]
        grad_tokens = [assemble(idx, pieces, start, count, grad_tokens)]
    grad_tokens = grad_tokens[0]
    return grad_tokens, grad_down, grad_up


def solution(mesh):
    fine = Mesh(mesh.devices.reshape(2, 4, 2, 2, 8), ("xh", "y", "c", "xl", "z"))
    everything = DP_AXES + SHARD_AXES
    in_specs = (
        P(everything, None),
        P(everything, None),
        P(DP_AXES, SHARD_AXES),
        P(SHARD_AXES, None),
        P(SHARD_AXES, None),
        P(),
        P(SHARD_AXES, None),
        P(),
    )
    out_specs = (P(everything, None), P(SHARD_AXES, None), P())
    return jax.shard_map(on_device, mesh=fine, in_specs=in_specs, out_specs=out_specs, check_vma=False)
```

time: 194 us -> 162 us (0.84)
  waiting for transfers between devices: 80.6 us -> 51.3 us
  starting transfers between devices: 62.3 us -> 44.7 us
  between operations: 1.02 us -> 14.2 us
  Pallas kernels: 22.5 us -> 34 us
  local copies, waits for them, and re-layouts: 21 us -> 9.85 us
    ppermute x19 -> x6, waiting for transfers between devices: 49.7 us -> 8.38 us  [the longest x1 8.03 us: on_device(): lax.ppermute(packet, X_AXES, across)]
    ppermute x19 -> x6, starting transfers between devices: 27.9 us -> 7.85 us  [the longest x2 2.65 us: on_device(): lax.ppermute(part, 'c', CORE)]
    unnamed x48 -> x20, local copies, waits for them, and re-layouts: 14.3 us -> 3.39 us
    all_to_all x3 -> x4, waiting for transfers between devices: 14.8 us -> 25.3 us  [the longest x1 17.1 us: on_device(): everyone = lax.all_to_all(packet, 'z', 0, 0, tiled=True)]
    ppermute x3 -> x2, waiting for transfers between devices: 1.59 us -> 10.4 us  [on_device(): lax.ppermute(b, X_AXES, inverse(across))]
    pallas_call x6, Pallas kernels: 20.3 us -> 27.4 us  [the longest x2 11.2 us: blocks(): pl.pallas_call(block_kernel, grid=(count,), in_specs=[source] * 4 + [pl.B...]
    ppermute x3 -> x2, waiting for transfers between devices: 13.5 us -> 7.18 us  [on_device(): lax.ppermute(a, X_AXES, inverse(there))]
    all_to_all x3 -> x4, starting transfers between devices: 20.2 us -> 23.5 us  [the longest x1 8.44 us: on_device(): everyone = lax.all_to_all(packet, 'z', 0, 0, tiled=True)]
  transfers between devices with their start and end apart: 34 -> 20, of which waited for: 11 -> 9; matrix products, arithmetic and copies ran while one was open for 5% -> 8% of each run, Pallas kernels for 6% -> 18%
where the time goes in v2:
time: 162 us; the launch traced here: 161 us
  waiting for transfers between devices  51.3 us (32%)
  starting transfers between devices  44.7 us (28%)
  Pallas kernels  34 us (21%)
  between operations  14.2 us (9%)
  local copies, waits for them, and re-layouts  9.85 us (6%)
  other arithmetic  6.54 us (4%)
    all_to_all x1, waiting for transfers between devices, on_device(): everyone = lax.all_to_all(packet, 'z', 0, 0, tiled=True)  17.1 us
    pallas_call x2, Pallas kernels, blocks(): pl.pallas_call(block_kernel, grid=(count,), in_specs=[source] * 4 + [pl.B...  11.2 us
    ppermute x2, waiting for transfers between devices, on_device(): lax.ppermute(b, X_AXES, inverse(across))  10.4 us
    all_to_all x1, starting transfers between devices, on_device(): everyone = lax.all_to_all(packet, 'z', 0, 0, tiled=True)  8.44 us
    ppermute x1, waiting for transfers between devices, on_device(): lax.ppermute(packet, X_AXES, across)  8.03 us
    ppermute x2, waiting for transfers between devices, on_device(): lax.ppermute(a, X_AXES, inverse(there))  7.18 us
    ppermute x3, starting transfers between devices, on_device(): lax.ppermute(out, 'y', [(i, (i + d) % 4) for i in range(4)]).astype(F32)  6.77 us
    all_to_all x1, starting transfers between devices, on_device(): slabs = lax.all_to_all(slabs, DP_AXES, 0, 0, tiled=True).astype(F32)  6.41 us
  transfers between devices with their start and end apart: 20, of which 9 were waited for; matrix products, arithmetic and copies ran while one was open for 8% of the time, Pallas kernels for 18%

profile of v2, /device:TPU:1, one launch (start us, length us, event | category | flops | bytes accessed | tf_op | source)
XLA Modules:
  0.0 160.6 jit_solution(16505403681833071672)
XLA Ops:
  7.2 0.8 convert_bitcast_fusion
  7.9 2.1 %collective-permute-start = (bf16[1,256]{1,0:T(2,128)(2,1)S(1)}, bf16[1,256]{1,0:T(2,128)(2,1)S(1)}, u32[]{:S(2)}, u32[]{:S(2)}) collective-permute-start(bf16[1,256]{1,0:T(2,128)(2,1)S(1)} %pad.4), channel_id=1, source_target_pairs={{0,8},{8,0},{1,9},{9,1},{2,10},{10,2},{3,11},{11,3},{4,12},{12,4},... | collective-permute-start | bytes 1544 | tf_op jit(solution)/shard_map/ppermute | solution.py:323
  10.1 0.6 pad_add_fusion.idx
  10.7 0.3 collective-permute-done
  11.0 0.6 broadcast_in_dim.11.ids
  11.7 3.1 %weight.1 = (bf16[512,512]{1,0:T(8,128)(2,1)}, bf16[8,80,512]{2,1,0:T(8,128)(2,1)}) custom-call(s32[4]{0:T(128)} %pad_add_fusion.idx, bf16[1024,512]{1,0:T(8,128)(2,1)} %levels.1, bf16[16,512]{1,0:T(8,128)(2,1)} %scales.1, f32[1,512]{1,0:T(1,128)} %second.1, bf16[64,1024]{1,0:T(8,128)(2,1)} %bitcast.47, bf16[64,512]{1,0:T(8,128)(2,1)} %up.4, ...), custom_call_target="tpu_custom_call" | custom-call | flops 1 | bytes 1 | tf_op jit(solution)/shard_map/weight/pallas_call | solution.py:62
  14.8 8.4 %all-to-all-start = ((bf16[8,80,512]{2,1,0:T(8,128)(2,1)}), bf16[8,80,512]{2,1,0:T(8,128)(2,1)S(1)}, u32[]{:S(2)}, u32[]{:S(2)}) async-start(bf16[8,80,512]{2,1,0:T(8,128)(2,1)} %get-tuple-element.17), calls=%async_computation | async-start | bytes 1310720 | tf_op jit(solution)/shard_map/all_to_all | solution.py:328
  23.2 0.0 all-gather.2.cloned.1.call-start
  23.3 0.8 copy.17.own
  24.0 0.6 maximum_bitcast_fusion.freqs
  24.7 0.0 all-gather.2.cloned.1.call-update
  24.7 17.1 %all-to-all-done.everyone = bf16[8,80,512]{2,1,0:T(8,128)(2,1)S(1)} async-done(((bf16[8,80,512]{2,1,0:T(8,128)(2,1)}), bf16[8,80,512]{2,1,0:T(8,128)(2,1)S(1)}, u32[]{:S(2)}, u32[]{:S(2)}) %all-to-all-start) | async-done | bytes 655392 | tf_op jit(solution)/shard_map/all_to_all | solution.py:328
  41.8 0.8 copy-done.8
  42.6 3.4 %grads.1 = (bf16[672,512]{1,0:T(8,128)(2,1)}, bf16[64,160]{1,0:T(8,128)(2,1)}) custom-call(s32[4]{0:T(128)} %pad_add_fusion.idx, bf16[8,80,512]{2,1,0:T(8,128)(2,1)} %copy-done.8, f32[160,1]{1,0:T(8,128)} %copy.17.own, bf16[160,512]{1,0:T(8,128)(2,1)} %rotated.1, f32[1,128]{1,0:T(1,128)} %maximum_bitcast_fusion.freqs, bf16[64,512]{1,0:T(8,128)(2,1)} %up.4), custom_call_target="tpu_custom_call" | custom-call | flops 1 | bytes 1 | tf_op jit(solution)/shard_map/grads/pallas_call | solution.py:110
  46.1 5.0 %down.1 = (f32[64,8192]{1,0:T(8,128)}, bf16[64,8192]{1,0:T(8,128)(2,1)}) custom-call(s32[4]{0:T(128)} %pad_add_fusion.idx, bf16[64,160]{1,0:T(8,128)(2,1)} %get-tuple-element.28.low, bf16[160,16384]{1,0:T(8,128)(2,1)} %tokens.3), custom_call_target="tpu_custom_call" | custom-call | flops 1 | bytes 1 | tf_op jit(solution)/shard_map/down/pallas_call | solution.py:163
  51.1 2.3 %fusion.7 = (bf16[32,8192]{1,0:T(8,128)(2,1)}, bf16[32,8192]{1,0:T(8,128)(2,1)}) fusion(bf16[64,8192]{1,0:T(8,128)(2,1)} %get-tuple-element.30), kind=kLoop, calls=%fused_computation.20 | loop fusion | bytes 2097152 | tf_op jit(solution)/shard_map/split | solution.py:345
  53.4 2.7 %collective-permute-start.10 = (bf16[32,8192]{1,0:T(8,128)(2,1)}, bf16[32,8192]{1,0:T(8,128)(2,1)S(1)}, u32[]{:S(2)}, u32[]{:S(2)}) collective-permute-start(bf16[32,8192]{1,0:T(8,128)(2,1)} %get-tuple-element.34), channel_id=1, source_target_pairs={{0,16},{16,0},{1,17},{17,1},{2,18},{18,2},{3,19},{19,3},{4,20},{20... | collective-permute-start | bytes 1572872 | tf_op jit(solution)/shard_map/ppermute | solution.py:345
  56.1 1.6 collective-permute-start.3
  57.7 1.5 collective-permute-start.2
  59.1 0.0 collective-permute-start.1
  59.1 0.0 collective-permute-done.10
  59.1 1.9 %convert_add_fusion = f32[64,8192]{1,0:T(8,128)S(1)} fusion(f32[64,8192]{1,0:T(8,128)} %get-tuple-element.29, bf16[32,8192]{1,0:T(8,128)(2,1)} %collective-permute-done.11, bf16[32,8192]{1,0:T(8,128)(2,1)S(1)} %collective-permute-done.10), kind=kLoop, calls=%fused_computation | loop fusion | flops 2621440 | bytes 5242880 | tf_op jit(solution)/shard_map/add | solution.py:346
  61.0 0.0 copy-start.7
  61.0 0.1 fusion.4
  61.1 1.4 collective-permute-start.12
  62.5 2.6 %collective-permute-start.14 = (bf16[16,8192]{1,0:T(8,128)(2,1)S(1)}, bf16[16,8192]{1,0:T(8,128)(2,1)}, u32[]{:S(2)}, u32[]{:S(2)}) collective-permute-start(bf16[16,8192]{1,0:T(8,128)(2,1)S(1)} %get-tuple-element.32), channel_id=1, source_target_pairs={{0,64},{32,96},{64,0},{96,32},{1,65},{33,97},{65,1},{97,33},{2,66}... | collective-permute-start | bytes 786440 | tf_op jit(solution)/shard_map/ppermute | solution.py:351
  65.1 8.0 %collective-permute-done.3.across.p3 = bf16[672,512]{1,0:T(8,128)(2,1)S(1)} collective-permute-done((bf16[672,512]{1,0:T(8,128)(2,1)S(1)}, bf16[672,512]{1,0:T(8,128)(2,1)S(1)}, u32[]{:S(2)}, u32[]{:S(2)}) %collective-permute-start.3) | collective-permute-done | bytes 688160 | tf_op jit(solution)/shard_map/ppermute | solution.py:341
  73.2 2.8 %collective-permute-start.13 = (bf16[16,8192]{1,0:T(8,128)(2,1)S(1)}, bf16[16,8192]{1,0:T(8,128)(2,1)}, u32[]{:S(2)}, u32[]{:S(2)}) collective-permute-start(bf16[16,8192]{1,0:T(8,128)(2,1)S(1)} %get-tuple-element.33), channel_id=1, source_target_pairs={{0,96},{32,0},{64,32},{96,64},{1,97},{33,1},{65,33},{97,65},{2,98}... | collective-permute-start | bytes 786440 | tf_op jit(solution)/shard_map/ppermute | solution.py:351
  75.9 0.0 collective-permute-done.2.there.p2
  75.9 0.0 collective-permute-done.1.core.p1
  75.9 0.8 copy-done.5
  76.8 0.9 copy-done.6
  77.6 6.1 %up.5 = f32[64,512]{1,0:T(8,128)} custom-call(s32[4]{0:T(128)} %pad_add_fusion.idx, bf16[160,16384]{1,0:T(8,128)(2,1)} %tokens.3, bf16[672,512]{1,0:T(8,128)(2,1)} %get-tuple-element.18.own.p0, bf16[672,512]{1,0:T(8,128)(2,1)} %copy-done.6, bf16[672,512]{1,0:T(8,128)(2,1)} %copy-done.5, bf16[672,512]{1,0:T(8,128)(2,1)} %copy-done.4), custom_call_target="tpu_custom_call" | custom-call | flops 1 | bytes 1 | tf_op jit(solution)/shard_map/up/pallas_call | solution.py:217
  83.7 5.1 %all-to-all-start.1 = ((f32[8,8,512]{2,1,0:T(8,128)}), f32[8,8,512]{2,1,0:T(8,128)S(1)}, u32[]{:S(2)}, u32[]{:S(2)}) async-start(f32[8,8,512]{2,1,0:T(8,128)} %bitcast.45), calls=%async_computation.1 | async-start | bytes 262144 | tf_op jit(solution)/shard_map/all_to_all | solution.py:354
  88.8 0.0 collective-permute-done.12
  88.8 0.0 collective-permute-done.14
  88.8 1.4 fusion.2
  90.2 0.1 copy.20
  90.3 3.8 %all-to-all-done.1 = f32[8,8,512]{2,1,0:T(8,128)S(1)} async-done(((f32[8,8,512]{2,1,0:T(8,128)}), f32[8,8,512]{2,1,0:T(8,128)S(1)}, u32[]{:S(2)}, u32[]{:S(2)}) %all-to-all-start.1) | async-done | bytes 131104 | tf_op jit(solution)/shard_map/all_to_all | solution.py:354
  94.2 1.0 copy.18
  95.2 3.6 %all-to-all-start.2 = ((bf16[16,24,512]{2,1,0:T(8,128)(2,1)}), bf16[16,24,512]{2,1,0:T(8,128)(2,1)S(1)}, u32[]{:S(2)}, u32[]{:S(2)}) async-start(bf16[16,24,512]{2,1,0:T(8,128)(2,1)} %copy.18), calls=%async_computation.2 | async-start | bytes 786432 | tf_op jit(solution)/shard_map/all_to_all | solution.py:359
  98.7 0.0 all-gather.2.cloned.1.call-done.weight
  98.7 5.6 %blocks.3 = (bf16[160,2048]{1,0:T(8,128)(2,1)}, bf16[160,2048]{1,0:T(8,128)(2,1)}, bf16[160,2048]{1,0:T(8,128)(2,1)}, bf16[160,2048]{1,0:T(8,128)(2,1)}) custom-call(bf16[672,512]{1,0:T(8,128)(2,1)} %get-tuple-element.18.own.p0, bf16[672,512]{1,0:T(8,128)(2,1)} %copy-done.6, bf16[672,512]{1,0:T(8,128)(2,1)} %copy-done.5, bf16[672,512]{1,0:T(8,128)(2,1)} %copy-done.4, ...), custom_call_target="tpu_custom_call" | custom-call | flops 1 | bytes 1 | tf_op jit(solution)/shard_map/blocks/pallas_call | solution.py:248
  104.3 1.0 collective-permute-start.7
  105.3 4.4 %all-to-all-done.2 = bf16[16,24,512]{2,1,0:T(8,128)(2,1)S(1)} async-done(((bf16[16,24,512]{2,1,0:T(8,128)(2,1)}), bf16[16,24,512]{2,1,0:T(8,128)(2,1)S(1)}, u32[]{:S(2)}, u32[]{:S(2)}) %all-to-all-start.2) | async-done | bytes 393248 | tf_op jit(solution)/shard_map/all_to_all | solution.py:359
  109.8 0.1 reduce_sum.22
  109.8 0.8 broadcast_in_dim.26
  110.6 6.4 %all-to-all-start.3 = ((bf16[16,24,512]{2,1,0:T(8,128)(2,1)}), bf16[16,24,512]{2,1,0:T(8,128)(2,1)}, u32[]{:S(2)}, u32[]{:S(2)}) async-start(bf16[16,24,512]{2,1,0:T(8,128)(2,1)} %broadcast_in_dim.26), calls=%async_computation.3 | async-start | bytes 786432 | tf_op jit(solution)/shard_map/all_to_all | solution.py:362
  117.0 0.8 collective-permute-start.8
  117.8 1.2 collective-permute-start.9
  119.0 5.6 %blocks.2 = (bf16[160,2048]{1,0:T(8,128)(2,1)}, bf16[160,2048]{1,0:T(8,128)(2,1)}, bf16[160,2048]{1,0:T(8,128)(2,1)}, bf16[160,2048]{1,0:T(8,128)(2,1)}) custom-call(bf16[672,512]{1,0:T(8,128)(2,1)} %get-tuple-element.18.own.p0, bf16[672,512]{1,0:T(8,128)(2,1)} %copy-done.6, bf16[672,512]{1,0:T(8,128)(2,1)} %copy-done.5, bf16[672,512]{1,0:T(8,128)(2,1)} %copy-done.4, ...), custom_call_target="tpu_custom_call" | custom-call | flops 1 | bytes 1 | tf_op jit(solution)/shard_map/blocks/pallas_call | solution.py:248
  124.6 1.9 %collective-permute-start.4 = (bf16[160,2048]{1,0:T(8,128)(2,1)}, bf16[160,2048]{1,0:T(8,128)(2,1)S(1)}, u32[]{:S(2)}, u32[]{:S(2)}) collective-permute-start(bf16[160,2048]{1,0:T(8,128)(2,1)} %get-tuple-element.21), channel_id=1, source_target_pairs={{0,16},{16,0},{1,17},{17,1},{2,18},{18,2},{3,19},{19,3},{4,20},{20... | collective-permute-start | bytes 1966088 | tf_op jit(solution)/shard_map/ppermute | solution.py:374
  126.5 1.7 %collective-permute-start.6 = (bf16[160,2048]{1,0:T(8,128)(2,1)}, bf16[160,2048]{1,0:T(8,128)(2,1)S(1)}, u32[]{:S(2)}, u32[]{:S(2)}) collective-permute-start(bf16[160,2048]{1,0:T(8,128)(2,1)} %get-tuple-element.23), channel_id=1, source_target_pairs={{152,0},{8,16},{16,8},{128,24},{24,128},{136,144},{144,136},{0,152... | collective-permute-start | bytes 1966088 | tf_op jit(solution)/shard_map/ppermute | solution.py:376
  128.2 1.1 convert_element_type.56
  129.3 0.1 fusion.3
  129.4 0.7 slice.21
  130.1 0.2 copy.19
  130.3 0.8 copy.21
  131.0 1.4 collective-permute-done.8.there
  132.5 5.2 %collective-permute-done.9.across = bf16[160,2048]{1,0:T(8,128)(2,1)} collective-permute-done((bf16[160,2048]{1,0:T(8,128)(2,1)}, bf16[160,2048]{1,0:T(8,128)(2,1)}, u32[]{:S(2)}, u32[]{:S(2)}) %collective-permute-start.9) | collective-permute-done | bytes 655392 | tf_op jit(solution)/shard_map/ppermute | solution.py:376
  137.6 3.0 %assemble.2.rest_0_ = bf16[160,16384]{1,0:T(8,128)(2,1)} custom-call(s32[4]{0:T(128)S(1)} %copy-done.2, bf16[160,2048]{1,0:T(8,128)(2,1)S(1)} %copy-done.1, bf16[160,2048]{1,0:T(8,128)(2,1)S(1)} %collective-permute-done.7.core, bf16[160,2048]{1,0:T(8,128)(2,1)} %collective-permute-done.8.there, bf16[160,2048]{1,0:T(8,128)(2,1)} %collective-permute-done.9.across), custom_call_target="tpu_custom_call" | custom-call | flops 1 | bytes 1 | tf_op jit(solution)/shard_map/assemble/pallas_call | solution.py:284
  140.6 5.8 %collective-permute-done.5.there = bf16[160,2048]{1,0:T(8,128)(2,1)S(1)} collective-permute-done((bf16[160,2048]{1,0:T(8,128)(2,1)}, bf16[160,2048]{1,0:T(8,128)(2,1)S(1)}, u32[]{:S(2)}, u32[]{:S(2)}) %collective-permute-start.5) | collective-permute-done | bytes 655392 | tf_op jit(solution)/shard_map/ppermute | solution.py:375
  146.4 5.2 %collective-permute-done.6.across = bf16[160,2048]{1,0:T(8,128)(2,1)S(1)} collective-permute-done((bf16[160,2048]{1,0:T(8,128)(2,1)}, bf16[160,2048]{1,0:T(8,128)(2,1)S(1)}, u32[]{:S(2)}, u32[]{:S(2)}) %collective-permute-start.6) | collective-permute-done | bytes 655392 | tf_op jit(solution)/shard_map/ppermute | solution.py:376
  151.6 2.2 %assemble.3 = bf16[160,16384]{1,0:T(8,128)(2,1)} custom-call(s32[4]{0:T(128)S(1)} %copy-done.2, bf16[160,2048]{1,0:T(8,128)(2,1)S(1)} %copy-done, bf16[160,2048]{1,0:T(8,128)(2,1)S(1)} %collective-permute-done.4.core, bf16[160,2048]{1,0:T(8,128)(2,1)S(1)} %collective-permute-done.5.there, ...), custom_call_target="tpu_custom_call", output_to_operand_aliasing={{}: (5, {})} | custom-call | flops 1 | bytes 1 | tf_op jit(solution)/shard_map/assemble/pallas_call | solution.py:284
  (28 shorter events, 0.2 us)
Async XLA Ops:
  7.9 3.1 %collective-permute-start = (bf16[1,256]{1,0:T(2,128)(2,1)S(1)}, bf16[1,256]{1,0:T(2,128)(2,1)S(1)}, u32[]{:S(2)}, u32[]{:S(2)}) collective-permute-start(bf16[1,256]{1,0:T(2,128)(2,1)S(1)} %pad.4), channel_id=1, source_target_pairs={{0,8},{8,0},{1,9},{9,1},{2,10},{10,2},{3,11},{11,3},{4,12},{12,4},... | collective-permute-start | bytes 1544 | tf_op jit(solution)/shard_map/ppermute | solution.py:323
  14.8 27.0 %all-to-all-start = ((bf16[8,80,512]{2,1,0:T(8,128)(2,1)}), bf16[8,80,512]{2,1,0:T(8,128)(2,1)S(1)}, u32[]{:S(2)}, u32[]{:S(2)}) async-start(bf16[8,80,512]{2,1,0:T(8,128)(2,1)} %get-tuple-element.17), calls=%async_computation | async-start | bytes 1310720 | tf_op jit(solution)/shard_map/all_to_all | solution.py:328
  23.2 75.5 %all-gather.2.cloned.1.call-start = ((), (), s32[]{:S(2)}) async-start(), calls=%async_computation.4 | async-start | bytes 4718592 | tf_op jit(solution)/shard_map/all_gather | solution.py:327
  41.8 0.8 copy-start.8
  51.1 5.0 %copy-start.3 = (bf16[672,512]{1,0:T(8,128)(2,1)S(1)}, bf16[672,512]{1,0:T(8,128)(2,1)}, u32[]{:S(2)}) copy-start(bf16[672,512]{1,0:T(8,128)(2,1)} %get-tuple-element.18.own.p0) | copy-start | bytes 2064388
  53.4 5.7 %collective-permute-start.10 = (bf16[32,8192]{1,0:T(8,128)(2,1)}, bf16[32,8192]{1,0:T(8,128)(2,1)S(1)}, u32[]{:S(2)}, u32[]{:S(2)}) collective-permute-start(bf16[32,8192]{1,0:T(8,128)(2,1)} %get-tuple-element.34), channel_id=1, source_target_pairs={{0,16},{16,0},{1,17},{17,1},{2,18},{18,2},{3,19},{19,3},{4,20},{20... | collective-permute-start | bytes 1572872 | tf_op jit(solution)/shard_map/ppermute | solution.py:345
  56.1 3.1 %collective-permute-start.11 = (bf16[32,8192]{1,0:T(8,128)(2,1)}, bf16[32,8192]{1,0:T(8,128)(2,1)}, u32[]{:S(2)}, u32[]{:S(2)}) collective-permute-start(bf16[32,8192]{1,0:T(8,128)(2,1)} %get-tuple-element.35), channel_id=1, source_target_pairs={{0,16},{16,0},{1,17},{17,1},{2,18},{18,2},{3,19},{19,3},{4,20},{20... | collective-permute-start | bytes 1572872 | tf_op jit(solution)/shard_map/ppermute | solution.py:345
  56.1 17.1 %collective-permute-start.3 = (bf16[672,512]{1,0:T(8,128)(2,1)S(1)}, bf16[672,512]{1,0:T(8,128)(2,1)S(1)}, u32[]{:S(2)}, u32[]{:S(2)}) collective-permute-start(bf16[672,512]{1,0:T(8,128)(2,1)S(1)} %copy-done.3), channel_id=1, source_target_pairs={{0,152},{16,8},{8,16},{24,128},{128,24},{144,136},{136,144},{152,0... | collective-permute-start | bytes 2064392 | tf_op jit(solution)/shard_map/ppermute | solution.py:341
  57.7 18.3 %collective-permute-start.2 = (bf16[672,512]{1,0:T(8,128)(2,1)S(1)}, bf16[672,512]{1,0:T(8,128)(2,1)S(1)}, u32[]{:S(2)}, u32[]{:S(2)}) collective-permute-start(bf16[672,512]{1,0:T(8,128)(2,1)S(1)} %copy-done.3), channel_id=1, source_target_pairs={{0,8},{16,152},{8,128},{24,16},{128,136},{144,24},{136,0},{152,144... | collective-permute-start | bytes 2064392 | tf_op jit(solution)/shard_map/ppermute | solution.py:340
  59.1 16.8 %collective-permute-start.1 = (bf16[672,512]{1,0:T(8,128)(2,1)S(1)}, bf16[672,512]{1,0:T(8,128)(2,1)S(1)}, u32[]{:S(2)}, u32[]{:S(2)}) collective-permute-start(bf16[672,512]{1,0:T(8,128)(2,1)S(1)} %copy-done.3), channel_id=1, source_target_pairs={{0,16},{16,0},{1,17},{17,1},{2,18},{18,2},{3,19},{19,3},{4,20},{20... | collective-permute-start | bytes 2064392 | tf_op jit(solution)/shard_map/ppermute | solution.py:339
  61.0 12.2 %copy-start.7 = (f32[64,8192]{1,0:T(8,128)}, f32[64,8192]{1,0:T(8,128)S(1)}, u32[]{:S(2)}) copy-start(f32[64,8192]{1,0:T(8,128)S(1)} %convert_add_fusion) | copy-start | bytes 6291460
  61.1 27.7 %collective-permute-start.12 = (bf16[16,8192]{1,0:T(8,128)(2,1)S(1)}, bf16[16,8192]{1,0:T(8,128)(2,1)}, u32[]{:S(2)}, u32[]{:S(2)}) collective-permute-start(bf16[16,8192]{1,0:T(8,128)(2,1)S(1)} %get-tuple-element.31), channel_id=1, source_target_pairs={{0,32},{32,64},{64,96},{96,0},{1,33},{33,65},{65,97},{97,1},{2,34}... | collective-permute-start | bytes 786440 | tf_op jit(solution)/shard_map/ppermute | solution.py:351
  62.5 26.3 %collective-permute-start.14 = (bf16[16,8192]{1,0:T(8,128)(2,1)S(1)}, bf16[16,8192]{1,0:T(8,128)(2,1)}, u32[]{:S(2)}, u32[]{:S(2)}) collective-permute-start(bf16[16,8192]{1,0:T(8,128)(2,1)S(1)} %get-tuple-element.32), channel_id=1, source_target_pairs={{0,64},{32,96},{64,0},{96,32},{1,65},{33,97},{65,1},{97,33},{2,66}... | collective-permute-start | bytes 786440 | tf_op jit(solution)/shard_map/ppermute | solution.py:351
  73.2 2.8 %copy-start.4 = (bf16[672,512]{1,0:T(8,128)(2,1)}, bf16[672,512]{1,0:T(8,128)(2,1)S(1)}, u32[]{:S(2)}) copy-start(bf16[672,512]{1,0:T(8,128)(2,1)S(1)} %collective-permute-done.3.across.p3) | copy-start | bytes 2064388
  73.2 15.7 %collective-permute-start.13 = (bf16[16,8192]{1,0:T(8,128)(2,1)S(1)}, bf16[16,8192]{1,0:T(8,128)(2,1)}, u32[]{:S(2)}, u32[]{:S(2)}) collective-permute-start(bf16[16,8192]{1,0:T(8,128)(2,1)S(1)} %get-tuple-element.33), channel_id=1, source_target_pairs={{0,96},{32,0},{64,32},{96,64},{1,97},{33,1},{65,33},{97,65},{2,98}... | collective-permute-start | bytes 786440 | tf_op jit(solution)/shard_map/ppermute | solution.py:351
  75.9 0.8 copy-start.5
  76.8 0.9 copy-start.6
  83.7 10.3 %all-to-all-start.1 = ((f32[8,8,512]{2,1,0:T(8,128)}), f32[8,8,512]{2,1,0:T(8,128)S(1)}, u32[]{:S(2)}, u32[]{:S(2)}) async-start(f32[8,8,512]{2,1,0:T(8,128)} %bitcast.45), calls=%async_computation.1 | async-start | bytes 262144 | tf_op jit(solution)/shard_map/all_to_all | solution.py:354
  95.2 14.6 %all-to-all-start.2 = ((bf16[16,24,512]{2,1,0:T(8,128)(2,1)}), bf16[16,24,512]{2,1,0:T(8,128)(2,1)S(1)}, u32[]{:S(2)}, u32[]{:S(2)}) async-start(bf16[16,24,512]{2,1,0:T(8,128)(2,1)} %copy.18), calls=%async_computation.2 | async-start | bytes 786432 | tf_op jit(solution)/shard_map/all_to_all | solution.py:359
  104.3 22.2 %collective-permute-start.7 = (bf16[160,2048]{1,0:T(8,128)(2,1)}, bf16[160,2048]{1,0:T(8,128)(2,1)S(1)}, u32[]{:S(2)}, u32[]{:S(2)}) collective-permute-start(bf16[160,2048]{1,0:T(8,128)(2,1)} %get-tuple-element.25), channel_id=1, source_target_pairs={{0,16},{16,0},{1,17},{17,1},{2,18},{18,2},{3,19},{19,3},{4,20},{20... | collective-permute-start | bytes 1966088 | tf_op jit(solution)/shard_map/ppermute | solution.py:374
  110.6 17.6 %all-to-all-start.3 = ((bf16[16,24,512]{2,1,0:T(8,128)(2,1)}), bf16[16,24,512]{2,1,0:T(8,128)(2,1)}, u32[]{:S(2)}, u32[]{:S(2)}) async-start(bf16[16,24,512]{2,1,0:T(8,128)(2,1)} %broadcast_in_dim.26), calls=%async_computation.3 | async-start | bytes 786432 | tf_op jit(solution)/shard_map/all_to_all | solution.py:362
  117.0 15.4 %collective-permute-start.8 = (bf16[160,2048]{1,0:T(8,128)(2,1)}, bf16[160,2048]{1,0:T(8,128)(2,1)}, u32[]{:S(2)}, u32[]{:S(2)}) collective-permute-start(bf16[160,2048]{1,0:T(8,128)(2,1)} %get-tuple-element.26), channel_id=1, source_target_pairs={{8,0},{152,16},{128,8},{16,24},{136,128},{24,144},{0,136},{144,152... | collective-permute-start | bytes 1966088 | tf_op jit(solution)/shard_map/ppermute | solution.py:375
  117.8 19.8 %collective-permute-start.9 = (bf16[160,2048]{1,0:T(8,128)(2,1)}, bf16[160,2048]{1,0:T(8,128)(2,1)}, u32[]{:S(2)}, u32[]{:S(2)}) collective-permute-start(bf16[160,2048]{1,0:T(8,128)(2,1)} %get-tuple-element.27), channel_id=1, source_target_pairs={{152,0},{8,16},{16,8},{128,24},{24,128},{136,144},{144,136},{0,152... | collective-permute-start | bytes 1966088 | tf_op jit(solution)/shard_map/ppermute | solution.py:376
  124.6 16.0 %collective-permute-start.4 = (bf16[160,2048]{1,0:T(8,128)(2,1)}, bf16[160,2048]{1,0:T(8,128)(2,1)S(1)}, u32[]{:S(2)}, u32[]{:S(2)}) collective-permute-start(bf16[160,2048]{1,0:T(8,128)(2,1)} %get-tuple-element.21), channel_id=1, source_target_pairs={{0,16},{16,0},{1,17},{17,1},{2,18},{18,2},{3,19},{19,3},{4,20},{20... | collective-permute-start | bytes 1966088 | tf_op jit(solution)/shard_map/ppermute | solution.py:374
  126.5 19.9 %collective-permute-start.5 = (bf16[160,2048]{1,0:T(8,128)(2,1)}, bf16[160,2048]{1,0:T(8,128)(2,1)S(1)}, u32[]{:S(2)}, u32[]{:S(2)}) collective-permute-start(bf16[160,2048]{1,0:T(8,128)(2,1)} %get-tuple-element.22), channel_id=1, source_target_pairs={{8,0},{152,16},{128,8},{16,24},{136,128},{24,144},{0,136},{144,152... | collective-permute-start | bytes 1966088 | tf_op jit(solution)/shard_map/ppermute | solution.py:375
  126.5 11.1 %copy-start.1 = (bf16[160,2048]{1,0:T(8,128)(2,1)S(1)}, bf16[160,2048]{1,0:T(8,128)(2,1)}, u32[]{:S(2)}) copy-start(bf16[160,2048]{1,0:T(8,128)(2,1)} %get-tuple-element.24.own) | copy-start | bytes 1966084
  126.5 11.1 %copy-start.2 = (s32[4]{0:T(128)S(1)}, s32[4]{0:T(128)}, u32[]{:S(2)}) copy-start(s32[4]{0:T(128)} %pad_add_fusion.idx) | copy-start | bytes 52
  126.5 25.1 %collective-permute-start.6 = (bf16[160,2048]{1,0:T(8,128)(2,1)}, bf16[160,2048]{1,0:T(8,128)(2,1)S(1)}, u32[]{:S(2)}, u32[]{:S(2)}) collective-permute-start(bf16[160,2048]{1,0:T(8,128)(2,1)} %get-tuple-element.23), channel_id=1, source_target_pairs={{152,0},{8,16},{16,8},{128,24},{24,128},{136,144},{144,136},{0,152... | collective-permute-start | bytes 1966088 | tf_op jit(solution)/shard_map/ppermute | solution.py:376
  137.6 13.9 %copy-start = (bf16[160,2048]{1,0:T(8,128)(2,1)S(1)}, bf16[160,2048]{1,0:T(8,128)(2,1)}, u32[]{:S(2)}) copy-start(bf16[160,2048]{1,0:T(8,128)(2,1)} %get-tuple-element.20.own) | copy-start | bytes 1966084
Sparse Core Ops, SparseCore 0:
  25.9 57.9 all-gather.1

commit v3 on v2

v3 whole, which is shorter than its diff:
```python
import functools

import jax
import jax.numpy as jnp
from jax import lax
from jax.experimental import pallas as pl
from jax.experimental.pallas import tpu as pltpu
from jax.sharding import Mesh, PartitionSpec as P

HEAD = 128
RANK = 64
BLOCK = 64
WIDTH = 16384
KEYS = 512
ROWS = 160
SHARDS = 16
NZ = 8
HALF = 512
LANES = 128
IDS = 16
ROPE_BASE = 500000.0
SCALE = 16.0 / RANK
TOKENS = 40960

BF = jnp.bfloat16
F32 = jnp.float32

X_AXES = ("xh", "c", "xl")
SHARD_AXES = ("xl", "z")
DP_AXES = ("xh", "y", "c")


BRIEF = pl.CostEstimate(flops=1, bytes_accessed=1, transcendentals=0)


def params(mib):
    return pltpu.CompilerParams(vmem_limit_bytes=mib * 1024 * 1024)


def dot(a, b, ca, cb):
    return lax.dot_general(a, b, (((ca,), (cb,)), ((), ())), preferred_element_type=F32)


def weight_kernel(idx, levels, scales, second, down, up, weight):
    scale = scales[...].astype(F32)
    n = HALF // BLOCK
    scale = jnp.where(idx[0] == 0, scale[:n], scale[n:])
    rows = []
    for j in range(n):
        level = levels[j * BLOCK : (j + 1) * BLOCK, :].astype(F32)
        rows.append((level * scale[j : j + 1]) * second[...])
    base = dot(up[...], down[...], 0, 0) * SCALE
    weight[...] = (jnp.concatenate(rows, axis=0).T + base).astype(BF)


def local_weight(idx, levels, scales, second, down, up):
    full = lambda shape: pl.BlockSpec(shape, lambda i, s: (0,) * len(shape))
    return pl.pallas_call(
        weight_kernel,
        grid_spec=pltpu.PrefetchScalarGridSpec(
            num_scalar_prefetch=1,
            grid=(1,),
            in_specs=[
                pl.BlockSpec((HALF, KEYS), lambda i, s: (s[0], 0)),
                full(scales.shape),
                full((1, KEYS)),
                pl.BlockSpec((RANK, HALF), lambda i, s: (0, s[0])),
                full((RANK, KEYS)),
            ],
            out_specs=full((KEYS, HALF)),
        ),
        out_shape=jax.ShapeDtypeStruct((KEYS, HALF), BF),
        compiler_params=params(56),
        cost_estimate=BRIEF,
        name="weight",
    )(idx, levels, scales, second, down, up)


def packet_kernel(idx, down, ids, after, packet):
    for k in range(SHARDS):
        packet[k, :RANK, :] = down[...]
        packet[k, RANK:, :] = ids[...]


def make_packet(idx, down, ids, after):
    full = lambda shape: pl.BlockSpec(shape, lambda i, s: (0,) * len(shape))
    return pl.pallas_call(
        packet_kernel,
        grid_spec=pltpu.PrefetchScalarGridSpec(
            num_scalar_prefetch=1,
            grid=(1,),
            in_specs=[
                pl.BlockSpec((RANK, LANES), lambda i, s: (0, s[0] * 4 + s[4])),
                full((IDS, LANES)),
                pl.BlockSpec(memory_space=pl.ANY),
            ],
            out_specs=full((SHARDS, RANK + IDS, LANES)),
        ),
        out_shape=jax.ShapeDtypeStruct((SHARDS, RANK + IDS, LANES), BF),
        compiler_params=params(56),
        cost_estimate=BRIEF,
        name="packet",
    )(idx, down, ids, after)


def grads_kernel(idx, everyone, own, rotated, freqs, up, grads, low):
    mine = own[...]
    count = jnp.zeros((ROWS, LANES), F32)
    for k in range(SHARDS):
        for r in range(2):
            row = everyone[k, r : r + 1, :].astype(F32)
            count = count + jnp.where(row < mine, 1.0, 0.0)
    first = jnp.sum(count, axis=1, keepdims=True)
    place = lax.broadcasted_iota(jnp.int32, (ROWS, 1), 0) + idx[3] * ROWS
    position = place.astype(F32) - first
    angle = position * freqs[...]
    cosine = jnp.cos(angle)
    lane = lax.broadcasted_iota(jnp.int32, (ROWS, HEAD), 1)
    sine = jnp.where(lane < HEAD // 2, 1.0, -1.0) * jnp.sin(angle)
    for h in range(KEYS // HEAD):
        cols = slice(h * HEAD, (h + 1) * HEAD)
        g = rotated[:, cols].astype(F32)
        grads[:, cols] = (g * cosine + pltpu.roll(g, HEAD // 2, 1) * sine).astype(BF)
    low[...] = dot(up[...], grads[...], 1, 1).astype(BF)


def make_grads(idx, everyone, own, rotated, freqs, up):
    full = lambda shape: pl.BlockSpec(shape, lambda i, s: (0,) * len(shape))
    return pl.pallas_call(
        grads_kernel,
        grid_spec=pltpu.PrefetchScalarGridSpec(
            num_scalar_prefetch=1,
            grid=(1,),
            in_specs=[
                pl.BlockSpec((SHARDS, IDS, LANES), lambda i, s: (0, RANK // IDS, 0)),
                full((ROWS, 1)),
                full((ROWS, KEYS)),
                full((1, HEAD)),
                full((RANK, KEYS)),
            ],
            out_specs=[full((ROWS, KEYS)), full((RANK, ROWS))],
        ),
        out_shape=[jax.ShapeDtypeStruct((ROWS, KEYS), BF), jax.ShapeDtypeStruct((RANK, ROWS), BF)],
        compiler_params=params(56),
        cost_estimate=BRIEF,
        name="grads",
    )(idx, everyone, own, rotated, freqs, up)


CHUNKS = 8
WIDE = WIDTH // CHUNKS
STEP = WIDE // (2 * HALF)


def down_kernel(idx, low, tokens, *refs):
    keep, send, (held, keep_held, send_held, sems) = refs[:4], refs[4:8], refs[8:]
    c, y = idx[0], idx[4]
    loads = [
        pltpu.make_async_copy(tokens.at[:, pl.ds(i * WIDE, WIDE)], held.at[i], sems.at[i]) for i in range(CHUNKS)
    ]
    for load in loads:
        load.start()
    stores = []
    for i in range(CHUNKS):
        loads[i].wait()
        for k in range(STEP):
            at = (i * STEP + k) * HALF
            mine = pl.multiple_of(k * 2 * HALF + c * HALF, HALF)
            other = pl.multiple_of(k * 2 * HALF + (1 - c) * HALF, HALF)
            send_held[:, at : at + HALF] = dot(low[...], held[i, :, pl.ds(other, HALF)], 1, 0).astype(BF)
            keep_held[:, at : at + HALF] = dot(low[...], held[i, :, pl.ds(mine, HALF)], 1, 0)
        if i % 4 == 3:
            cols = pl.ds((i - 3) * STEP * HALF, 4 * STEP * HALF)
            for d in range(4):
                rows = pl.ds(pl.multiple_of(lax.rem(y + d, 4) * 16, 16), 16)
                for source, target in ((send_held, send[d]), (keep_held, keep[d])):
                    sem = sems.at[CHUNKS + len(stores)]
                    stores.append(pltpu.make_async_copy(source.at[rows, cols], target.at[:, cols], sem))
                    stores[-1].start()
    for store in stores:
        store.wait()


def down_part(idx, low, tokens):
    anywhere = pl.BlockSpec(memory_space=pl.ANY)
    return pl.pallas_call(
        down_kernel,
        in_specs=[pl.BlockSpec(memory_space=pltpu.SMEM), pl.BlockSpec(memory_space=pltpu.VMEM), anywhere],
        out_specs=[anywhere] * 8,
        out_shape=[jax.ShapeDtypeStruct((RANK // 4, WIDTH // 2), dtype) for dtype in [F32] * 4 + [BF] * 4],
        scratch_shapes=[
            pltpu.VMEM((CHUNKS, ROWS, WIDE), BF),
            pltpu.VMEM((RANK, WIDTH // 2), F32),
            pltpu.VMEM((RANK, WIDTH // 2), BF),
            pltpu.SemaphoreType.DMA((CHUNKS + 16,)),
        ],
        compiler_params=params(56),
        cost_estimate=BRIEF,
        name="down",
    )(idx, low, tokens)


def up_kernel(idx, tokens, *refs):
    given, (grads, _, out, held, lows, sems) = refs[:2], refs[2:]
    c = idx[0]
    loads = [
        pltpu.make_async_copy(tokens.at[:, pl.ds(i * WIDE, WIDE)], held.at[i], sems.at[i]) for i in range(CHUNKS)
    ]
    pieces = [pltpu.make_async_copy(p, lows.at[k], sems.at[CHUNKS + k]) for k, p in enumerate(given)]
    for copy in pieces + loads:
        copy.start()
    for copy in pieces:
        copy.wait()
    total = jnp.zeros((ROWS, RANK), F32)
    for i in range(CHUNKS):
        loads[i].wait()
        for k in range(STEP):
            for p in range(2):
                h = c if p == 0 else 1 - c
                at = pl.multiple_of(k * 2 * HALF + h * HALF, HALF)
                rows = jnp.concatenate([lows[p, q, i * STEP + k] for q in range(4)], axis=1)
                total = total + dot(held[i, :, pl.ds(at, HALF)], rows, 1, 1)
    out[...] = dot(total.astype(BF), grads[...], 0, 0)


def up_part(idx, tokens, lows, grads, after):
    anywhere = pl.BlockSpec(memory_space=pl.ANY)
    return pl.pallas_call(
        up_kernel,
        in_specs=[pl.BlockSpec(memory_space=pltpu.SMEM)]
        + [anywhere] * 3
        + [pl.BlockSpec(memory_space=pltpu.VMEM)]
        + [anywhere],
        out_specs=pl.BlockSpec(memory_space=pltpu.VMEM),
        out_shape=jax.ShapeDtypeStruct((RANK, KEYS), F32),
        scratch_shapes=[
            pltpu.VMEM((CHUNKS, ROWS, WIDE), BF),
            pltpu.VMEM((2, 4, SHARDS, RANK, LANES), BF),
            pltpu.SemaphoreType.DMA((CHUNKS + 2,)),
        ],
        compiler_params=params(56),
        cost_estimate=BRIEF,
        name="up",
    )(idx, tokens, *lows, grads, after)


def block_kernel(own, core, there, across, weight, o0, o1, o2, o3, rows, held, made, sems):
    loads = [
        pltpu.make_async_copy(weight.at[pl.ds(i * KEYS, KEYS), :], held.at[i], sems.at[4 * NZ + i]) for i in range(NZ)
    ]
    for load in loads:
        load.start()
    for k, source in enumerate((own, core, there, across)):
        rows[k * ROWS : (k + 1) * ROWS, :] = source[...]
    stores = []
    for i in range(NZ):
        loads[i].wait()
        made[i] = dot(rows[...], held[i], 1, 0).astype(BF)
        for k, out in enumerate((o0, o1, o2, o3)):
            stores.append(
                pltpu.make_async_copy(
                    made.at[i, pl.ds(k * ROWS, ROWS), :],
                    out.at[:, pl.ds(i * HALF, HALF)],
                    sems.at[4 * i + k],
                )
            )
            stores[-1].start()
    for store in stores:
        store.wait()


def blocks(sources, weight):
    anywhere = pl.BlockSpec(memory_space=pl.ANY)
    return pl.pallas_call(
        block_kernel,
        in_specs=[pl.BlockSpec(memory_space=pltpu.VMEM)] * 4 + [anywhere],
        out_specs=[anywhere] * 4,
        out_shape=[jax.ShapeDtypeStruct((ROWS, NZ * HALF), BF)] * 4,
        scratch_shapes=[
            pltpu.VMEM((4 * ROWS, KEYS), BF),
            pltpu.VMEM((NZ, KEYS, HALF), BF),
            pltpu.VMEM((NZ, 4 * ROWS, HALF), BF),
            pltpu.SemaphoreType.DMA((5 * NZ,)),
        ],
        compiler_params=params(56),
        cost_estimate=BRIEF,
        name="blocks",
    )(*sources, weight)


def assemble_kernel(start, count, idx, own, core, there, across, *rest):
    out, sems = rest[-2:]
    copies = []
    for k, piece in enumerate((own, core, there, across)):
        x = idx[2] if k < 2 else 1 - idx[2]
        h = idx[0] if k % 2 == 0 else 1 - idx[0]
        for j in range(count):
            col = pl.multiple_of(((x * NZ + start + j) * 2 + h) * HALF, HALF)
            copies.append(
                pltpu.make_async_copy(
                    piece.at[:, pl.ds(j * HALF, HALF)],
                    out.at[:, pl.ds(col, HALF)],
                    sems.at[len(copies)],
                )
            )
    for copy in copies:
        copy.start()
    for copy in copies:
        copy.wait()


def assemble(idx, pieces, start, count, before):
    anywhere = pl.BlockSpec(memory_space=pl.ANY)
    return pl.pallas_call(
        functools.partial(assemble_kernel, start, count),
        in_specs=[pl.BlockSpec(memory_space=pltpu.SMEM)]
        + [pl.BlockSpec(memory_space=pltpu.VMEM)] * 4
        + [anywhere] * len(before),
        out_specs=anywhere,
        scratch_shapes=[pltpu.SemaphoreType.DMA((4 * count,))],
        out_shape=jax.ShapeDtypeStruct((ROWS, WIDTH), BF),
        input_output_aliases={5: 0} if before else {},
        compiler_params=params(8),
        cost_estimate=BRIEF,
        name="assemble",
    )(idx, *pieces, *before)


def x_permutation(swap):
    at = lambda x, c: ((x // 2) * 2 + c) * 2 + x % 2
    pairs = []
    for x in range(4):
        for c in range(2):
            if (c ^ swap) == 0:
                pairs.append((at(x, c), at((x + 1) % 4, 0)))
            else:
                pairs.append((at(x, c), at((x - 1) % 4, 1)))
    return pairs


def inverse(pairs):
    return [(b, a) for a, b in pairs]


CORE = [(0, 1), (1, 0)]


def on_device(tokens, rotated, documents, levels, scales, second, down, up):
    xh, y, c, xl, z = (lax.axis_index(a) for a in ("xh", "y", "c", "xl", "z"))
    idx = jnp.stack([c, xh, xl, xl * NZ + z, y]).astype(jnp.int32)

    weight = local_weight(idx, levels, scales, second, down.T, up)

    ids = jnp.pad(documents.astype(BF), ((0, 0), (0, 2 * LANES - ROWS)), constant_values=1000.0)
    ids = jnp.pad(ids.reshape(2, LANES), ((0, IDS - 2), (0, 0)))
    packet = make_packet(idx, down.T, ids, weight)
    weight = lax.all_gather(weight, "z", tiled=True)
    everyone = lax.all_to_all(packet, SHARD_AXES, 0, 0, tiled=True)

    half = HEAD // 2
    freqs = ROPE_BASE ** (-jnp.arange(half, dtype=F32) * 2.0 / HEAD)
    freqs = jnp.concatenate([freqs, freqs])[None, :]
    own = documents.astype(F32).reshape(ROWS, 1)
    grads, low = make_grads(idx, everyone, own, rotated, freqs, up)

    there, across = x_permutation(0), x_permutation(1)
    sources = [
        grads,
        lax.ppermute(grads, "c", CORE),
        lax.ppermute(grads, X_AXES, there),
        lax.ppermute(grads, X_AXES, across),
    ]

    made = down_part(idx, low, tokens)
    keep, send = made[:4], made[4:]
    sent = [lax.ppermute(part, "c", CORE) for part in send]

    lows = jnp.broadcast_to(everyone[None, :, :RANK], (4, SHARDS, RANK, LANES))
    lows = lax.all_to_all(lows, "y", 0, 0, tiled=True)
    lows, sent = lax.optimization_barrier((lows, sent))
    lows = [lows, lax.ppermute(lows, "c", CORE)]

    total = [a + b.astype(F32) for a, b in zip(keep, sent)]
    mine = total[0]
    for d in (1, 3, 2):
        mine = mine + lax.ppermute(total[d].astype(BF), "y", [(i, (i + d) % 4) for i in range(4)]).astype(F32)

    parts = blocks(sources, weight)
    pieces = [
        parts[0],
        lax.ppermute(parts[1], "c", CORE),
        lax.ppermute(parts[2], X_AXES, inverse(there)),
        lax.ppermute(parts[3], X_AXES, inverse(across)),
    ]

    up_total = up_part(idx, tokens, lows, grads, parts[0]).reshape(8, 8, KEYS)
    up_total = jnp.sum(lax.all_to_all(up_total, ("y", "c"), 0, 0, tiled=True), axis=0)

    slabs = mine.reshape(RANK // 4, SHARDS, HALF).transpose(1, 0, 2)
    up_total = jnp.broadcast_to(up_total[None], (SHARDS,) + up_total.shape)
    slabs = jnp.concatenate([slabs, up_total], axis=1).astype(BF)
    slabs, pieces[2] = lax.optimization_barrier((slabs, pieces[2]))
    slabs = lax.all_to_all(slabs, SHARD_AXES, 0, 0, tiled=True)
    slabs = jnp.sum(slabs.astype(F32), axis=0).astype(BF)
    slabs, pieces[3] = lax.optimization_barrier((slabs, pieces[3]))
    slabs = jnp.broadcast_to(slabs[None], (16,) + slabs.shape)
    slabs = lax.all_to_all(slabs, DP_AXES, 0, 0, tiled=True).astype(F32)
    slabs = slabs.reshape(2, 4, 2, RANK // 4 + 8, KEYS)
    factor = SCALE / jnp.sqrt(jnp.float32(TOKENS))
    slabs = factor * (slabs[0] + slabs[1])
    grad_down = slabs[:, :, : RANK // 4].transpose(1, 3, 0, 2).reshape(2 * HALF, RANK)
    grad_up = slabs[:, :, RANK // 4 :].reshape(RANK, KEYS)

    grad_tokens = assemble(idx, pieces, 0, NZ, [])
    return grad_tokens, grad_down, grad_up


def solution(mesh):
    fine = Mesh(mesh.devices.reshape(2, 4, 2, 2, 8), ("xh", "y", "c", "xl", "z"))
    everything = DP_AXES + SHARD_AXES
    in_specs = (
        P(everything, None),
        P(everything, None),
        P(DP_AXES, SHARD_AXES),
        P(SHARD_AXES, None),
        P(SHARD_AXES, None),
        P(),
        P(SHARD_AXES, None),
        P(),
    )
    out_specs = (P(everything, None), P(SHARD_AXES, None), P())
    return jax.shard_map(on_device, mesh=fine, in_specs=in_specs, out_specs=out_specs, check_vma=False)
```

time: 162 us -> 146 us (0.901)
  blocking collectives: 0 us -> 36.5 us
  waiting for transfers between devices: 51.3 us -> 16.2 us
  starting transfers between devices: 44.7 us -> 34.6 us
  local copies, waits for them, and re-layouts: 9.85 us -> 5.73 us
  Pallas kernels: 34 us -> 32 us
    all_to_all x0 -> x2, blocking collectives: none -> 36.5 us  [the longest x1 21.1 us: on_device(): everyone = lax.all_to_all(packet, SHARD_AXES, 0, 0, tiled=True)]
    ppermute x15 -> x14, waiting for transfers between devices: 25.9 us -> 1.3 us  [the longest x1 1.03 us: on_device(): lax.ppermute(grads, 'c', CORE)]
    all_to_all x2 -> x1, waiting for transfers between devices: 21.5 us -> 0.01 us  [on_device(): lows = lax.all_to_all(lows, 'y', 0, 0, tiled=True)]
    all_to_all x2 -> x1, starting transfers between devices: 12 us -> 4.21 us  [on_device(): lows = lax.all_to_all(lows, 'y', 0, 0, tiled=True)]
    all_to_all x1, waiting for transfers between devices: 0.01 us -> 5.54 us  [on_device(): slabs = lax.all_to_all(slabs, DP_AXES, 0, 0, tiled=True).astype(F32)]
    all_gather x1, waiting for transfers between devices: 0.02 us -> 5.24 us  [on_device(): weight = lax.all_gather(weight, 'z', tiled=True)]
    ppermute x15 -> x14, starting transfers between devices: 21.2 us -> 16.2 us  [the longest x4 6.22 us: on_device(): sent = [lax.ppermute(part, 'c', CORE) for part in send]]
    convert_element_type x0 -> x3, other arithmetic: none -> 3.67 us  [on_device(): total[d].astype(BF)]
  transfers between devices with their start and end apart: 20 -> 18, of which waited for: 9 -> 5; matrix products, arithmetic and copies ran while one was open for 8% -> 6% of each run, Pallas kernels for 18% -> 20%
where the time goes in v3:
time: 146 us; the launch traced here: 145 us
  blocking collectives  36.5 us (25%)
  starting transfers between devices  34.6 us (24%)
  Pallas kernels  32 us (22%)
  waiting for transfers between devices  16.2 us (11%)
  between operations  14.3 us (10%)
  local copies, waits for them, and re-layouts  5.73 us (4%)
  other arithmetic  5.63 us (4%)
    all_to_all x1, blocking collectives, on_device(): everyone = lax.all_to_all(packet, SHARD_AXES, 0, 0, tiled=True)  21.1 us
    all_to_all x1, blocking collectives, on_device(): slabs = lax.all_to_all(slabs, SHARD_AXES, 0, 0, tiled=True)  15.4 us
    all_to_all x1, starting transfers between devices, on_device(): slabs = lax.all_to_all(slabs, DP_AXES, 0, 0, tiled=True).astype(F32)  8.07 us
    pallas_call x1, Pallas kernels, blocks(): pl.pallas_call(block_kernel, in_specs=[pl.BlockSpec(memory_space=pltpu.VM...  7.49 us
    pallas_call x1, Pallas kernels, up_part(): pl.pallas_call(up_kernel, in_specs=[pl.BlockSpec(memory_space=pltpu.SMEM)...  6.7 us
    ppermute x4, starting transfers between devices, on_device(): sent = [lax.ppermute(part, 'c', CORE) for part in send]  6.22 us
    all_to_all x1, starting transfers between devices, on_device(): lax.all_to_all(up_total, ('y', 'c'), 0, 0, tiled=True)  6.1 us
    all_to_all x1, waiting for transfers between devices, on_device(): slabs = lax.all_to_all(slabs, DP_AXES, 0, 0, tiled=True).astype(F32)  5.54 us
  transfers between devices with their start and end apart: 18, of which 5 were waited for; matrix products, arithmetic and copies ran while one was open for 6% of the time, Pallas kernels for 20%

profile of v3, /device:TPU:1, one launch (start us, length us, event | category | flops | bytes accessed | tf_op | source)
XLA Modules:
  0.0 144.9 jit_solution(4225622588403984451)
XLA Ops:
  7.2 0.0 all-gather.2.cloned.1.call-start
  7.2 0.6 stack.23.idx
  7.8 3.0 %weight.1.after = bf16[512,512]{1,0:T(8,128)(2,1)} custom-call(s32[5]{0:T(128)} %stack.23.idx, bf16[1024,512]{1,0:T(8,128)(2,1)} %levels.1, bf16[16,512]{1,0:T(8,128)(2,1)} %scales.1, f32[1,512]{1,0:T(1,128)} %second.1, bf16[64,1024]{1,0:T(8,128)(2,1)} %bitcast.34, bf16[64,512]{1,0:T(8,128)(2,1)} %up.4), custom_call_target="tpu_custom_call" | custom-call | flops 1 | bytes 1 | tf_op jit(solution)/shard_map/weight/pallas_call | solution.py:58
  10.8 0.0 all-gather.2.cloned.1.call-update
  10.9 0.6 pad.9.ids
  11.5 2.2 %packet.1 = bf16[16,80,128]{2,1,0:T(8,128)(2,1)} custom-call(s32[5]{0:T(128)} %stack.23.idx, bf16[64,1024]{1,0:T(8,128)(2,1)} %bitcast.35, bf16[16,128]{1,0:T(8,128)(2,1)} %pad.9.ids, bf16[512,512]{1,0:T(8,128)(2,1)} %weight.1.after), custom_call_target="tpu_custom_call" | custom-call | flops 1 | bytes 1 | tf_op jit(solution)/shard_map/packet/pallas_call | solution.py:87
  13.7 21.1 %all_to_all.25.everyone = bf16[16,80,128]{2,1,0:T(8,128)(2,1)S(1)} all-to-all(bf16[16,80,128]{2,1,0:T(8,128)(2,1)} %packet.1), channel_id=1, replica_groups=mesh['xh'=2,'y'=4,'c'=2,'xl'=2,'z'=8] {'xl','z'}, dimensions={0} | all-to-all | bytes 655360 | tf_op jit(solution)/shard_map/all_to_all | solution.py:358
  34.8 1.2 broadcast_in_dim.9
  36.1 4.2 %all-to-all-start.1 = ((bf16[4,16,64,128]{3,2,1,0:T(8,128)(2,1)}), bf16[4,16,64,128]{3,2,1,0:T(8,128)(2,1)S(1)}, u32[]{:S(2)}, u32[]{:S(2)}) async-start(bf16[4,16,64,128]{3,2,1,0:T(8,128)(2,1)} %broadcast_in_dim.9), calls=%async_computation.1 | async-start | bytes 2097152 | tf_op jit(solution)/shard_map/all_to_all | solution.py:379
  40.3 0.8 copy.14.own
  41.0 0.6 maximum_bitcast_fusion.freqs
  41.6 3.2 %grads.1 = (bf16[160,512]{1,0:T(8,128)(2,1)}, bf16[64,160]{1,0:T(8,128)(2,1)}) custom-call(s32[5]{0:T(128)} %stack.23.idx, bf16[16,80,128]{2,1,0:T(8,128)(2,1)} %copy-done.3, f32[160,1]{1,0:T(8,128)} %copy.14.own, bf16[160,512]{1,0:T(8,128)(2,1)} %rotated.1, f32[1,128]{1,0:T(1,128)} %maximum_bitcast_fusion.freqs, bf16[64,512]{1,0:T(8,128)(2,1)} %up.4), custom_call_target="tpu_custom_call" | custom-call | flops 1 | bytes 1 | tf_op jit(solution)/shard_map/grads/pallas_call | solution.py:129
  44.8 5.1 %down.1 = (f32[16,8192]{1,0:T(8,128)}, f32[16,8192]{1,0:T(8,128)}, f32[16,8192]{1,0:T(8,128)}, f32[16,8192]{1,0:T(8,128)}, bf16[16,8192]{1,0:T(8,128)(2,1)}, /*i...) custom-call(s32[5]{0:T(128)} %stack.23.idx, bf16[64,160]{1,0:T(8,128)(2,1)} %get-tuple-element.29.low, ...), custom_call_target="tpu_custom_call" | custom-call | flops 1 | bytes 1 | tf_op jit(solution)/shard_map/down/pallas_call | solution.py:186
  50.0 5.6 %collective-permute-start.4 = (bf16[16,8192]{1,0:T(8,128)(2,1)}, bf16[16,8192]{1,0:T(8,128)(2,1)S(1)}, u32[]{:S(2)}, u32[]{:S(2)}) collective-permute-start(bf16[16,8192]{1,0:T(8,128)(2,1)} %get-tuple-element.31), channel_id=1, source_target_pairs={{0,16},{16,0},{1,17},{17,1},{2,18},{18,2},{3,19},{19,3},{4,20},{20... | collective-permute-start | bytes 786440 | tf_op jit(solution)/shard_map/ppermute | solution.py:376
  55.6 0.1 collective-permute-start.5
  55.7 0.4 collective-permute-start.6
  56.1 0.1 collective-permute-start.7
  56.2 0.6 collective-permute-start.2
  56.7 0.2 collective-permute-done.4
  56.9 2.2 %collective-permute-start.1 = (bf16[160,512]{1,0:T(8,128)(2,1)S(1)}, bf16[160,512]{1,0:T(8,128)(2,1)}, u32[]{:S(2)}, u32[]{:S(2)}) collective-permute-start(bf16[160,512]{1,0:T(8,128)(2,1)S(1)} %copy-done.4), channel_id=1, source_target_pairs={{0,8},{16,152},{8,128},{24,16},{128,136},{144,24},{136,0},{152,144... | collective-permute-start | bytes 491528 | tf_op jit(solution)/shard_map/ppermute | solution.py:370
  59.2 0.0 collective-permute-done.5
  59.2 0.0 collective-permute-done.6
  59.2 0.0 collective-permute-done.7
  59.2 0.0 all-to-all-done.1.refs_0_
  59.2 2.2 %add_convert_fusion.3 = bf16[16,8192]{1,0:T(8,128)(2,1)} fusion(f32[16,8192]{1,0:T(8,128)} %get-tuple-element.36, bf16[16,8192]{1,0:T(8,128)(2,1)S(1)} %collective-permute-done.5), kind=kLoop, calls=%fused_computation.3 | loop fusion | flops 393216 | bytes 1048576 | tf_op jit(solution)/shard_map/convert_element_type | solution.py:386
  61.4 1.8 %collective-permute-start.8 = (bf16[16,8192]{1,0:T(8,128)(2,1)}, bf16[16,8192]{1,0:T(8,128)(2,1)S(1)}, u32[]{:S(2)}, u32[]{:S(2)}) collective-permute-start(bf16[16,8192]{1,0:T(8,128)(2,1)} %add_convert_fusion.3), channel_id=1, source_target_pairs={{0,32},{32,64},{64,96},{96,0},{1,33},{33,65},{65,97},{97,1},{2,34}... | collective-permute-start | bytes 786440 | tf_op jit(solution)/shard_map/ppermute | solution.py:386
  63.1 0.7 add_convert_fusion.2
  63.9 1.2 collective-permute-start.9
  65.1 0.0 collective-permute-start.11
  65.1 0.7 add_convert_fusion.1
  65.8 0.0 collective-permute-done.2.across
  65.8 1.8 %collective-permute-start.10 = (bf16[16,8192]{1,0:T(8,128)(2,1)}, bf16[16,8192]{1,0:T(8,128)(2,1)}, u32[]{:S(2)}, u32[]{:S(2)}) collective-permute-start(bf16[16,8192]{1,0:T(8,128)(2,1)} %add_convert_fusion.1), channel_id=1, source_target_pairs={{0,64},{32,96},{64,0},{96,32},{1,65},{33,97},{65,1},{97,33},{2,66}... | collective-permute-start | bytes 786440 | tf_op jit(solution)/shard_map/ppermute | solution.py:386
  67.6 0.0 collective-permute-done.1.there
  67.6 0.8 collective-permute-start
  68.4 1.0 collective-permute-done.core
  69.4 5.2 %all-gather.2.cloned.1.call-done.weight = bf16[4096,512]{1,0:T(8,128)(2,1)} async-done(((bf16[512,512]{1,0:T(8,128)(2,1)}), bf16[4096,512]{1,0:T(8,128)(2,1)}) %all-gather.2.cloned.1.call-update) | async-done | bytes 4194320 | tf_op jit(solution)/shard_map/all_gather | solution.py:357
  74.7 7.5 %blocks.1 = (bf16[160,4096]{1,0:T(8,128)(2,1)}, bf16[160,4096]{1,0:T(8,128)(2,1)}, bf16[160,4096]{1,0:T(8,128)(2,1)}, bf16[160,4096]{1,0:T(8,128)(2,1)}) custom-call(bf16[160,512]{1,0:T(8,128)(2,1)} %get-tuple-element.26.own.refs_2_, bf16[160,512]{1,0:T(8,128)(2,1)} %copy-done.8, bf16[160,512]{1,0:T(8,128)(2,1)} %collective-permute-done.1.there, ...), custom_call_target="tpu_custom_call" | custom-call | flops 1 | bytes 1 | tf_op jit(solution)/shard_map/blocks/pallas_call | solution.py:274
  82.2 0.5 collective-permute-start.3
  82.7 0.0 collective-permute-done.11.refs_1_
  82.7 1.2 collective-permute-start.12
  83.9 6.7 %up.5 = f32[64,512]{1,0:T(8,128)} custom-call(s32[5]{0:T(128)} %stack.23.idx, bf16[160,16384]{1,0:T(8,128)(2,1)} %tokens.3, bf16[4,16,64,128]{3,2,1,0:T(8,128)(2,1)} %copy-done.2, bf16[4,16,64,128]{3,2,1,0:T(8,128)(2,1)} %collective-permute-done.11.refs_1_, bf16[160,512]{1,0:T(8,128)(2,1)} %get-tuple-element.26.own.refs_2_, ...), custom_call_target="tpu_custom_call" | custom-call | flops 1 | bytes 1 | tf_op jit(solution)/shard_map/up/pallas_call | solution.py:228
  90.6 6.1 %all-to-all-start.2 = ((f32[8,8,512]{2,1,0:T(8,128)}), f32[8,8,512]{2,1,0:T(8,128)S(1)}, u32[]{:S(2)}, u32[]{:S(2)}) async-start(f32[8,8,512]{2,1,0:T(8,128)} %bitcast.33), calls=%async_computation.2 | async-start | bytes 262144 | tf_op jit(solution)/shard_map/all_to_all | solution.py:397
  96.7 0.0 collective-permute-done.8
  96.7 0.0 collective-permute-start.13
  96.7 0.0 collective-permute-done.9
  96.7 0.0 collective-permute-done.10
  96.7 1.1 add_convert_fusion
  97.9 4.1 %all-to-all-done.2 = f32[8,8,512]{2,1,0:T(8,128)S(1)} async-done(((f32[8,8,512]{2,1,0:T(8,128)}), f32[8,8,512]{2,1,0:T(8,128)S(1)}, u32[]{:S(2)}, u32[]{:S(2)}) %all-to-all-start.2) | async-done | bytes 131104 | tf_op jit(solution)/shard_map/all_to_all | solution.py:397
  102.0 0.0 copy-start
  102.0 0.0 copy-start.1
  102.1 0.0 collective-permute-done.12.there
  102.1 15.4 %all_to_all.26 = bf16[16,24,512]{2,1,0:T(8,128)(2,1)S(1)} all-to-all(bf16[16,24,512]{2,1,0:T(8,128)(2,1)S(1)} %pad_maximum_fusion), channel_id=1, replica_groups=mesh['xh'=2,'y'=4,'c'=2,'xl'=2,'z'=8] {'xl','z'}, dimensions={0} | all-to-all | bytes 786432 | tf_op jit(solution)/shard_map/all_to_all | solution.py:403
  117.4 0.1 reduce_sum.22
  117.5 0.0 collective-permute-done.13.across
  117.5 0.8 broadcast_in_dim.11
  118.3 8.1 %all-to-all-start.4 = ((bf16[16,24,512]{2,1,0:T(8,128)(2,1)}), bf16[16,24,512]{2,1,0:T(8,128)(2,1)S(1)}, u32[]{:S(2)}, u32[]{:S(2)}) async-start(bf16[16,24,512]{2,1,0:T(8,128)(2,1)} %broadcast_in_dim.11), calls=%async_computation.4 | async-start | bytes 786432 | tf_op jit(solution)/shard_map/all_to_all | solution.py:407
  126.4 0.0 collective-permute-done.3.core
  126.4 4.3 %assemble.1 = bf16[160,16384]{1,0:T(8,128)(2,1)} custom-call(s32[5]{0:T(128)S(1)} %copy-done.1, bf16[160,4096]{1,0:T(8,128)(2,1)S(1)} %copy-done, bf16[160,4096]{1,0:T(8,128)(2,1)S(1)} %collective-permute-done.3.core, bf16[160,4096]{1,0:T(8,128)(2,1)} %collective-permute-done.12.there, bf16[160,4096]{1,0:T(8,128)(2,1)} %collective-permute-done.13.across), custom_call_target="tpu_custom_call" | custom-call | flops 1 | bytes 1 | tf_op jit(solution)/shard_map/assemble/pallas_call | solution.py:314
  130.7 5.5 %all-to-all-done.4 = bf16[16,24,512]{2,1,0:T(8,128)(2,1)S(1)} async-done(((bf16[16,24,512]{2,1,0:T(8,128)(2,1)}), bf16[16,24,512]{2,1,0:T(8,128)(2,1)S(1)}, u32[]{:S(2)}, u32[]{:S(2)}) %all-to-all-start.4) | async-done | bytes 393248 | tf_op jit(solution)/shard_map/all_to_all | solution.py:407
  136.3 0.1 convert_element_type.58
  136.4 0.1 fusion
  136.4 0.7 slice.26
  137.1 0.2 copy.16
  137.3 0.8 copy.18
  (27 shorter events, 0.2 us)
Async XLA Ops:
  7.2 3.7 %copy-start.9 = (s32[1,160]{1,0:T(1,128)S(1)}, s32[1,160]{1,0:T(1,128)}, u32[]{:S(2)}) copy-start(s32[1,160]{1,0:T(1,128)} %param.10) | copy-start | bytes 1924
  7.2 67.5 %all-gather.2.cloned.1.call-start = ((), (), s32[]{:S(2)}) async-start(), calls=%async_computation.5 | async-start | bytes 4718592 | tf_op jit(solution)/shard_map/all_gather | solution.py:357
  34.8 1.3 copy-start.3
  36.1 23.1 %all-to-all-start.1 = ((bf16[4,16,64,128]{3,2,1,0:T(8,128)(2,1)}), bf16[4,16,64,128]{3,2,1,0:T(8,128)(2,1)S(1)}, u32[]{:S(2)}, u32[]{:S(2)}) async-start(bf16[4,16,64,128]{3,2,1,0:T(8,128)(2,1)} %broadcast_in_dim.9), calls=%async_computation.1 | async-start | bytes 2097152 | tf_op jit(solution)/shard_map/all_to_all | solution.py:379
  44.8 11.4 %copy-start.4 = (bf16[160,512]{1,0:T(8,128)(2,1)S(1)}, bf16[160,512]{1,0:T(8,128)(2,1)}, u32[]{:S(2)}) copy-start(bf16[160,512]{1,0:T(8,128)(2,1)} %get-tuple-element.26.own.refs_2_) | copy-start | bytes 491524
  49.9 13.2 %copy-start.7 = (f32[16,8192]{1,0:T(8,128)S(1)}, f32[16,8192]{1,0:T(8,128)}, u32[]{:S(2)}) copy-start(f32[16,8192]{1,0:T(8,128)} %get-tuple-element.38) | copy-start | bytes 1572868
  49.9 15.1 %copy-start.6 = (f32[16,8192]{1,0:T(8,128)S(1)}, f32[16,8192]{1,0:T(8,128)}, u32[]{:S(2)}) copy-start(f32[16,8192]{1,0:T(8,128)} %get-tuple-element.40) | copy-start | bytes 1572868
  50.0 7.0 %collective-permute-start.4 = (bf16[16,8192]{1,0:T(8,128)(2,1)}, bf16[16,8192]{1,0:T(8,128)(2,1)S(1)}, u32[]{:S(2)}, u32[]{:S(2)}) collective-permute-start(bf16[16,8192]{1,0:T(8,128)(2,1)} %get-tuple-element.31), channel_id=1, source_target_pairs={{0,16},{16,0},{1,17},{17,1},{2,18},{18,2},{3,19},{19,3},{4,20},{20... | collective-permute-start | bytes 786440 | tf_op jit(solution)/shard_map/ppermute | solution.py:376
  55.6 3.6 %collective-permute-start.5 = (bf16[16,8192]{1,0:T(8,128)(2,1)}, bf16[16,8192]{1,0:T(8,128)(2,1)S(1)}, u32[]{:S(2)}, u32[]{:S(2)}) collective-permute-start(bf16[16,8192]{1,0:T(8,128)(2,1)} %get-tuple-element.32), channel_id=1, source_target_pairs={{0,16},{16,0},{1,17},{17,1},{2,18},{18,2},{3,19},{19,3},{4,20},{20... | collective-permute-start | bytes 786440 | tf_op jit(solution)/shard_map/ppermute | solution.py:376
  55.7 3.5 %collective-permute-start.6 = (bf16[16,8192]{1,0:T(8,128)(2,1)}, bf16[16,8192]{1,0:T(8,128)(2,1)S(1)}, u32[]{:S(2)}, u32[]{:S(2)}) collective-permute-start(bf16[16,8192]{1,0:T(8,128)(2,1)} %get-tuple-element.33), channel_id=1, source_target_pairs={{0,16},{16,0},{1,17},{17,1},{2,18},{18,2},{3,19},{19,3},{4,20},{20... | collective-permute-start | bytes 786440 | tf_op jit(solution)/shard_map/ppermute | solution.py:376
  56.1 3.1 %collective-permute-start.7 = (bf16[16,8192]{1,0:T(8,128)(2,1)}, bf16[16,8192]{1,0:T(8,128)(2,1)S(1)}, u32[]{:S(2)}, u32[]{:S(2)}) collective-permute-start(bf16[16,8192]{1,0:T(8,128)(2,1)} %get-tuple-element.34), channel_id=1, source_target_pairs={{0,16},{16,0},{1,17},{17,1},{2,18},{18,2},{3,19},{19,3},{4,20},{20... | collective-permute-start | bytes 786440 | tf_op jit(solution)/shard_map/ppermute | solution.py:376
  56.2 9.7 %collective-permute-start.2 = (bf16[160,512]{1,0:T(8,128)(2,1)S(1)}, bf16[160,512]{1,0:T(8,128)(2,1)}, u32[]{:S(2)}, u32[]{:S(2)}) collective-permute-start(bf16[160,512]{1,0:T(8,128)(2,1)S(1)} %copy-done.4), channel_id=1, source_target_pairs={{0,152},{16,8},{8,16},{24,128},{128,24},{144,136},{136,144},{152,0... | collective-permute-start | bytes 491528 | tf_op jit(solution)/shard_map/ppermute | solution.py:371
  56.9 10.7 %collective-permute-start.1 = (bf16[160,512]{1,0:T(8,128)(2,1)S(1)}, bf16[160,512]{1,0:T(8,128)(2,1)}, u32[]{:S(2)}, u32[]{:S(2)}) collective-permute-start(bf16[160,512]{1,0:T(8,128)(2,1)S(1)} %copy-done.4), channel_id=1, source_target_pairs={{0,8},{16,152},{8,128},{24,16},{128,136},{144,24},{136,0},{152,144... | collective-permute-start | bytes 491528 | tf_op jit(solution)/shard_map/ppermute | solution.py:370
  59.2 6.6 %copy-start.2 = (bf16[4,16,64,128]{3,2,1,0:T(8,128)(2,1)}, bf16[4,16,64,128]{3,2,1,0:T(8,128)(2,1)S(1)}, u32[]{:S(2)}) copy-start(bf16[4,16,64,128]{3,2,1,0:T(8,128)(2,1)S(1)} %all-to-all-done.1.refs_0_) | copy-start | bytes 3145732
  61.4 35.3 %collective-permute-start.8 = (bf16[16,8192]{1,0:T(8,128)(2,1)}, bf16[16,8192]{1,0:T(8,128)(2,1)S(1)}, u32[]{:S(2)}, u32[]{:S(2)}) collective-permute-start(bf16[16,8192]{1,0:T(8,128)(2,1)} %add_convert_fusion.3), channel_id=1, source_target_pairs={{0,32},{32,64},{64,96},{96,0},{1,33},{33,65},{65,97},{97,1},{2,34}... | collective-permute-start | bytes 786440 | tf_op jit(solution)/shard_map/ppermute | solution.py:386
  63.9 32.8 %collective-permute-start.9 = (bf16[16,8192]{1,0:T(8,128)(2,1)}, bf16[16,8192]{1,0:T(8,128)(2,1)S(1)}, u32[]{:S(2)}, u32[]{:S(2)}) collective-permute-start(bf16[16,8192]{1,0:T(8,128)(2,1)} %add_convert_fusion.2), channel_id=1, source_target_pairs={{0,96},{32,0},{64,32},{96,64},{1,97},{33,1},{65,33},{97,65},{2,98}... | collective-permute-start | bytes 786440 | tf_op jit(solution)/shard_map/ppermute | solution.py:386
  65.1 17.6 %collective-permute-start.11 = (bf16[4,16,64,128]{3,2,1,0:T(8,128)(2,1)S(1)}, bf16[4,16,64,128]{3,2,1,0:T(8,128)(2,1)}, u32[]{:S(2)}, u32[]{:S(2)}) collective-permute-start(bf16[4,16,64,128]{3,2,1,0:T(8,128)(2,1)S(1)} %all-to-all-done.1.refs_0_), channel_id=1, source_target_pairs={{0,16},{16,0},{1,17},{17,1},{2,18},{18,2},{3,19},{19,3},{4,20},{20... | collective-permute-start | bytes 3145736 | tf_op jit(solution)/shard_map/ppermute | solution.py:381
  65.8 30.9 %collective-permute-start.10 = (bf16[16,8192]{1,0:T(8,128)(2,1)}, bf16[16,8192]{1,0:T(8,128)(2,1)}, u32[]{:S(2)}, u32[]{:S(2)}) collective-permute-start(bf16[16,8192]{1,0:T(8,128)(2,1)} %add_convert_fusion.1), channel_id=1, source_target_pairs={{0,64},{32,96},{64,0},{96,32},{1,65},{33,97},{65,1},{97,33},{2,66}... | collective-permute-start | bytes 786440 | tf_op jit(solution)/shard_map/ppermute | solution.py:386
  67.6 1.8 %collective-permute-start = (bf16[160,512]{1,0:T(8,128)(2,1)S(1)}, bf16[160,512]{1,0:T(8,128)(2,1)S(1)}, u32[]{:S(2)}, u32[]{:S(2)}) collective-permute-start(bf16[160,512]{1,0:T(8,128)(2,1)S(1)} %copy-done.4), channel_id=1, source_target_pairs={{0,16},{16,0},{1,17},{17,1},{2,18},{18,2},{3,19},{19,3},{4,20},{20... | collective-permute-start | bytes 491528 | tf_op jit(solution)/shard_map/ppermute | solution.py:369
  69.4 5.2 %copy-start.8 = (bf16[160,512]{1,0:T(8,128)(2,1)}, bf16[160,512]{1,0:T(8,128)(2,1)S(1)}, u32[]{:S(2)}) copy-start(bf16[160,512]{1,0:T(8,128)(2,1)S(1)} %collective-permute-done.core) | copy-start | bytes 491524
  82.2 44.2 %collective-permute-start.3 = (bf16[160,4096]{1,0:T(8,128)(2,1)}, bf16[160,4096]{1,0:T(8,128)(2,1)S(1)}, u32[]{:S(2)}, u32[]{:S(2)}) collective-permute-start(bf16[160,4096]{1,0:T(8,128)(2,1)} %get-tuple-element.28), channel_id=1, source_target_pairs={{0,16},{16,0},{1,17},{17,1},{2,18},{18,2},{3,19},{19,3},{4,20},{20... | collective-permute-start | bytes 3932168 | tf_op jit(solution)/shard_map/ppermute | solution.py:391
  82.7 19.4 %collective-permute-start.12 = (bf16[160,4096]{1,0:T(8,128)(2,1)}, bf16[160,4096]{1,0:T(8,128)(2,1)}, u32[]{:S(2)}, u32[]{:S(2)}) collective-permute-start(bf16[160,4096]{1,0:T(8,128)(2,1)} %get-tuple-element.43), channel_id=1, source_target_pairs={{8,0},{152,16},{128,8},{16,24},{136,128},{24,144},{0,136},{144,152... | collective-permute-start | bytes 3932168 | tf_op jit(solution)/shard_map/ppermute | solution.py:392
  83.9 12.9 %copy-start.5 = (f32[16,8192]{1,0:T(8,128)S(1)}, f32[16,8192]{1,0:T(8,128)}, u32[]{:S(2)}) copy-start(f32[16,8192]{1,0:T(8,128)} %get-tuple-element.30) | copy-start | bytes 1572868
  90.6 11.4 %all-to-all-start.2 = ((f32[8,8,512]{2,1,0:T(8,128)}), f32[8,8,512]{2,1,0:T(8,128)S(1)}, u32[]{:S(2)}, u32[]{:S(2)}) async-start(f32[8,8,512]{2,1,0:T(8,128)} %bitcast.33), calls=%async_computation.2 | async-start | bytes 262144 | tf_op jit(solution)/shard_map/all_to_all | solution.py:397
  96.7 20.8 %collective-permute-start.13 = (bf16[160,4096]{1,0:T(8,128)(2,1)}, bf16[160,4096]{1,0:T(8,128)(2,1)}, u32[]{:S(2)}, u32[]{:S(2)}) collective-permute-start(bf16[160,4096]{1,0:T(8,128)(2,1)} %get-tuple-element.46), channel_id=1, source_target_pairs={{152,0},{8,16},{16,8},{128,24},{24,128},{136,144},{144,136},{0,152... | collective-permute-start | bytes 3932168 | tf_op jit(solution)/shard_map/ppermute | solution.py:393
  102.0 24.3 %copy-start = (bf16[160,4096]{1,0:T(8,128)(2,1)S(1)}, bf16[160,4096]{1,0:T(8,128)(2,1)}, u32[]{:S(2)}) copy-start(bf16[160,4096]{1,0:T(8,128)(2,1)} %get-tuple-element.27.refs_3_.own) | copy-start | bytes 3932164
  102.0 24.3 %copy-start.1 = (s32[5]{0:T(128)S(1)}, s32[5]{0:T(128)}, u32[]{:S(2)}) copy-start(s32[5]{0:T(128)} %stack.23.idx) | copy-start | bytes 64
  118.3 18.0 %all-to-all-start.4 = ((bf16[16,24,512]{2,1,0:T(8,128)(2,1)}), bf16[16,24,512]{2,1,0:T(8,128)(2,1)S(1)}, u32[]{:S(2)}, u32[]{:S(2)}) async-start(bf16[16,24,512]{2,1,0:T(8,128)(2,1)} %broadcast_in_dim.11), calls=%async_computation.4 | async-start | bytes 786432 | tf_op jit(solution)/shard_map/all_to_all | solution.py:407
Sparse Core Ops, SparseCore 0:
  11.0 63.6 all-gather.1

commit v4 on v3

--- a/solution.py
+++ b/solution.py
@@ -41,7 +41,10 @@
     return lax.dot_general(a, b, (((ca,), (cb,)), ((), ())), preferred_element_type=F32)
 
 
-def weight_kernel(idx, levels, scales, second, down, up, weight):
+def weight_kernel(idx, levels, scales, second, down, up, eighth, ids, weight, packet):
+    for k in range(SHARDS):
+        packet[k, :RANK, :] = eighth[...]
+        packet[k, RANK:, :] = ids[...]
     scale = scales[...].astype(F32)
     n = HALF // BLOCK
     scale = jnp.where(idx[0] == 0, scale[:n], scale[n:])
@@ -53,7 +56,7 @@
     weight[...] = (jnp.concatenate(rows, axis=0).T + base).astype(BF)
 
 
-def local_weight(idx, levels, scales, second, down, up):
+def local_weight(idx, levels, scales, second, down, up, ids):
     full = lambda shape: pl.BlockSpec(shape, lambda i, s: (0,) * len(shape))
     return pl.pallas_call(
         weight_kernel,
@@ -66,41 +69,19 @@
                 full((1, KEYS)),
                 pl.BlockSpec((RANK, HALF), lambda i, s: (0, s[0])),
                 full((RANK, KEYS)),
-            ],
-            out_specs=full((KEYS, HALF)),
-        ),
-        out_shape=jax.ShapeDtypeStruct((KEYS, HALF), BF),
-        compiler_params=params(56),
-        cost_estimate=BRIEF,
-        name="weight",
-    )(idx, levels, scales, second, down, up)
-
-
-def packet_kernel(idx, down, ids, after, packet):
-    for k in range(SHARDS):
-        packet[k, :RANK, :] = down[...]
-        packet[k, RANK:, :] = ids[...]
-
-
-def make_packet(idx, down, ids, after):
-    full = lambda shape: pl.BlockSpec(shape, lambda i, s: (0,) * len(shape))
-    return pl.pallas_call(
-        packet_kernel,
-        grid_spec=pltpu.PrefetchScalarGridSpec(
-            num_scalar_prefetch=1,
-            grid=(1,),
-            in_specs=[
                 pl.BlockSpec((RANK, LANES), lambda i, s: (0, s[0] * 4 + s[4])),
                 full((IDS, LANES)),
-                pl.BlockSpec(memory_space=pl.ANY),
             ],
-            out_specs=full((SHARDS, RANK + IDS, LANES)),
+            out_specs=[full((KEYS, HALF)), full((SHARDS, RANK + IDS, LANES))],
         ),
-        out_shape=jax.ShapeDtypeStruct((SHARDS, RANK + IDS, LANES), BF),
+        out_shape=[
+            jax.ShapeDtypeStruct((KEYS, HALF), BF),
+            jax.ShapeDtypeStruct((SHARDS, RANK + IDS, LANES), BF),
+        ],
         compiler_params=params(56),
         cost_estimate=BRIEF,
-        name="packet",
-    )(idx, down, ids, after)
+        name="weight",
+    )(idx, levels, scales, second, down, up, down, ids)
 
 
 def grads_kernel(idx, everyone, own, rotated, freqs, up, grads, low):
@@ -153,8 +134,8 @@
 
 
 def down_kernel(idx, low, tokens, *refs):
-    keep, send, (held, keep_held, send_held, sems) = refs[:4], refs[4:8], refs[8:]
-    c, y = idx[0], idx[4]
+    keep, send, (held, keep_held, send_held, sems) = refs[:2], refs[2:4], refs[4:]
+    c, x = idx[0], idx[2]
     loads = [
         pltpu.make_async_copy(tokens.at[:, pl.ds(i * WIDE, WIDE)], held.at[i], sems.at[i]) for i in range(CHUNKS)
     ]
@@ -169,14 +150,12 @@
             other = pl.multiple_of(k * 2 * HALF + (1 - c) * HALF, HALF)
             send_held[:, at : at + HALF] = dot(low[...], held[i, :, pl.ds(other, HALF)], 1, 0).astype(BF)
             keep_held[:, at : at + HALF] = dot(low[...], held[i, :, pl.ds(mine, HALF)], 1, 0)
-        if i % 4 == 3:
-            cols = pl.ds((i - 3) * STEP * HALF, 4 * STEP * HALF)
-            for d in range(4):
-                rows = pl.ds(pl.multiple_of(lax.rem(y + d, 4) * 16, 16), 16)
-                for source, target in ((send_held, send[d]), (keep_held, keep[d])):
-                    sem = sems.at[CHUNKS + len(stores)]
-                    stores.append(pltpu.make_async_copy(source.at[rows, cols], target.at[:, cols], sem))
-                    stores[-1].start()
+    for d in range(2):
+        half = WIDTH // 4
+        cols = pl.ds(pl.multiple_of(lax.rem(x + d, 2) * half, half), half)
+        for source, target in ((send_held, send[d]), (keep_held, keep[d])):
+            stores.append(pltpu.make_async_copy(source.at[:, cols], target, sems.at[CHUNKS + len(stores)]))
+            stores[-1].start()
     for store in stores:
         store.wait()
 
@@ -186,13 +165,13 @@
     return pl.pallas_call(
         down_kernel,
         in_specs=[pl.BlockSpec(memory_space=pltpu.SMEM), pl.BlockSpec(memory_space=pltpu.VMEM), anywhere],
-        out_specs=[anywhere] * 8,
-        out_shape=[jax.ShapeDtypeStruct((RANK // 4, WIDTH // 2), dtype) for dtype in [F32] * 4 + [BF] * 4],
+        out_specs=[anywhere] * 4,
+        out_shape=[jax.ShapeDtypeStruct((RANK, WIDTH // 4), dtype) for dtype in (F32, F32, BF, BF)],
         scratch_shapes=[
             pltpu.VMEM((CHUNKS, ROWS, WIDE), BF),
             pltpu.VMEM((RANK, WIDTH // 2), F32),
             pltpu.VMEM((RANK, WIDTH // 2), BF),
-            pltpu.SemaphoreType.DMA((CHUNKS + 16,)),
+            pltpu.SemaphoreType.DMA((CHUNKS + 4,)),
         ],
         compiler_params=params(56),
         cost_estimate=BRIEF,
@@ -201,7 +180,7 @@
 
 
 def up_kernel(idx, tokens, *refs):
-    given, (grads, _, out, held, lows, sems) = refs[:2], refs[2:]
+    given, (grads, out, held, lows, sems) = refs[:2], refs[2:]
     c = idx[0]
     loads = [
         pltpu.make_async_copy(tokens.at[:, pl.ds(i * WIDE, WIDE)], held.at[i], sems.at[i]) for i in range(CHUNKS)
@@ -220,19 +199,21 @@
                 at = pl.multiple_of(k * 2 * HALF + h * HALF, HALF)
                 rows = jnp.concatenate([lows[p, q, i * STEP + k] for q in range(4)], axis=1)
                 total = total + dot(held[i, :, pl.ds(at, HALF)], rows, 1, 1)
-    out[...] = dot(total.astype(BF), grads[...], 0, 0)
-
-
-def up_part(idx, tokens, lows, grads, after):
+    product = dot(total.astype(BF), grads[...], 0, 0).astype(BF)
+    for k in range(8):
+        half = (k // 2) % 2 * (KEYS // 2)
+        out[k] = product[:, half : half + KEYS // 2]
+
+
+def up_part(idx, tokens, lows, grads):
     anywhere = pl.BlockSpec(memory_space=pl.ANY)
     return pl.pallas_call(
         up_kernel,
         in_specs=[pl.BlockSpec(memory_space=pltpu.SMEM)]
         + [anywhere] * 3
-        + [pl.BlockSpec(memory_space=pltpu.VMEM)]
-        + [anywhere],
+        + [pl.BlockSpec(memory_space=pltpu.VMEM)],
         out_specs=pl.BlockSpec(memory_space=pltpu.VMEM),
-        out_shape=jax.ShapeDtypeStruct((RANK, KEYS), F32),
+        out_shape=jax.ShapeDtypeStruct((8, RANK, KEYS // 2), BF),
         scratch_shapes=[
             pltpu.VMEM((CHUNKS, ROWS, WIDE), BF),
             pltpu.VMEM((2, 4, SHARDS, RANK, LANES), BF),
@@ -241,10 +222,10 @@
         compiler_params=params(56),
         cost_estimate=BRIEF,
         name="up",
-    )(idx, tokens, *lows, grads, after)
-
-
-def block_kernel(own, core, there, across, weight, o0, o1, o2, o3, rows, held, made, sems):
+    )(idx, tokens, *lows, grads)
+
+
+def block_kernel(own, core, there, across, weight, after, o0, o1, o2, o3, rows, held, made, sems):
     loads = [
         pltpu.make_async_copy(weight.at[pl.ds(i * KEYS, KEYS), :], held.at[i], sems.at[4 * NZ + i]) for i in range(NZ)
     ]
@@ -269,11 +250,11 @@
         store.wait()
 
 
-def blocks(sources, weight):
+def blocks(sources, weight, after):
     anywhere = pl.BlockSpec(memory_space=pl.ANY)
     return pl.pallas_call(
         block_kernel,
-        in_specs=[pl.BlockSpec(memory_space=pltpu.VMEM)] * 4 + [anywhere],
+        in_specs=[pl.BlockSpec(memory_space=pltpu.VMEM)] * 4 + [anywhere] * 2,
         out_specs=[anywhere] * 4,
         out_shape=[jax.ShapeDtypeStruct((ROWS, NZ * HALF), BF)] * 4,
         scratch_shapes=[
@@ -285,17 +266,17 @@
         compiler_params=params(56),
         cost_estimate=BRIEF,
         name="blocks",
-    )(*sources, weight)
-
-
-def assemble_kernel(start, count, idx, own, core, there, across, *rest):
-    out, sems = rest[-2:]
+    )(*sources, weight, after)
+
+
+def assemble_kernel(places, idx, *refs):
+    out, sems = refs[-2:]
     copies = []
-    for k, piece in enumerate((own, core, there, across)):
+    for k, piece in zip(places, refs):
         x = idx[2] if k < 2 else 1 - idx[2]
         h = idx[0] if k % 2 == 0 else 1 - idx[0]
-        for j in range(count):
-            col = pl.multiple_of(((x * NZ + start + j) * 2 + h) * HALF, HALF)
+        for j in range(NZ):
+            col = pl.multiple_of(((x * NZ + j) * 2 + h) * HALF, HALF)
             copies.append(
                 pltpu.make_async_copy(
                     piece.at[:, pl.ds(j * HALF, HALF)],
@@ -309,17 +290,17 @@
         copy.wait()
 
 
-def assemble(idx, pieces, start, count, before):
+def assemble(idx, places, pieces, before):
     anywhere = pl.BlockSpec(memory_space=pl.ANY)
     return pl.pallas_call(
-        functools.partial(assemble_kernel, start, count),
+        functools.partial(assemble_kernel, places),
         in_specs=[pl.BlockSpec(memory_space=pltpu.SMEM)]
-        + [pl.BlockSpec(memory_space=pltpu.VMEM)] * 4
+        + [pl.BlockSpec(memory_space=pltpu.VMEM)] * len(pieces)
         + [anywhere] * len(before),
         out_specs=anywhere,
-        scratch_shapes=[pltpu.SemaphoreType.DMA((4 * count,))],
+        scratch_shapes=[pltpu.SemaphoreType.DMA((NZ * len(pieces),))],
         out_shape=jax.ShapeDtypeStruct((ROWS, WIDTH), BF),
-        input_output_aliases={5: 0} if before else {},
+        input_output_aliases={1 + len(pieces): 0} if before else {},
         compiler_params=params(8),
         cost_estimate=BRIEF,
         name="assemble",
@@ -349,11 +330,9 @@
     xh, y, c, xl, z = (lax.axis_index(a) for a in ("xh", "y", "c", "xl", "z"))
     idx = jnp.stack([c, xh, xl, xl * NZ + z, y]).astype(jnp.int32)
 
-    weight = local_weight(idx, levels, scales, second, down.T, up)
-
     ids = jnp.pad(documents.astype(BF), ((0, 0), (0, 2 * LANES - ROWS)), constant_values=1000.0)
     ids = jnp.pad(ids.reshape(2, LANES), ((0, IDS - 2), (0, 0)))
-    packet = make_packet(idx, down.T, ids, weight)
+    weight, packet = local_weight(idx, levels, scales, second, down.T, up, ids)
     weight = lax.all_gather(weight, "z", tiled=True)
     everyone = lax.all_to_all(packet, SHARD_AXES, 0, 0, tiled=True)
 
@@ -372,7 +351,7 @@
     ]
 
     made = down_part(idx, low, tokens)
-    keep, send = made[:4], made[4:]
+    keep, send = made[:2], made[2:]
     sent = [lax.ppermute(part, "c", CORE) for part in send]
 
     lows = jnp.broadcast_to(everyone[None, :, :RANK], (4, SHARDS, RANK, LANES))
@@ -380,12 +359,20 @@
     lows, sent = lax.optimization_barrier((lows, sent))
     lows = [lows, lax.ppermute(lows, "c", CORE)]
 
-    total = [a + b.astype(F32) for a, b in zip(keep, sent)]
-    mine = total[0]
-    for d in (1, 3, 2):
-        mine = mine + lax.ppermute(total[d].astype(BF), "y", [(i, (i + d) % 4) for i in range(4)]).astype(F32)
-
-    parts = blocks(sources, weight)
+    halves = [(a + b.astype(F32)).reshape(2, RANK // 2, WIDTH // 4) for a, b in zip(keep, sent)]
+    own_half = lax.dynamic_index_in_dim(halves[0], xh, 0, keepdims=False)
+    parcels = [
+        lax.dynamic_index_in_dim(half, at, 0, keepdims=False).astype(BF)
+        for half, at in ((halves[0], 1 - xh), (halves[1], xh), (halves[1], 1 - xh))
+    ]
+    parcels, sources[1:] = lax.optimization_barrier((parcels, sources[1:]))
+    parcels = [
+        lax.ppermute(parcel, ("xh", "xl"), [(i, i ^ bits) for i in range(4)])
+        for parcel, bits in zip(parcels, (2, 1, 3))
+    ]
+
+    up_total = up_part(idx, tokens, lows, grads)
+    parts = blocks(sources, weight, up_total)
     pieces = [
         parts[0],
         lax.ppermute(parts[1], "c", CORE),
@@ -393,25 +380,33 @@
         lax.ppermute(parts[3], X_AXES, inverse(across)),
     ]
 
-    up_total = up_part(idx, tokens, lows, grads, parts[0]).reshape(8, 8, KEYS)
-    up_total = jnp.sum(lax.all_to_all(up_total, ("y", "c"), 0, 0, tiled=True), axis=0)
-
-    slabs = mine.reshape(RANK // 4, SHARDS, HALF).transpose(1, 0, 2)
-    up_total = jnp.broadcast_to(up_total[None], (SHARDS,) + up_total.shape)
-    slabs = jnp.concatenate([slabs, up_total], axis=1).astype(BF)
+    up_total = lax.all_to_all(up_total, X_AXES, 0, 0, tiled=True)
+    parcels, up_total, _ = lax.optimization_barrier((parcels, up_total, parts[0]))
+    up_total = jnp.sum(up_total.astype(F32), axis=0).reshape(4, RANK // 8, KEYS)
+    total = own_half + parcels[0].astype(F32) + parcels[1].astype(F32) + parcels[2].astype(F32)
+    total = jnp.concatenate([total.reshape(4, RANK // 8, WIDTH // 4), up_total], axis=2)
+    mine = lax.dynamic_index_in_dim(total, y, 0, keepdims=False)
+    for d in (1, 3, 2):
+        out = lax.dynamic_index_in_dim(total, (y + d) % 4, 0, keepdims=False).astype(BF)
+        mine = mine + lax.ppermute(out, "y", [(i, (i + d) % 4) for i in range(4)]).astype(F32)
+    total = mine.astype(BF)
+
+    slabs = total[:, : WIDTH // 4].reshape(RANK // 8, NZ, HALF).transpose(1, 0, 2)
+    up_total = jnp.broadcast_to(total[None, :, WIDTH // 4 :], (NZ, RANK // 8, KEYS))
+    slabs = jnp.concatenate([slabs, up_total], axis=1)
+    slabs = lax.all_to_all(slabs, "z", 0, 0, tiled=True)
+    slabs = jnp.sum(slabs.astype(F32), axis=0).astype(BF)
     slabs, pieces[2] = lax.optimization_barrier((slabs, pieces[2]))
-    slabs = lax.all_to_all(slabs, SHARD_AXES, 0, 0, tiled=True)
-    slabs = jnp.sum(slabs.astype(F32), axis=0).astype(BF)
-    slabs, pieces[3] = lax.optimization_barrier((slabs, pieces[3]))
     slabs = jnp.broadcast_to(slabs[None], (16,) + slabs.shape)
     slabs = lax.all_to_all(slabs, DP_AXES, 0, 0, tiled=True).astype(F32)
-    slabs = slabs.reshape(2, 4, 2, RANK // 4 + 8, KEYS)
     factor = SCALE / jnp.sqrt(jnp.float32(TOKENS))
-    slabs = factor * (slabs[0] + slabs[1])
-    grad_down = slabs[:, :, : RANK // 4].transpose(1, 3, 0, 2).reshape(2 * HALF, RANK)
-    grad_up = slabs[:, :, RANK // 4 :].reshape(RANK, KEYS)
-
-    grad_tokens = assemble(idx, pieces, 0, NZ, [])
+    slabs = factor * slabs.reshape(2, 4, 2, RANK // 4, KEYS)
+    grad_down = slabs[:, :, :, : RANK // 8].transpose(2, 4, 0, 1, 3).reshape(2 * HALF, RANK)
+    grad_up = slabs[0, :, :, RANK // 8 :].reshape(4, 2, RANK // 4, KEYS // 2)
+    grad_up = grad_up.transpose(0, 2, 1, 3).reshape(RANK, KEYS)
+
+    grad_tokens = assemble(idx, (0, 1, 2), pieces[:3], [])
+    grad_tokens = assemble(idx, (3,), pieces[3:], [grad_tokens])
     return grad_tokens, grad_down, grad_up
 
 

time: 146 us -> 138 us (0.945)
  waiting for transfers between devices: 16.2 us -> 9.26 us
  blocking collectives: 36.5 us -> 31.2 us
  starting transfers between devices: 34.6 us -> 37.5 us
    ppermute x1, waiting for transfers between devices: 0.03 us -> 5.65 us  [on_device(): lax.ppermute(parts[3], X_AXES, inverse(across))]
    all_to_all x1, waiting for transfers between devices: 5.54 us -> 0.1 us  [on_device(): slabs = lax.all_to_all(slabs, DP_AXES, 0, 0, tiled=True).astype(F32)]
    all_gather x1, waiting for transfers between devices: 5.24 us -> 0.01 us  [on_device(): weight = lax.all_gather(weight, 'z', tiled=True)]
    all_to_all x1, waiting for transfers between devices: 4.1 us -> 0.01 us  [on_device(): up_total = lax.all_to_all(up_total, X_AXES, 0, 0, tiled=True)]
    all_to_all x1, blocking collectives: 15.4 us -> 11.4 us  [on_device(): slabs = lax.all_to_all(slabs, 'z', 0, 0, tiled=True)]
    ppermute x3 -> x6, starting transfers between devices: 4.71 us -> 8.15 us  [the longest x3 4.74 us: on_device(): lax.ppermute(out, 'y', [(i, (i + d) % 4) for i in range(4)]).astype(F32)]
    convert_element_type x4 -> x2, other arithmetic: 3.75 us -> 0.73 us  [the longest x1 0.69 us: on_device(): lax.dynamic_index_in_dim(total, (y + d) % 4, 0, keepdims=False).astype(BF)]
    ppermute x1, waiting for transfers between devices: 0.01 us -> 2.23 us  [on_device(): lax.ppermute(parts[2], X_AXES, inverse(there))]
  transfers between devices with their start and end apart: 18 -> 19, of which waited for: 5 -> 4; matrix products, arithmetic and copies ran while one was open for 6% -> 4% of each run, Pallas kernels for 20% -> 21%
where the time goes in v4:
time: 138 us; the launch traced here: 136 us
  starting transfers between devices  37.5 us (27%)
  Pallas kernels  31.9 us (23%)
  blocking collectives  31.2 us (23%)
  between operations  14.3 us (10%)
  waiting for transfers between devices  9.26 us (7%)
  local copies, waits for them, and re-layouts  6.77 us (5%)
  other arithmetic  4.89 us (4%)
    all_to_all x1, blocking collectives, on_device(): everyone = lax.all_to_all(packet, SHARD_AXES, 0, 0, tiled=True)  19.8 us
    all_to_all x1, blocking collectives, on_device(): slabs = lax.all_to_all(slabs, 'z', 0, 0, tiled=True)  11.4 us
    pallas_call x1, Pallas kernels, blocks(): pl.pallas_call(block_kernel, in_specs=[pl.BlockSpec(memory_space=pltpu.VM...  7.46 us
    pallas_call x1, Pallas kernels, up_part(): pl.pallas_call(up_kernel, in_specs=[pl.BlockSpec(memory_space=pltpu.SMEM)...  6.74 us
    all_to_all x1, starting transfers between devices, on_device(): slabs = lax.all_to_all(slabs, DP_AXES, 0, 0, tiled=True).astype(F32)  6.33 us
    all_to_all x1, starting transfers between devices, on_device(): up_total = lax.all_to_all(up_total, X_AXES, 0, 0, tiled=True)  6.04 us
    pallas_call x2, Pallas kernels, assemble(): pl.pallas_call(functools.partial(assemble_kernel, places), in_specs=[pl.B...  5.89 us
    ppermute x1, waiting for transfers between devices, on_device(): lax.ppermute(parts[3], X_AXES, inverse(across))  5.65 us
  transfers between devices with their start and end apart: 19, of which 4 were waited for; matrix products, arithmetic and copies ran while one was open for 4% of the time, Pallas kernels for 21%

profile of v4, /device:TPU:1, one launch (start us, length us, event | category | flops | bytes accessed | tf_op | source)
XLA Modules:
  0.0 135.9 jit_solution(3292685912686739062)
XLA Ops:
  7.2 0.0 all-gather.2.cloned.1.call-start
  7.2 0.8 convert_bitcast_fusion
  8.0 0.6 pad.9.ids
  8.6 0.6 stack.23.idx
  9.2 3.1 %weight.1 = (bf16[512,512]{1,0:T(8,128)(2,1)}, bf16[16,80,128]{2,1,0:T(8,128)(2,1)}) custom-call(s32[5]{0:T(128)} %stack.23.idx, bf16[1024,512]{1,0:T(8,128)(2,1)} %levels.1, bf16[16,512]{1,0:T(8,128)(2,1)} %scales.1, f32[1,512]{1,0:T(1,128)} %second.1, bf16[64,1024]{1,0:T(8,128)(2,1)} %bitcast.63, bf16[64,512]{1,0:T(8,128)(2,1)} %up.4, ...), custom_call_target="tpu_custom_call" | custom-call | flops 1 | bytes 1 | tf_op jit(solution)/shard_map/weight/pallas_call | solution.py:61
  12.3 0.0 all-gather.2.cloned.1.call-update
  12.3 19.8 %all_to_all.25.everyone = bf16[16,80,128]{2,1,0:T(8,128)(2,1)S(1)} all-to-all(bf16[16,80,128]{2,1,0:T(8,128)(2,1)} %get-tuple-element.30), channel_id=1, replica_groups=mesh['xh'=2,'y'=4,'c'=2,'xl'=2,'z'=8] {'xl','z'}, dimensions={0} | all-to-all | bytes 655360 | tf_op jit(solution)/shard_map/all_to_all | solution.py:337
  32.2 1.2 broadcast_in_dim.9
  33.4 4.2 %all-to-all-start.1 = ((bf16[4,16,64,128]{3,2,1,0:T(8,128)(2,1)}), bf16[4,16,64,128]{3,2,1,0:T(8,128)(2,1)S(1)}, u32[]{:S(2)}, u32[]{:S(2)}) async-start(bf16[4,16,64,128]{3,2,1,0:T(8,128)(2,1)} %broadcast_in_dim.9), calls=%async_computation.1 | async-start | bytes 2097152 | tf_op jit(solution)/shard_map/all_to_all | solution.py:358
  37.6 0.8 copy.13.own
  38.3 0.6 maximum_bitcast_fusion.freqs
  38.9 3.2 %grads.1 = (bf16[160,512]{1,0:T(8,128)(2,1)}, bf16[64,160]{1,0:T(8,128)(2,1)}) custom-call(s32[5]{0:T(128)} %stack.23.idx, bf16[16,80,128]{2,1,0:T(8,128)(2,1)} %copy-done.3, f32[160,1]{1,0:T(8,128)} %copy.13.own, bf16[160,512]{1,0:T(8,128)(2,1)} %rotated.1, f32[1,128]{1,0:T(1,128)} %maximum_bitcast_fusion.freqs, bf16[64,512]{1,0:T(8,128)(2,1)} %up.4), custom_call_target="tpu_custom_call" | custom-call | flops 1 | bytes 1 | tf_op jit(solution)/shard_map/grads/pallas_call | solution.py:110
  42.1 5.6 %down.1 = (f32[64,4096]{1,0:T(8,128)}, f32[64,4096]{1,0:T(8,128)}, bf16[64,4096]{1,0:T(8,128)(2,1)}, bf16[64,4096]{1,0:T(8,128)(2,1)}) custom-call(s32[5]{0:T(128)} %stack.23.idx, bf16[64,160]{1,0:T(8,128)(2,1)} %get-tuple-element.32.low, bf16[160,16384]{1,0:T(8,128)(2,1)} %tokens.3), custom_call_target="tpu_custom_call" | custom-call | flops 1 | bytes 1 | tf_op jit(solution)/shard_map/down/pallas_call | solution.py:165
  47.7 4.8 %collective-permute-start = (bf16[64,4096]{1,0:T(8,128)(2,1)}, bf16[64,4096]{1,0:T(8,128)(2,1)S(1)}, u32[]{:S(2)}, u32[]{:S(2)}) collective-permute-start(bf16[64,4096]{1,0:T(8,128)(2,1)} %get-tuple-element.34), channel_id=1, source_target_pairs={{0,16},{16,0},{1,17},{17,1},{2,18},{18,2},{3,19},{19,3},{4,20},{20... | collective-permute-start | bytes 1572872 | tf_op jit(solution)/shard_map/ppermute | solution.py:355
  52.5 0.1 collective-permute-start.1
  52.6 0.4 collective-permute-start.2
  53.0 1.2 collective-permute-start.3
  54.3 1.3 collective-permute-start.4
  55.6 0.0 collective-permute-done
  55.6 0.0 collective-permute-done.1
  55.6 0.0 all-to-all-done.1.refs_0_
  55.6 0.0 copy-start.2
  55.6 0.8 collective-permute-start.5
  56.4 1.4 %convert_add_fusion.1 = f32[64,4096]{1,0:T(8,128)S(1)} fusion(f32[64,4096]{1,0:T(8,128)} %get-tuple-element.33, bf16[64,4096]{1,0:T(8,128)(2,1)S(1)} %collective-permute-done), kind=kLoop, calls=%fused_computation.5 | loop fusion | flops 524288 | bytes 2621440 | tf_op jit(solution)/shard_map/add | solution.py:362
  57.9 0.1 copy-done.5
  58.0 0.1 convert_add_fusion
  58.2 0.0 collective-permute-done.2.core
  58.2 0.0 collective-permute-done.3.there
  58.2 1.2 collective-permute-done.4.across
  59.4 2.8 %collective-permute-start.10 = (bf16[32,4096]{1,0:T(8,128)(2,1)S(1)}, bf16[32,4096]{1,0:T(8,128)(2,1)S(1)}, u32[]{:S(2)}, u32[]{:S(2)}) collective-permute-start(bf16[32,4096]{1,0:T(8,128)(2,1)S(1)} %get-tuple-element.49), channel_id=1, source_target_pairs={{0,136},{8,128},{128,8},{136,0},{1,137},{9,129},{129,9},{137,1},{2... | collective-permute-start | bytes 786440 | tf_op jit(solution)/shard_map/ppermute | solution.py:370
  62.3 0.0 collective-permute-start.8
  62.3 0.6 collective-permute-start.9
  62.8 0.0 collective-permute-done.5.refs_1_
  62.9 1.0 copy-done.4
  63.9 6.7 %up.5.after = bf16[8,64,256]{2,1,0:T(8,128)(2,1)} custom-call(s32[5]{0:T(128)} %stack.23.idx, bf16[160,16384]{1,0:T(8,128)(2,1)} %tokens.3, bf16[4,16,64,128]{3,2,1,0:T(8,128)(2,1)} %copy-done.2, bf16[4,16,64,128]{3,2,1,0:T(8,128)(2,1)} %copy-done.4, bf16[160,512]{1,0:T(8,128)(2,1)} %get-tuple-element.31.refs_2_.own), custom_call_target="tpu_custom_call" | custom-call | flops 1 | bytes 1 | tf_op jit(solution)/shard_map/up/pallas_call | solution.py:210
  70.6 6.0 %all-to-all-start.2 = ((bf16[8,64,256]{2,1,0:T(8,128)(2,1)}), bf16[8,64,256]{2,1,0:T(8,128)(2,1)S(1)}, u32[]{:S(2)}, u32[]{:S(2)}) async-start(bf16[8,64,256]{2,1,0:T(8,128)(2,1)} %up.5.after), calls=%async_computation.2 | async-start | bytes 524288 | tf_op jit(solution)/shard_map/all_to_all | solution.py:383
  76.6 7.5 %blocks.1 = (bf16[160,4096]{1,0:T(8,128)(2,1)}, bf16[160,4096]{1,0:T(8,128)(2,1)}, bf16[160,4096]{1,0:T(8,128)(2,1)}, bf16[160,4096]{1,0:T(8,128)(2,1)}) custom-call(bf16[160,512]{1,0:T(8,128)(2,1)} %get-tuple-element.31.refs_2_.own, bf16[160,512]{1,0:T(8,128)(2,1)} %copy-done.7, bf16[160,512]{1,0:T(8,128)(2,1)} %collective-permute-done.3.there, ...), custom_call_target="tpu_custom_call" | custom-call | flops 1 | bytes 1 | tf_op jit(solution)/shard_map/blocks/pallas_call | solution.py:255
  84.1 0.0 collective-permute-done.10
  84.1 0.0 collective-permute-done.8
  84.1 0.0 collective-permute-done.9
  84.1 0.0 all-to-all-done.2
  84.2 1.2 fusion.2
  85.4 0.7 fusion.19
  86.1 1.8 %collective-permute-start.11 = (bf16[8,4608]{1,0:T(8,128)(2,1)}, bf16[8,4608]{1,0:T(8,128)(2,1)S(1)}, u32[]{:S(2)}, u32[]{:S(2)}) collective-permute-start(bf16[8,4608]{1,0:T(8,128)(2,1)} %get-tuple-element.57), channel_id=1, source_target_pairs={{0,32},{32,64},{64,96},{96,0},{1,33},{33,65},{65,97},{97,1},{2,34}... | collective-permute-start | bytes 221192 | tf_op jit(solution)/shard_map/ppermute | solution.py:391
  87.8 1.3 collective-permute-start.12
  89.1 1.7 %collective-permute-start.13 = (bf16[8,4608]{1,0:T(8,128)(2,1)S(1)}, bf16[8,4608]{1,0:T(8,128)(2,1)S(1)}, u32[]{:S(2)}, u32[]{:S(2)}) collective-permute-start(bf16[8,4608]{1,0:T(8,128)(2,1)S(1)} %get-tuple-element.59), channel_id=1, source_target_pairs={{0,64},{32,96},{64,0},{96,32},{1,65},{33,97},{65,1},{97,33},{2,66}... | collective-permute-start | bytes 221192 | tf_op jit(solution)/shard_map/ppermute | solution.py:391
  90.8 1.4 %collective-permute-start.14 = (bf16[160,4096]{1,0:T(8,128)(2,1)}, bf16[160,4096]{1,0:T(8,128)(2,1)S(1)}, u32[]{:S(2)}, u32[]{:S(2)}) collective-permute-start(bf16[160,4096]{1,0:T(8,128)(2,1)} %get-tuple-element.54), channel_id=1, source_target_pairs={{8,0},{152,16},{128,8},{16,24},{136,128},{24,144},{0,136},{144,152... | collective-permute-start | bytes 3932168 | tf_op jit(solution)/shard_map/ppermute | solution.py:379
  92.2 2.7 %collective-permute-start.7 = (bf16[160,4096]{1,0:T(8,128)(2,1)}, bf16[160,4096]{1,0:T(8,128)(2,1)}, u32[]{:S(2)}, u32[]{:S(2)}) collective-permute-start(bf16[160,4096]{1,0:T(8,128)(2,1)} %get-tuple-element.46), channel_id=1, source_target_pairs={{0,16},{16,0},{1,17},{17,1},{2,18},{18,2},{3,19},{19,3},{4,20},{20... | collective-permute-start | bytes 3932168 | tf_op jit(solution)/shard_map/ppermute | solution.py:378
  94.9 0.0 collective-permute-done.11
  94.9 0.0 collective-permute-start.6
  94.9 0.0 collective-permute-done.13
  95.0 11.4 %all_to_all.26 = bf16[8,16,512]{2,1,0:T(8,128)(2,1)S(1)} all-to-all(bf16[8,16,512]{2,1,0:T(8,128)(2,1)S(1)} %pad_maximum_fusion), channel_id=1, replica_groups=mesh['xh'=2,'y'=4,'c'=2,'xl'=2,'z'=8] {'z'}, dimensions={0} | all-to-all | bytes 262144 | tf_op jit(solution)/shard_map/all_to_all | solution.py:397
  106.5 2.2 %collective-permute-done.14.refs_2_ = bf16[160,4096]{1,0:T(8,128)(2,1)S(1)} collective-permute-done((bf16[160,4096]{1,0:T(8,128)(2,1)}, bf16[160,4096]{1,0:T(8,128)(2,1)S(1)}, u32[]{:S(2)}, u32[]{:S(2)}) %collective-permute-start.14) | collective-permute-done | bytes 1310752 | tf_op jit(solution)/shard_map/ppermute | solution.py:379
  108.7 0.7 broadcast_in_dim.11
  109.4 6.3 %all-to-all-start.4 = ((bf16[16,16,512]{2,1,0:T(8,128)(2,1)}), bf16[16,16,512]{2,1,0:T(8,128)(2,1)S(1)}, u32[]{:S(2)}, u32[]{:S(2)}) async-start(bf16[16,16,512]{2,1,0:T(8,128)(2,1)} %broadcast_in_dim.11), calls=%async_computation.4 | async-start | bytes 524288 | tf_op jit(solution)/shard_map/all_to_all | solution.py:401
  115.8 0.0 collective-permute-done.7.refs_1_
  115.8 3.4 %assemble.2.refs_1_ = bf16[160,16384]{1,0:T(8,128)(2,1)} custom-call(s32[5]{0:T(128)S(1)} %copy-done.1, bf16[160,4096]{1,0:T(8,128)(2,1)S(1)} %copy-done, bf16[160,4096]{1,0:T(8,128)(2,1)} %collective-permute-done.7.refs_1_, bf16[160,4096]{1,0:T(8,128)(2,1)S(1)} %collective-permute-done.14.refs_2_), custom_call_target="tpu_custom_call" | custom-call | flops 1 | bytes 1 | tf_op jit(solution)/shard_map/assemble/pallas_call | solution.py:295
  119.2 5.6 %collective-permute-done.6.refs_0_ = bf16[160,4096]{1,0:T(8,128)(2,1)} collective-permute-done((bf16[160,4096]{1,0:T(8,128)(2,1)}, bf16[160,4096]{1,0:T(8,128)(2,1)}, u32[]{:S(2)}, u32[]{:S(2)}) %collective-permute-start.6) | collective-permute-done | bytes 1310752 | tf_op jit(solution)/shard_map/ppermute | solution.py:380
  124.9 2.4 %assemble.3 = bf16[160,16384]{1,0:T(8,128)(2,1)} custom-call(s32[5]{0:T(128)S(1)} %copy-done.1, bf16[160,4096]{1,0:T(8,128)(2,1)} %collective-permute-done.6.refs_0_, bf16[160,16384]{1,0:T(8,128)(2,1)} %assemble.2.refs_1_), custom_call_target="tpu_custom_call", output_to_operand_aliasing={{}: (2, {})} | custom-call | flops 1 | bytes 1 | tf_op jit(solution)/shard_map/assemble/pallas_call | solution.py:295
  127.3 0.1 all-to-all-done.4
  127.4 0.1 convert_multiply_fusion
  127.5 0.7 slice.23
  128.3 0.1 copy.14
  128.4 0.7 copy.15
  (30 shorter events, 0.3 us)
Async XLA Ops:
  7.2 69.5 %all-gather.2.cloned.1.call-start = ((), (), s32[]{:S(2)}) async-start(), calls=%async_computation.5 | async-start | bytes 4718592 | tf_op jit(solution)/shard_map/all_gather | solution.py:336
  32.2 1.3 copy-start.3
  33.4 22.2 %all-to-all-start.1 = ((bf16[4,16,64,128]{3,2,1,0:T(8,128)(2,1)}), bf16[4,16,64,128]{3,2,1,0:T(8,128)(2,1)S(1)}, u32[]{:S(2)}, u32[]{:S(2)}) async-start(bf16[4,16,64,128]{3,2,1,0:T(8,128)(2,1)} %broadcast_in_dim.9), calls=%async_computation.1 | async-start | bytes 2097152 | tf_op jit(solution)/shard_map/all_to_all | solution.py:358
  42.1 10.6 %copy-start.6 = (bf16[160,512]{1,0:T(8,128)(2,1)S(1)}, bf16[160,512]{1,0:T(8,128)(2,1)}, u32[]{:S(2)}) copy-start(bf16[160,512]{1,0:T(8,128)(2,1)} %get-tuple-element.31.refs_2_.own) | copy-start | bytes 491524
  47.7 7.9 %collective-permute-start = (bf16[64,4096]{1,0:T(8,128)(2,1)}, bf16[64,4096]{1,0:T(8,128)(2,1)S(1)}, u32[]{:S(2)}, u32[]{:S(2)}) collective-permute-start(bf16[64,4096]{1,0:T(8,128)(2,1)} %get-tuple-element.34), channel_id=1, source_target_pairs={{0,16},{16,0},{1,17},{17,1},{2,18},{18,2},{3,19},{19,3},{4,20},{20... | collective-permute-start | bytes 1572872 | tf_op jit(solution)/shard_map/ppermute | solution.py:355
  52.5 3.0 %collective-permute-start.1 = (bf16[64,4096]{1,0:T(8,128)(2,1)}, bf16[64,4096]{1,0:T(8,128)(2,1)S(1)}, u32[]{:S(2)}, u32[]{:S(2)}) collective-permute-start(bf16[64,4096]{1,0:T(8,128)(2,1)} %get-tuple-element.35), channel_id=1, source_target_pairs={{0,16},{16,0},{1,17},{17,1},{2,18},{18,2},{3,19},{19,3},{4,20},{20... | collective-permute-start | bytes 1572872 | tf_op jit(solution)/shard_map/ppermute | solution.py:355
  52.6 5.6 %collective-permute-start.2 = (bf16[160,512]{1,0:T(8,128)(2,1)S(1)}, bf16[160,512]{1,0:T(8,128)(2,1)S(1)}, u32[]{:S(2)}, u32[]{:S(2)}) collective-permute-start(bf16[160,512]{1,0:T(8,128)(2,1)S(1)} %copy-done.6), channel_id=1, source_target_pairs={{0,16},{16,0},{1,17},{17,1},{2,18},{18,2},{3,19},{19,3},{4,20},{20... | collective-permute-start | bytes 491528 | tf_op jit(solution)/shard_map/ppermute | solution.py:348
  53.0 5.2 %collective-permute-start.3 = (bf16[160,512]{1,0:T(8,128)(2,1)S(1)}, bf16[160,512]{1,0:T(8,128)(2,1)}, u32[]{:S(2)}, u32[]{:S(2)}) collective-permute-start(bf16[160,512]{1,0:T(8,128)(2,1)S(1)} %copy-done.6), channel_id=1, source_target_pairs={{0,8},{16,152},{8,128},{24,16},{128,136},{144,24},{136,0},{152,144... | collective-permute-start | bytes 491528 | tf_op jit(solution)/shard_map/ppermute | solution.py:349
  54.3 5.1 %collective-permute-start.4 = (bf16[160,512]{1,0:T(8,128)(2,1)S(1)}, bf16[160,512]{1,0:T(8,128)(2,1)}, u32[]{:S(2)}, u32[]{:S(2)}) collective-permute-start(bf16[160,512]{1,0:T(8,128)(2,1)S(1)} %copy-done.6), channel_id=1, source_target_pairs={{0,152},{16,8},{8,16},{24,128},{128,24},{144,136},{136,144},{152,0... | collective-permute-start | bytes 491528 | tf_op jit(solution)/shard_map/ppermute | solution.py:350
  55.6 2.3 %copy-start.2 = (bf16[4,16,64,128]{3,2,1,0:T(8,128)(2,1)}, bf16[4,16,64,128]{3,2,1,0:T(8,128)(2,1)S(1)}, u32[]{:S(2)}) copy-start(bf16[4,16,64,128]{3,2,1,0:T(8,128)(2,1)S(1)} %all-to-all-done.1.refs_0_) | copy-start | bytes 3145732
  55.6 7.3 %collective-permute-start.5 = (bf16[4,16,64,128]{3,2,1,0:T(8,128)(2,1)S(1)}, bf16[4,16,64,128]{3,2,1,0:T(8,128)(2,1)S(1)}, u32[]{:S(2)}, u32[]{:S(2)}) collective-permute-start(bf16[4,16,64,128]{3,2,1,0:T(8,128)(2,1)S(1)} %all-to-all-done.1.refs_0_), channel_id=1, source_target_pairs={{0,16},{16,0},{1,17},{17,1},{2,18},{18,2},{3,19},{19,3},{4,20},{20... | collective-permute-start | bytes 3145736 | tf_op jit(solution)/shard_map/ppermute | solution.py:360
  56.4 1.6 %copy-start.5 = (f32[64,4096]{1,0:T(8,128)S(1)}, f32[64,4096]{1,0:T(8,128)}, u32[]{:S(2)}) copy-start(f32[64,4096]{1,0:T(8,128)} %get-tuple-element.37) | copy-start | bytes 3145732
  58.2 1.2 copy-start.7
  59.4 24.7 %collective-permute-start.10 = (bf16[32,4096]{1,0:T(8,128)(2,1)S(1)}, bf16[32,4096]{1,0:T(8,128)(2,1)S(1)}, u32[]{:S(2)}, u32[]{:S(2)}) collective-permute-start(bf16[32,4096]{1,0:T(8,128)(2,1)S(1)} %get-tuple-element.49), channel_id=1, source_target_pairs={{0,136},{8,128},{128,8},{136,0},{1,137},{9,129},{129,9},{137,1},{2... | collective-permute-start | bytes 786440 | tf_op jit(solution)/shard_map/ppermute | solution.py:370
  62.3 21.9 %collective-permute-start.8 = (bf16[32,4096]{1,0:T(8,128)(2,1)S(1)}, bf16[32,4096]{1,0:T(8,128)(2,1)}, u32[]{:S(2)}, u32[]{:S(2)}) collective-permute-start(bf16[32,4096]{1,0:T(8,128)(2,1)S(1)} %fusion.3), channel_id=1, source_target_pairs={{0,128},{8,136},{128,0},{136,8},{1,129},{9,137},{129,1},{137,9},{2... | collective-permute-start | bytes 786440 | tf_op jit(solution)/shard_map/ppermute | solution.py:370
  62.3 21.9 %collective-permute-start.9 = (bf16[32,4096]{1,0:T(8,128)(2,1)S(1)}, bf16[32,4096]{1,0:T(8,128)(2,1)}, u32[]{:S(2)}, u32[]{:S(2)}) collective-permute-start(bf16[32,4096]{1,0:T(8,128)(2,1)S(1)} %get-tuple-element.48), channel_id=1, source_target_pairs={{0,8},{8,0},{128,136},{136,128},{1,9},{9,1},{129,137},{137,129},{2... | collective-permute-start | bytes 786440 | tf_op jit(solution)/shard_map/ppermute | solution.py:370
  62.9 1.0 copy-start.4
  70.6 13.5 %all-to-all-start.2 = ((bf16[8,64,256]{2,1,0:T(8,128)(2,1)}), bf16[8,64,256]{2,1,0:T(8,128)(2,1)S(1)}, u32[]{:S(2)}, u32[]{:S(2)}) async-start(bf16[8,64,256]{2,1,0:T(8,128)(2,1)} %up.5.after), calls=%async_computation.2 | async-start | bytes 524288 | tf_op jit(solution)/shard_map/all_to_all | solution.py:383
  86.1 29.7 %copy-start = (bf16[160,4096]{1,0:T(8,128)(2,1)S(1)}, bf16[160,4096]{1,0:T(8,128)(2,1)}, u32[]{:S(2)}) copy-start(bf16[160,4096]{1,0:T(8,128)(2,1)} %get-tuple-element.45.refs_0_) | copy-start | bytes 3932164
  86.1 29.7 %copy-start.1 = (s32[5]{0:T(128)S(1)}, s32[5]{0:T(128)}, u32[]{:S(2)}) copy-start(s32[5]{0:T(128)} %stack.23.idx) | copy-start | bytes 64
  86.1 8.8 %collective-permute-start.11 = (bf16[8,4608]{1,0:T(8,128)(2,1)}, bf16[8,4608]{1,0:T(8,128)(2,1)S(1)}, u32[]{:S(2)}, u32[]{:S(2)}) collective-permute-start(bf16[8,4608]{1,0:T(8,128)(2,1)} %get-tuple-element.57), channel_id=1, source_target_pairs={{0,32},{32,64},{64,96},{96,0},{1,33},{33,65},{65,97},{97,1},{2,34}... | collective-permute-start | bytes 221192 | tf_op jit(solution)/shard_map/ppermute | solution.py:391
  87.8 7.1 %collective-permute-start.12 = (bf16[8,4608]{1,0:T(8,128)(2,1)}, bf16[8,4608]{1,0:T(8,128)(2,1)S(1)}, u32[]{:S(2)}, u32[]{:S(2)}) collective-permute-start(bf16[8,4608]{1,0:T(8,128)(2,1)} %get-tuple-element.58), channel_id=1, source_target_pairs={{0,96},{32,0},{64,32},{96,64},{1,97},{33,1},{65,33},{97,65},{2,98}... | collective-permute-start | bytes 221192 | tf_op jit(solution)/shard_map/ppermute | solution.py:391
  89.1 5.8 %collective-permute-start.13 = (bf16[8,4608]{1,0:T(8,128)(2,1)S(1)}, bf16[8,4608]{1,0:T(8,128)(2,1)S(1)}, u32[]{:S(2)}, u32[]{:S(2)}) collective-permute-start(bf16[8,4608]{1,0:T(8,128)(2,1)S(1)} %get-tuple-element.59), channel_id=1, source_target_pairs={{0,64},{32,96},{64,0},{96,32},{1,65},{33,97},{65,1},{97,33},{2,66}... | collective-permute-start | bytes 221192 | tf_op jit(solution)/shard_map/ppermute | solution.py:391
  90.8 17.9 %collective-permute-start.14 = (bf16[160,4096]{1,0:T(8,128)(2,1)}, bf16[160,4096]{1,0:T(8,128)(2,1)S(1)}, u32[]{:S(2)}, u32[]{:S(2)}) collective-permute-start(bf16[160,4096]{1,0:T(8,128)(2,1)} %get-tuple-element.54), channel_id=1, source_target_pairs={{8,0},{152,16},{128,8},{16,24},{136,128},{24,144},{0,136},{144,152... | collective-permute-start | bytes 3932168 | tf_op jit(solution)/shard_map/ppermute | solution.py:379
  92.2 23.6 %collective-permute-start.7 = (bf16[160,4096]{1,0:T(8,128)(2,1)}, bf16[160,4096]{1,0:T(8,128)(2,1)}, u32[]{:S(2)}, u32[]{:S(2)}) collective-permute-start(bf16[160,4096]{1,0:T(8,128)(2,1)} %get-tuple-element.46), channel_id=1, source_target_pairs={{0,16},{16,0},{1,17},{17,1},{2,18},{18,2},{3,19},{19,3},{4,20},{20... | collective-permute-start | bytes 3932168 | tf_op jit(solution)/shard_map/ppermute | solution.py:378
  94.9 30.0 %collective-permute-start.6 = (bf16[160,4096]{1,0:T(8,128)(2,1)}, bf16[160,4096]{1,0:T(8,128)(2,1)}, u32[]{:S(2)}, u32[]{:S(2)}) collective-permute-start(bf16[160,4096]{1,0:T(8,128)(2,1)} %get-tuple-element.44), channel_id=1, source_target_pairs={{152,0},{8,16},{16,8},{128,24},{24,128},{136,144},{144,136},{0,152... | collective-permute-start | bytes 3932168 | tf_op jit(solution)/shard_map/ppermute | solution.py:380
  109.4 18.0 %all-to-all-start.4 = ((bf16[16,16,512]{2,1,0:T(8,128)(2,1)}), bf16[16,16,512]{2,1,0:T(8,128)(2,1)S(1)}, u32[]{:S(2)}, u32[]{:S(2)}) async-start(bf16[16,16,512]{2,1,0:T(8,128)(2,1)} %broadcast_in_dim.11), calls=%async_computation.4 | async-start | bytes 524288 | tf_op jit(solution)/shard_map/all_to_all | solution.py:401
Sparse Core Ops, SparseCore 0:
  12.4 60.8 all-gather.1

commit v5 on v4

--- a/solution.py
+++ b/solution.py
@@ -225,24 +225,24 @@
     )(idx, tokens, *lows, grads)
 
 
-def block_kernel(own, core, there, across, weight, after, o0, o1, o2, o3, rows, held, made, sems):
+def block_kernel(first, second, weight, after, o0, o1, rows, held, made, sems):
     loads = [
-        pltpu.make_async_copy(weight.at[pl.ds(i * KEYS, KEYS), :], held.at[i], sems.at[4 * NZ + i]) for i in range(NZ)
+        pltpu.make_async_copy(weight.at[pl.ds(i * KEYS, KEYS), :], held.at[i], sems.at[2 * NZ + i]) for i in range(NZ)
     ]
     for load in loads:
         load.start()
-    for k, source in enumerate((own, core, there, across)):
-        rows[k * ROWS : (k + 1) * ROWS, :] = source[...]
+    rows[:ROWS, :] = first[...]
+    rows[ROWS:, :] = second[...]
     stores = []
     for i in range(NZ):
         loads[i].wait()
         made[i] = dot(rows[...], held[i], 1, 0).astype(BF)
-        for k, out in enumerate((o0, o1, o2, o3)):
+        for k, out in enumerate((o0, o1)):
             stores.append(
                 pltpu.make_async_copy(
                     made.at[i, pl.ds(k * ROWS, ROWS), :],
                     out.at[:, pl.ds(i * HALF, HALF)],
-                    sems.at[4 * i + k],
+                    sems.at[2 * i + k],
                 )
             )
             stores[-1].start()
@@ -254,14 +254,14 @@
     anywhere = pl.BlockSpec(memory_space=pl.ANY)
     return pl.pallas_call(
         block_kernel,
-        in_specs=[pl.BlockSpec(memory_space=pltpu.VMEM)] * 4 + [anywhere] * 2,
-        out_specs=[anywhere] * 4,
-        out_shape=[jax.ShapeDtypeStruct((ROWS, NZ * HALF), BF)] * 4,
+        in_specs=[pl.BlockSpec(memory_space=pltpu.VMEM)] * 2 + [anywhere] * 2,
+        out_specs=[anywhere] * 2,
+        out_shape=[jax.ShapeDtypeStruct((ROWS, NZ * HALF), BF)] * 2,
         scratch_shapes=[
-            pltpu.VMEM((4 * ROWS, KEYS), BF),
+            pltpu.VMEM((2 * ROWS, KEYS), BF),
             pltpu.VMEM((NZ, KEYS, HALF), BF),
-            pltpu.VMEM((NZ, 4 * ROWS, HALF), BF),
-            pltpu.SemaphoreType.DMA((5 * NZ,)),
+            pltpu.VMEM((NZ, 2 * ROWS, HALF), BF),
+            pltpu.SemaphoreType.DMA((3 * NZ,)),
         ],
         compiler_params=params(56),
         cost_estimate=BRIEF,
@@ -372,16 +372,17 @@
     ]
 
     up_total = up_part(idx, tokens, lows, grads)
-    parts = blocks(sources, weight, up_total)
+    away = blocks(sources[2:], weight, up_total)
+    here = blocks(sources[:2], weight, away[0])
     pieces = [
-        parts[0],
-        lax.ppermute(parts[1], "c", CORE),
-        lax.ppermute(parts[2], X_AXES, inverse(there)),
-        lax.ppermute(parts[3], X_AXES, inverse(across)),
+        here[0],
+        lax.ppermute(here[1], "c", CORE),
+        lax.ppermute(away[0], X_AXES, inverse(there)),
+        lax.ppermute(away[1], X_AXES, inverse(across)),
     ]
 
     up_total = lax.all_to_all(up_total, X_AXES, 0, 0, tiled=True)
-    parcels, up_total, _ = lax.optimization_barrier((parcels, up_total, parts[0]))
+    parcels, up_total, _ = lax.optimization_barrier((parcels, up_total, away[0]))
     up_total = jnp.sum(up_total.astype(F32), axis=0).reshape(4, RANK // 8, KEYS)
     total = own_half + parcels[0].astype(F32) + parcels[1].astype(F32) + parcels[2].astype(F32)
     total = jnp.concatenate([total.reshape(4, RANK // 8, WIDTH // 4), up_total], axis=2)
@@ -394,6 +395,7 @@
     slabs = total[:, : WIDTH // 4].reshape(RANK // 8, NZ, HALF).transpose(1, 0, 2)
     up_total = jnp.broadcast_to(total[None, :, WIDTH // 4 :], (NZ, RANK // 8, KEYS))
     slabs = jnp.concatenate([slabs, up_total], axis=1)
+    slabs, pieces[0] = lax.optimization_barrier((slabs, pieces[0]))
     slabs = lax.all_to_all(slabs, "z", 0, 0, tiled=True)
     slabs = jnp.sum(slabs.astype(F32), axis=0).astype(BF)
     slabs, pieces[2] = lax.optimization_barrier((slabs, pieces[2]))

time: 138 us -> 137 us (level); the launches traced: 136 us -> 136 us
  waiting for transfers between devices: 9.26 us -> 4.15 us
  Pallas kernels: 31.9 us -> 35.1 us
    ppermute x3, waiting for transfers between devices: 7.88 us -> 0.4 us  [the longest x1 0.39 us: on_device(): lax.ppermute(away[1], X_AXES, inverse(across))]
    pallas_call x1 -> x2, Pallas kernels: 7.46 us -> 11.4 us  [blocks(): pl.pallas_call(block_kernel, in_specs=[pl.BlockSpec(memory_space=pltpu.VM...]
    all_to_all x1, waiting for transfers between devices: 0.1 us -> 1.83 us  [on_device(): slabs = lax.all_to_all(slabs, DP_AXES, 0, 0, tiled=True).astype(F32)]
    unnamed x17 -> x19, local copies, waits for them, and re-layouts: 1.83 us -> 3.18 us
  transfers between devices with their start and end apart: 19 -> 19, of which waited for: 4 -> 4; matrix products, arithmetic and copies ran while one was open for 4% -> 4% of each run, Pallas kernels for 21% -> 24%
where the time goes in v5:
time: 137 us; the launch traced here: 136 us
  starting transfers between devices  37.8 us (28%)
  Pallas kernels  35.1 us (26%)
  blocking collectives  31.8 us (23%)
  between operations  14.3 us (10%)
  local copies, waits for them, and re-layouts  8.12 us (6%)
  other arithmetic  4.96 us (4%)
  waiting for transfers between devices  4.15 us (3%)
    all_to_all x1, blocking collectives, on_device(): everyone = lax.all_to_all(packet, SHARD_AXES, 0, 0, tiled=True)  19.8 us
    all_to_all x1, blocking collectives, on_device(): slabs = lax.all_to_all(slabs, 'z', 0, 0, tiled=True)  11.9 us
    pallas_call x2, Pallas kernels, blocks(): pl.pallas_call(block_kernel, in_specs=[pl.BlockSpec(memory_space=pltpu.VM...  11.4 us
    pallas_call x1, Pallas kernels, up_part(): pl.pallas_call(up_kernel, in_specs=[pl.BlockSpec(memory_space=pltpu.SMEM)...  6.74 us
    all_to_all x1, starting transfers between devices, on_device(): slabs = lax.all_to_all(slabs, DP_AXES, 0, 0, tiled=True).astype(F32)  6.59 us
    all_to_all x1, starting transfers between devices, on_device(): up_total = lax.all_to_all(up_total, X_AXES, 0, 0, tiled=True)  6.06 us
    pallas_call x1, Pallas kernels, down_part(): pl.pallas_call(down_kernel, in_specs=[pl.BlockSpec(memory_space=pltpu.SME...  5.6 us
    pallas_call x2, Pallas kernels, assemble(): pl.pallas_call(functools.partial(assemble_kernel, places), in_specs=[pl.B...  5.1 us
  transfers between devices with their start and end apart: 19, of which 4 were waited for; matrix products, arithmetic and copies ran while one was open for 4% of the time, Pallas kernels for 24%

profile of v5, /device:TPU:1, one launch (start us, length us, event | category | flops | bytes accessed | tf_op | source)
XLA Modules:
  0.0 136.3 jit_solution(279559345124920676)
XLA Ops:
  7.2 0.0 all-gather.2.cloned.1.call-start
  7.2 0.8 convert_bitcast_fusion
  8.0 0.6 pad.9.ids
  8.6 0.6 stack.23.idx
  9.2 3.1 %weight.1 = (bf16[512,512]{1,0:T(8,128)(2,1)}, bf16[16,80,128]{2,1,0:T(8,128)(2,1)}) custom-call(s32[5]{0:T(128)} %stack.23.idx, bf16[1024,512]{1,0:T(8,128)(2,1)} %levels.1, bf16[16,512]{1,0:T(8,128)(2,1)} %scales.1, f32[1,512]{1,0:T(1,128)} %second.1, bf16[64,1024]{1,0:T(8,128)(2,1)} %bitcast.63, bf16[64,512]{1,0:T(8,128)(2,1)} %up.4, ...), custom_call_target="tpu_custom_call" | custom-call | flops 1 | bytes 1 | tf_op jit(solution)/shard_map/weight/pallas_call | solution.py:61
  12.3 0.0 all-gather.2.cloned.1.call-update
  12.3 19.8 %all_to_all.25.everyone = bf16[16,80,128]{2,1,0:T(8,128)(2,1)S(1)} all-to-all(bf16[16,80,128]{2,1,0:T(8,128)(2,1)} %get-tuple-element.32), channel_id=1, replica_groups=mesh['xh'=2,'y'=4,'c'=2,'xl'=2,'z'=8] {'xl','z'}, dimensions={0} | all-to-all | bytes 655360 | tf_op jit(solution)/shard_map/all_to_all | solution.py:337
  32.2 1.2 broadcast_in_dim.9
  33.4 4.2 %all-to-all-start.1 = ((bf16[4,16,64,128]{3,2,1,0:T(8,128)(2,1)}), bf16[4,16,64,128]{3,2,1,0:T(8,128)(2,1)S(1)}, u32[]{:S(2)}, u32[]{:S(2)}) async-start(bf16[4,16,64,128]{3,2,1,0:T(8,128)(2,1)} %broadcast_in_dim.9), calls=%async_computation.1 | async-start | bytes 2097152 | tf_op jit(solution)/shard_map/all_to_all | solution.py:358
  37.6 0.8 copy.13.own
  38.3 0.7 maximum_bitcast_fusion.freqs
  39.0 3.2 %grads.1 = (bf16[160,512]{1,0:T(8,128)(2,1)}, bf16[64,160]{1,0:T(8,128)(2,1)}) custom-call(s32[5]{0:T(128)} %stack.23.idx, bf16[16,80,128]{2,1,0:T(8,128)(2,1)} %copy-done.3, f32[160,1]{1,0:T(8,128)} %copy.13.own, bf16[160,512]{1,0:T(8,128)(2,1)} %rotated.1, f32[1,128]{1,0:T(1,128)} %maximum_bitcast_fusion.freqs, bf16[64,512]{1,0:T(8,128)(2,1)} %up.4), custom_call_target="tpu_custom_call" | custom-call | flops 1 | bytes 1 | tf_op jit(solution)/shard_map/grads/pallas_call | solution.py:110
  42.2 5.6 %down.1 = (f32[64,4096]{1,0:T(8,128)}, f32[64,4096]{1,0:T(8,128)}, bf16[64,4096]{1,0:T(8,128)(2,1)}, bf16[64,4096]{1,0:T(8,128)(2,1)}) custom-call(s32[5]{0:T(128)} %stack.23.idx, bf16[64,160]{1,0:T(8,128)(2,1)} %get-tuple-element.33.low, bf16[160,16384]{1,0:T(8,128)(2,1)} %tokens.3), custom_call_target="tpu_custom_call" | custom-call | flops 1 | bytes 1 | tf_op jit(solution)/shard_map/down/pallas_call | solution.py:165
  47.8 4.9 %collective-permute-start = (bf16[64,4096]{1,0:T(8,128)(2,1)}, bf16[64,4096]{1,0:T(8,128)(2,1)S(1)}, u32[]{:S(2)}, u32[]{:S(2)}) collective-permute-start(bf16[64,4096]{1,0:T(8,128)(2,1)} %get-tuple-element.35), channel_id=1, source_target_pairs={{0,16},{16,0},{1,17},{17,1},{2,18},{18,2},{3,19},{19,3},{4,20},{20... | collective-permute-start | bytes 1572872 | tf_op jit(solution)/shard_map/ppermute | solution.py:355
  52.6 0.1 collective-permute-start.1
  52.7 0.4 collective-permute-start.2
  53.1 1.2 collective-permute-start.3
  54.4 1.3 collective-permute-start.4
  55.6 0.0 collective-permute-done
  55.6 0.0 collective-permute-done.1
  55.7 0.0 all-to-all-done.1.refs_0_
  55.7 0.0 copy-start.2
  55.7 0.8 collective-permute-start.5
  56.5 1.4 %convert_add_fusion.1 = f32[64,4096]{1,0:T(8,128)S(1)} fusion(f32[64,4096]{1,0:T(8,128)} %get-tuple-element.34, bf16[64,4096]{1,0:T(8,128)(2,1)S(1)} %collective-permute-done), kind=kLoop, calls=%fused_computation.5 | loop fusion | flops 524288 | bytes 2621440 | tf_op jit(solution)/shard_map/add | solution.py:362
  57.9 0.1 copy-done.5
  58.1 0.1 convert_add_fusion
  58.3 1.2 collective-permute-done.4.second
  59.5 2.5 %collective-permute-start.7 = (bf16[32,4096]{1,0:T(8,128)(2,1)S(1)}, bf16[32,4096]{1,0:T(8,128)(2,1)S(1)}, u32[]{:S(2)}, u32[]{:S(2)}) collective-permute-start(bf16[32,4096]{1,0:T(8,128)(2,1)S(1)} %fusion.3), channel_id=1, source_target_pairs={{0,128},{8,136},{128,0},{136,8},{1,129},{9,137},{129,1},{137,9},{2... | collective-permute-start | bytes 786440 | tf_op jit(solution)/shard_map/ppermute | solution.py:370
  62.0 0.9 collective-permute-start.8
  62.9 0.0 collective-permute-start.9
  62.9 0.0 collective-permute-done.5.refs_1_
  62.9 1.0 copy-done.4
  63.9 6.7 %up.5.after = bf16[8,64,256]{2,1,0:T(8,128)(2,1)} custom-call(s32[5]{0:T(128)} %stack.23.idx, bf16[160,16384]{1,0:T(8,128)(2,1)} %tokens.3, bf16[4,16,64,128]{3,2,1,0:T(8,128)(2,1)} %copy-done.2, bf16[4,16,64,128]{3,2,1,0:T(8,128)(2,1)} %copy-done.4, bf16[160,512]{1,0:T(8,128)(2,1)} %get-tuple-element.40.refs_2_.first), custom_call_target="tpu_custom_call" | custom-call | flops 1 | bytes 1 | tf_op jit(solution)/shard_map/up/pallas_call | solution.py:210
  70.7 6.1 %all-to-all-start.2 = ((bf16[8,64,256]{2,1,0:T(8,128)(2,1)}), bf16[8,64,256]{2,1,0:T(8,128)(2,1)S(1)}, u32[]{:S(2)}, u32[]{:S(2)}) async-start(bf16[8,64,256]{2,1,0:T(8,128)(2,1)} %up.5.after), calls=%async_computation.2 | async-start | bytes 524288 | tf_op jit(solution)/shard_map/all_to_all | solution.py:384
  76.7 5.7 %blocks.2 = (bf16[160,4096]{1,0:T(8,128)(2,1)}, bf16[160,4096]{1,0:T(8,128)(2,1)}) custom-call(bf16[160,512]{1,0:T(8,128)(2,1)} %collective-permute-done.3.first, bf16[160,512]{1,0:T(8,128)(2,1)} %collective-permute-done.4.second, bf16[4096,512]{1,0:T(8,128)(2,1)} %all-gather.2.cloned.1.call-done.weight, bf16[8,64,256]{2,1,0:T(8,128)(2,1)} %up.5.after), custom_call_target="tpu_custom_call" | custom-call | flops 1 | bytes 1 | tf_op jit(solution)/shard_map/blocks/pallas_call | solution.py:255
  82.5 0.0 collective-permute-done.7
  82.5 0.0 collective-permute-done.9
  82.5 0.6 all-to-all-done.2
  83.2 0.0 copy-done.7
  83.2 1.1 fusion.2
  84.4 0.7 fusion.19
  85.1 3.3 %collective-permute-start.12 = (bf16[8,4608]{1,0:T(8,128)(2,1)}, bf16[8,4608]{1,0:T(8,128)(2,1)S(1)}, u32[]{:S(2)}, u32[]{:S(2)}) collective-permute-start(bf16[8,4608]{1,0:T(8,128)(2,1)} %get-tuple-element.63), channel_id=1, source_target_pairs={{0,64},{32,96},{64,0},{96,32},{1,65},{33,97},{65,1},{97,33},{2,66}... | collective-permute-start | bytes 221192 | tf_op jit(solution)/shard_map/ppermute | solution.py:392
  88.3 0.9 collective-permute-start.11
  89.2 0.6 collective-permute-start.10
  89.8 1.4 %collective-permute-start.14 = (bf16[160,4096]{1,0:T(8,128)(2,1)}, bf16[160,4096]{1,0:T(8,128)(2,1)S(1)}, u32[]{:S(2)}, u32[]{:S(2)}) collective-permute-start(bf16[160,4096]{1,0:T(8,128)(2,1)} %get-tuple-element.49.after), channel_id=1, source_target_pairs={{8,0},{152,16},{128,8},{16,24},{136,128},{24,144},{0,136},{144,152... | collective-permute-start | bytes 3932168 | tf_op jit(solution)/shard_map/ppermute | solution.py:380
  91.2 2.2 %collective-permute-start.6 = (bf16[160,4096]{1,0:T(8,128)(2,1)}, bf16[160,4096]{1,0:T(8,128)(2,1)S(1)}, u32[]{:S(2)}, u32[]{:S(2)}) collective-permute-start(bf16[160,4096]{1,0:T(8,128)(2,1)} %get-tuple-element.45), channel_id=1, source_target_pairs={{152,0},{8,16},{16,8},{128,24},{24,128},{136,144},{144,136},{0,152... | collective-permute-start | bytes 3932168 | tf_op jit(solution)/shard_map/ppermute | solution.py:381
  93.4 5.7 %blocks.3 = (bf16[160,4096]{1,0:T(8,128)(2,1)}, bf16[160,4096]{1,0:T(8,128)(2,1)}) custom-call(bf16[160,512]{1,0:T(8,128)(2,1)} %get-tuple-element.40.refs_2_.first, bf16[160,512]{1,0:T(8,128)(2,1)} %copy-done.8, bf16[4096,512]{1,0:T(8,128)(2,1)} %all-gather.2.cloned.1.call-done.weight, bf16[160,4096]{1,0:T(8,128)(2,1)} %get-tuple-element.49.after), custom_call_target="tpu_custom_call" | custom-call | flops 1 | bytes 1 | tf_op jit(solution)/shard_map/blocks/pallas_call | solution.py:255
  99.2 0.0 collective-permute-done.12
  99.2 0.6 collective-permute-start.13
  99.8 0.0 collective-permute-done.11
  99.9 11.9 %all_to_all.26 = bf16[8,16,512]{2,1,0:T(8,128)(2,1)S(1)} all-to-all(bf16[8,16,512]{2,1,0:T(8,128)(2,1)S(1)} %pad_maximum_fusion), channel_id=1, replica_groups=mesh['xh'=2,'y'=4,'c'=2,'xl'=2,'z'=8] {'z'}, dimensions={0} | all-to-all | bytes 262144 | tf_op jit(solution)/shard_map/all_to_all | solution.py:399
  111.8 0.0 collective-permute-done.14.refs_2_
  111.9 0.7 broadcast_in_dim.11
  112.6 6.6 %all-to-all-start.4 = ((bf16[16,16,512]{2,1,0:T(8,128)(2,1)}), bf16[16,16,512]{2,1,0:T(8,128)(2,1)S(1)}, u32[]{:S(2)}, u32[]{:S(2)}) async-start(bf16[16,16,512]{2,1,0:T(8,128)(2,1)} %broadcast_in_dim.11), calls=%async_computation.4 | async-start | bytes 524288 | tf_op jit(solution)/shard_map/all_to_all | solution.py:403
  119.2 0.0 collective-permute-done.13.refs_1_
  119.2 1.3 copy-done
  120.5 3.4 %assemble.2.refs_1_ = bf16[160,16384]{1,0:T(8,128)(2,1)} custom-call(s32[5]{0:T(128)S(1)} %copy-done.1, bf16[160,4096]{1,0:T(8,128)(2,1)S(1)} %copy-done, bf16[160,4096]{1,0:T(8,128)(2,1)} %collective-permute-done.13.refs_1_, bf16[160,4096]{1,0:T(8,128)(2,1)S(1)} %collective-permute-done.14.refs_2_), custom_call_target="tpu_custom_call" | custom-call | flops 1 | bytes 1 | tf_op jit(solution)/shard_map/assemble/pallas_call | solution.py:295
  124.0 0.4 collective-permute-done.6.refs_0_
  124.3 1.7 %assemble.3 = bf16[160,16384]{1,0:T(8,128)(2,1)} custom-call(s32[5]{0:T(128)S(1)} %copy-done.1, bf16[160,4096]{1,0:T(8,128)(2,1)S(1)} %collective-permute-done.6.refs_0_, bf16[160,16384]{1,0:T(8,128)(2,1)} %assemble.2.refs_1_), custom_call_target="tpu_custom_call", output_to_operand_aliasing={{}: (2, {})} | custom-call | flops 1 | bytes 1 | tf_op jit(solution)/shard_map/assemble/pallas_call | solution.py:295
  126.0 1.8 %all-to-all-done.4 = bf16[16,16,512]{2,1,0:T(8,128)(2,1)S(1)} async-done(((bf16[16,16,512]{2,1,0:T(8,128)(2,1)}), bf16[16,16,512]{2,1,0:T(8,128)(2,1)S(1)}, u32[]{:S(2)}, u32[]{:S(2)}) %all-to-all-start.4) | async-done | bytes 262176 | tf_op jit(solution)/shard_map/all_to_all | solution.py:403
  127.8 0.1 convert_multiply_fusion
  127.9 0.7 slice.23
  128.7 0.1 copy.14
  128.8 0.7 copy.15
  (33 shorter events, 0.3 us)
Async XLA Ops:
  7.2 69.6 %all-gather.2.cloned.1.call-start = ((), (), s32[]{:S(2)}) async-start(), calls=%async_computation.5 | async-start | bytes 4718592 | tf_op jit(solution)/shard_map/all_gather | solution.py:336
  32.2 1.3 copy-start.3
  33.4 22.2 %all-to-all-start.1 = ((bf16[4,16,64,128]{3,2,1,0:T(8,128)(2,1)}), bf16[4,16,64,128]{3,2,1,0:T(8,128)(2,1)S(1)}, u32[]{:S(2)}, u32[]{:S(2)}) async-start(bf16[4,16,64,128]{3,2,1,0:T(8,128)(2,1)} %broadcast_in_dim.9), calls=%async_computation.1 | async-start | bytes 2097152 | tf_op jit(solution)/shard_map/all_to_all | solution.py:358
  42.2 10.6 %copy-start.6 = (bf16[160,512]{1,0:T(8,128)(2,1)S(1)}, bf16[160,512]{1,0:T(8,128)(2,1)}, u32[]{:S(2)}) copy-start(bf16[160,512]{1,0:T(8,128)(2,1)} %get-tuple-element.40.refs_2_.first) | copy-start | bytes 491524
  47.8 7.9 %collective-permute-start = (bf16[64,4096]{1,0:T(8,128)(2,1)}, bf16[64,4096]{1,0:T(8,128)(2,1)S(1)}, u32[]{:S(2)}, u32[]{:S(2)}) collective-permute-start(bf16[64,4096]{1,0:T(8,128)(2,1)} %get-tuple-element.35), channel_id=1, source_target_pairs={{0,16},{16,0},{1,17},{17,1},{2,18},{18,2},{3,19},{19,3},{4,20},{20... | collective-permute-start | bytes 1572872 | tf_op jit(solution)/shard_map/ppermute | solution.py:355
  52.6 3.0 %collective-permute-start.1 = (bf16[64,4096]{1,0:T(8,128)(2,1)}, bf16[64,4096]{1,0:T(8,128)(2,1)S(1)}, u32[]{:S(2)}, u32[]{:S(2)}) collective-permute-start(bf16[64,4096]{1,0:T(8,128)(2,1)} %get-tuple-element.36), channel_id=1, source_target_pairs={{0,16},{16,0},{1,17},{17,1},{2,18},{18,2},{3,19},{19,3},{4,20},{20... | collective-permute-start | bytes 1572872 | tf_op jit(solution)/shard_map/ppermute | solution.py:355
  52.7 5.5 %collective-permute-start.2 = (bf16[160,512]{1,0:T(8,128)(2,1)S(1)}, bf16[160,512]{1,0:T(8,128)(2,1)S(1)}, u32[]{:S(2)}, u32[]{:S(2)}) collective-permute-start(bf16[160,512]{1,0:T(8,128)(2,1)S(1)} %copy-done.6), channel_id=1, source_target_pairs={{0,16},{16,0},{1,17},{17,1},{2,18},{18,2},{3,19},{19,3},{4,20},{20... | collective-permute-start | bytes 491528 | tf_op jit(solution)/shard_map/ppermute | solution.py:348
  53.1 5.1 %collective-permute-start.3 = (bf16[160,512]{1,0:T(8,128)(2,1)S(1)}, bf16[160,512]{1,0:T(8,128)(2,1)}, u32[]{:S(2)}, u32[]{:S(2)}) collective-permute-start(bf16[160,512]{1,0:T(8,128)(2,1)S(1)} %copy-done.6), channel_id=1, source_target_pairs={{0,8},{16,152},{8,128},{24,16},{128,136},{144,24},{136,0},{152,144... | collective-permute-start | bytes 491528 | tf_op jit(solution)/shard_map/ppermute | solution.py:349
  54.4 5.1 %collective-permute-start.4 = (bf16[160,512]{1,0:T(8,128)(2,1)S(1)}, bf16[160,512]{1,0:T(8,128)(2,1)}, u32[]{:S(2)}, u32[]{:S(2)}) collective-permute-start(bf16[160,512]{1,0:T(8,128)(2,1)S(1)} %copy-done.6), channel_id=1, source_target_pairs={{0,152},{16,8},{8,16},{24,128},{128,24},{144,136},{136,144},{152,0... | collective-permute-start | bytes 491528 | tf_op jit(solution)/shard_map/ppermute | solution.py:350
  55.7 2.3 %copy-start.2 = (bf16[4,16,64,128]{3,2,1,0:T(8,128)(2,1)}, bf16[4,16,64,128]{3,2,1,0:T(8,128)(2,1)S(1)}, u32[]{:S(2)}) copy-start(bf16[4,16,64,128]{3,2,1,0:T(8,128)(2,1)S(1)} %all-to-all-done.1.refs_0_) | copy-start | bytes 3145732
  55.7 7.3 %collective-permute-start.5 = (bf16[4,16,64,128]{3,2,1,0:T(8,128)(2,1)S(1)}, bf16[4,16,64,128]{3,2,1,0:T(8,128)(2,1)S(1)}, u32[]{:S(2)}, u32[]{:S(2)}) collective-permute-start(bf16[4,16,64,128]{3,2,1,0:T(8,128)(2,1)S(1)} %all-to-all-done.1.refs_0_), channel_id=1, source_target_pairs={{0,16},{16,0},{1,17},{17,1},{2,18},{18,2},{3,19},{19,3},{4,20},{20... | collective-permute-start | bytes 3145736 | tf_op jit(solution)/shard_map/ppermute | solution.py:360
  56.5 1.6 %copy-start.5 = (f32[64,4096]{1,0:T(8,128)S(1)}, f32[64,4096]{1,0:T(8,128)}, u32[]{:S(2)}) copy-start(f32[64,4096]{1,0:T(8,128)} %get-tuple-element.38) | copy-start | bytes 3145732
  58.3 1.3 copy-start.8
  59.5 22.9 %collective-permute-start.7 = (bf16[32,4096]{1,0:T(8,128)(2,1)S(1)}, bf16[32,4096]{1,0:T(8,128)(2,1)S(1)}, u32[]{:S(2)}, u32[]{:S(2)}) collective-permute-start(bf16[32,4096]{1,0:T(8,128)(2,1)S(1)} %fusion.3), channel_id=1, source_target_pairs={{0,128},{8,136},{128,0},{136,8},{1,129},{9,137},{129,1},{137,9},{2... | collective-permute-start | bytes 786440 | tf_op jit(solution)/shard_map/ppermute | solution.py:370
  62.0 20.4 %collective-permute-start.8 = (bf16[32,4096]{1,0:T(8,128)(2,1)S(1)}, bf16[32,4096]{1,0:T(8,128)(2,1)S(1)}, u32[]{:S(2)}, u32[]{:S(2)}) collective-permute-start(bf16[32,4096]{1,0:T(8,128)(2,1)S(1)} %get-tuple-element.47), channel_id=1, source_target_pairs={{0,8},{8,0},{128,136},{136,128},{1,9},{9,1},{129,137},{137,129},{2... | collective-permute-start | bytes 786440 | tf_op jit(solution)/shard_map/ppermute | solution.py:370
  62.9 19.6 %collective-permute-start.9 = (bf16[32,4096]{1,0:T(8,128)(2,1)S(1)}, bf16[32,4096]{1,0:T(8,128)(2,1)}, u32[]{:S(2)}, u32[]{:S(2)}) collective-permute-start(bf16[32,4096]{1,0:T(8,128)(2,1)S(1)} %get-tuple-element.48), channel_id=1, source_target_pairs={{0,136},{8,128},{128,8},{136,0},{1,137},{9,129},{129,9},{137,1},{2... | collective-permute-start | bytes 786440 | tf_op jit(solution)/shard_map/ppermute | solution.py:370
  62.9 1.0 copy-start.4
  70.7 12.4 %all-to-all-start.2 = ((bf16[8,64,256]{2,1,0:T(8,128)(2,1)}), bf16[8,64,256]{2,1,0:T(8,128)(2,1)S(1)}, u32[]{:S(2)}, u32[]{:S(2)}) async-start(bf16[8,64,256]{2,1,0:T(8,128)(2,1)} %up.5.after), calls=%async_computation.2 | async-start | bytes 524288 | tf_op jit(solution)/shard_map/all_to_all | solution.py:384
  82.5 0.7 copy-start.7
  85.1 14.1 %collective-permute-start.12 = (bf16[8,4608]{1,0:T(8,128)(2,1)}, bf16[8,4608]{1,0:T(8,128)(2,1)S(1)}, u32[]{:S(2)}, u32[]{:S(2)}) collective-permute-start(bf16[8,4608]{1,0:T(8,128)(2,1)} %get-tuple-element.63), channel_id=1, source_target_pairs={{0,64},{32,96},{64,0},{96,32},{1,65},{33,97},{65,1},{97,33},{2,66}... | collective-permute-start | bytes 221192 | tf_op jit(solution)/shard_map/ppermute | solution.py:392
  88.3 11.4 %collective-permute-start.11 = (bf16[8,4608]{1,0:T(8,128)(2,1)}, bf16[8,4608]{1,0:T(8,128)(2,1)S(1)}, u32[]{:S(2)}, u32[]{:S(2)}) collective-permute-start(bf16[8,4608]{1,0:T(8,128)(2,1)} %get-tuple-element.62), channel_id=1, source_target_pairs={{0,96},{32,0},{64,32},{96,64},{1,97},{33,1},{65,33},{97,65},{2,98}... | collective-permute-start | bytes 221192 | tf_op jit(solution)/shard_map/ppermute | solution.py:392
  89.2 10.6 %collective-permute-start.10 = (bf16[8,4608]{1,0:T(8,128)(2,1)S(1)}, bf16[8,4608]{1,0:T(8,128)(2,1)S(1)}, u32[]{:S(2)}, u32[]{:S(2)}) collective-permute-start(bf16[8,4608]{1,0:T(8,128)(2,1)S(1)} %get-tuple-element.61), channel_id=1, source_target_pairs={{0,32},{32,64},{64,96},{96,0},{1,33},{33,65},{65,97},{97,1},{2,34}... | collective-permute-start | bytes 221192 | tf_op jit(solution)/shard_map/ppermute | solution.py:392
  89.8 22.0 %collective-permute-start.14 = (bf16[160,4096]{1,0:T(8,128)(2,1)}, bf16[160,4096]{1,0:T(8,128)(2,1)S(1)}, u32[]{:S(2)}, u32[]{:S(2)}) collective-permute-start(bf16[160,4096]{1,0:T(8,128)(2,1)} %get-tuple-element.49.after), channel_id=1, source_target_pairs={{8,0},{152,16},{128,8},{16,24},{136,128},{24,144},{0,136},{144,152... | collective-permute-start | bytes 3932168 | tf_op jit(solution)/shard_map/ppermute | solution.py:380
  91.2 33.2 %collective-permute-start.6 = (bf16[160,4096]{1,0:T(8,128)(2,1)}, bf16[160,4096]{1,0:T(8,128)(2,1)S(1)}, u32[]{:S(2)}, u32[]{:S(2)}) collective-permute-start(bf16[160,4096]{1,0:T(8,128)(2,1)} %get-tuple-element.45), channel_id=1, source_target_pairs={{152,0},{8,16},{16,8},{128,24},{24,128},{136,144},{144,136},{0,152... | collective-permute-start | bytes 3932168 | tf_op jit(solution)/shard_map/ppermute | solution.py:381
  99.2 20.0 %copy-start.1 = (s32[5]{0:T(128)S(1)}, s32[5]{0:T(128)}, u32[]{:S(2)}) copy-start(s32[5]{0:T(128)} %stack.23.idx) | copy-start | bytes 64
  99.2 20.0 %collective-permute-start.13 = (bf16[160,4096]{1,0:T(8,128)(2,1)}, bf16[160,4096]{1,0:T(8,128)(2,1)}, u32[]{:S(2)}, u32[]{:S(2)}) collective-permute-start(bf16[160,4096]{1,0:T(8,128)(2,1)} %get-tuple-element.57), channel_id=1, source_target_pairs={{0,16},{16,0},{1,17},{17,1},{2,18},{18,2},{3,19},{19,3},{4,20},{20... | collective-permute-start | bytes 3932168 | tf_op jit(solution)/shard_map/ppermute | solution.py:379
  112.6 15.3 %all-to-all-start.4 = ((bf16[16,16,512]{2,1,0:T(8,128)(2,1)}), bf16[16,16,512]{2,1,0:T(8,128)(2,1)S(1)}, u32[]{:S(2)}, u32[]{:S(2)}) async-start(bf16[16,16,512]{2,1,0:T(8,128)(2,1)} %broadcast_in_dim.11), calls=%async_computation.4 | async-start | bytes 524288 | tf_op jit(solution)/shard_map/all_to_all | solution.py:403
  119.2 1.3 copy-start
Sparse Core Ops, SparseCore 0:
  12.4 60.8 all-gather.1

commit v6 on v5

--- a/solution.py
+++ b/solution.py
@@ -42,9 +42,11 @@
 
 
 def weight_kernel(idx, levels, scales, second, down, up, eighth, ids, weight, packet):
+    row = lax.broadcasted_iota(jnp.int32, (IDS, LANES), 0)
+    table = jnp.where(row == 0, ids[:, :LANES], ids[:, LANES:]).astype(F32).astype(BF)
     for k in range(SHARDS):
         packet[k, :RANK, :] = eighth[...]
-        packet[k, RANK:, :] = ids[...]
+        packet[k, RANK:, :] = table
     scale = scales[...].astype(F32)
     n = HALF // BLOCK
     scale = jnp.where(idx[0] == 0, scale[:n], scale[n:])
@@ -70,7 +72,7 @@
                 pl.BlockSpec((RANK, HALF), lambda i, s: (0, s[0])),
                 full((RANK, KEYS)),
                 pl.BlockSpec((RANK, LANES), lambda i, s: (0, s[0] * 4 + s[4])),
-                full((IDS, LANES)),
+                full((1, 2 * LANES)),
             ],
             out_specs=[full((KEYS, HALF)), full((SHARDS, RANK + IDS, LANES))],
         ),
@@ -330,8 +332,7 @@
     xh, y, c, xl, z = (lax.axis_index(a) for a in ("xh", "y", "c", "xl", "z"))
     idx = jnp.stack([c, xh, xl, xl * NZ + z, y]).astype(jnp.int32)
 
-    ids = jnp.pad(documents.astype(BF), ((0, 0), (0, 2 * LANES - ROWS)), constant_values=1000.0)
-    ids = jnp.pad(ids.reshape(2, LANES), ((0, IDS - 2), (0, 0)))
+    ids = jnp.pad(documents, ((0, 0), (0, 2 * LANES - ROWS)), constant_values=1000)
     weight, packet = local_weight(idx, levels, scales, second, down.T, up, ids)
     weight = lax.all_gather(weight, "z", tiled=True)
     everyone = lax.all_to_all(packet, SHARD_AXES, 0, 0, tiled=True)

time: 137 us -> 137 us (level)
    unnamed x19 -> x21, local copies, waits for them, and re-layouts: 3.18 us -> 3.17 us
where the time goes in v6:
time: 137 us; the launch traced here: 136 us
  starting transfers between devices  38 us (28%)
  Pallas kernels  35.1 us (26%)
  blocking collectives  31.8 us (23%)
  between operations  14.3 us (10%)
  local copies, waits for them, and re-layouts  8.81 us (6%)
  waiting for transfers between devices  4.19 us (3%)
  other arithmetic  4.14 us (3%)
    all_to_all x1, blocking collectives, on_device(): everyone = lax.all_to_all(packet, SHARD_AXES, 0, 0, tiled=True)  19.8 us
    all_to_all x1, blocking collectives, on_device(): slabs = lax.all_to_all(slabs, 'z', 0, 0, tiled=True)  11.9 us
    pallas_call x2, Pallas kernels, blocks(): pl.pallas_call(block_kernel, in_specs=[pl.BlockSpec(memory_space=pltpu.VM...  11.5 us
    pallas_call x1, Pallas kernels, up_part(): pl.pallas_call(up_kernel, in_specs=[pl.BlockSpec(memory_space=pltpu.SMEM)...  6.73 us
    all_to_all x1, starting transfers between devices, on_device(): slabs = lax.all_to_all(slabs, DP_AXES, 0, 0, tiled=True).astype(F32)  6.62 us
    all_to_all x1, starting transfers between devices, on_device(): up_total = lax.all_to_all(up_total, X_AXES, 0, 0, tiled=True)  6.08 us
    pallas_call x1, Pallas kernels, down_part(): pl.pallas_call(down_kernel, in_specs=[pl.BlockSpec(memory_space=pltpu.SME...  5.6 us
    pallas_call x2, Pallas kernels, assemble(): pl.pallas_call(functools.partial(assemble_kernel, places), in_specs=[pl.B...  5.1 us
  transfers between devices with their start and end apart: 19, of which 4 were waited for; matrix products, arithmetic and copies ran while one was open for 4% of the time, Pallas kernels for 24%

profile of v6, /device:TPU:1, one launch (start us, length us, event | category | flops | bytes accessed | tf_op | source)
XLA Modules:
  0.0 136.3 jit_solution(16348108322565492556)
XLA Ops:
  7.2 0.0 all-gather.2.cloned.1.call-start
  7.2 1.2 pad.4.ids
  8.5 0.7 stack.23.idx
  9.1 3.1 %weight.1 = (bf16[512,512]{1,0:T(8,128)(2,1)}, bf16[16,80,128]{2,1,0:T(8,128)(2,1)}) custom-call(s32[5]{0:T(128)} %stack.23.idx, bf16[1024,512]{1,0:T(8,128)(2,1)} %levels.1, bf16[16,512]{1,0:T(8,128)(2,1)} %scales.1, f32[1,512]{1,0:T(1,128)} %second.1, bf16[64,1024]{1,0:T(8,128)(2,1)} %bitcast.62, bf16[64,512]{1,0:T(8,128)(2,1)} %up.4, ...), custom_call_target="tpu_custom_call" | custom-call | flops 1 | bytes 1 | tf_op jit(solution)/shard_map/weight/pallas_call | solution.py:63
  12.2 0.0 all-gather.2.cloned.1.call-update
  12.2 19.8 %all_to_all.25.everyone = bf16[16,80,128]{2,1,0:T(8,128)(2,1)S(1)} all-to-all(bf16[16,80,128]{2,1,0:T(8,128)(2,1)} %get-tuple-element.32), channel_id=1, replica_groups=mesh['xh'=2,'y'=4,'c'=2,'xl'=2,'z'=8] {'xl','z'}, dimensions={0} | all-to-all | bytes 655360 | tf_op jit(solution)/shard_map/all_to_all | solution.py:338
  32.1 1.2 broadcast_in_dim.9
  33.3 4.3 %all-to-all-start.1 = ((bf16[4,16,64,128]{3,2,1,0:T(8,128)(2,1)}), bf16[4,16,64,128]{3,2,1,0:T(8,128)(2,1)S(1)}, u32[]{:S(2)}, u32[]{:S(2)}) async-start(bf16[4,16,64,128]{3,2,1,0:T(8,128)(2,1)} %broadcast_in_dim.9), calls=%async_computation.1 | async-start | bytes 2097152 | tf_op jit(solution)/shard_map/all_to_all | solution.py:359
  37.6 0.8 copy.13.own
  38.4 0.6 maximum_bitcast_fusion.freqs
  39.0 3.2 %grads.1 = (bf16[160,512]{1,0:T(8,128)(2,1)}, bf16[64,160]{1,0:T(8,128)(2,1)}) custom-call(s32[5]{0:T(128)} %stack.23.idx, bf16[16,80,128]{2,1,0:T(8,128)(2,1)} %copy-done.3, f32[160,1]{1,0:T(8,128)} %copy.13.own, bf16[160,512]{1,0:T(8,128)(2,1)} %rotated.1, f32[1,128]{1,0:T(1,128)} %maximum_bitcast_fusion.freqs, bf16[64,512]{1,0:T(8,128)(2,1)} %up.4), custom_call_target="tpu_custom_call" | custom-call | flops 1 | bytes 1 | tf_op jit(solution)/shard_map/grads/pallas_call | solution.py:112
  42.2 5.6 %down.1 = (f32[64,4096]{1,0:T(8,128)}, f32[64,4096]{1,0:T(8,128)}, bf16[64,4096]{1,0:T(8,128)(2,1)}, bf16[64,4096]{1,0:T(8,128)(2,1)}) custom-call(s32[5]{0:T(128)} %stack.23.idx, bf16[64,160]{1,0:T(8,128)(2,1)} %get-tuple-element.33.low, bf16[160,16384]{1,0:T(8,128)(2,1)} %tokens.3), custom_call_target="tpu_custom_call" | custom-call | flops 1 | bytes 1 | tf_op jit(solution)/shard_map/down/pallas_call | solution.py:167
  47.8 4.9 %collective-permute-start = (bf16[64,4096]{1,0:T(8,128)(2,1)}, bf16[64,4096]{1,0:T(8,128)(2,1)S(1)}, u32[]{:S(2)}, u32[]{:S(2)}) collective-permute-start(bf16[64,4096]{1,0:T(8,128)(2,1)} %get-tuple-element.35), channel_id=1, source_target_pairs={{0,16},{16,0},{1,17},{17,1},{2,18},{18,2},{3,19},{19,3},{4,20},{20... | collective-permute-start | bytes 1572872 | tf_op jit(solution)/shard_map/ppermute | solution.py:356
  52.6 0.1 collective-permute-start.1
  52.7 0.4 collective-permute-start.2
  53.2 1.2 collective-permute-start.3
  54.4 1.3 collective-permute-start.4
  55.6 0.0 collective-permute-done
  55.7 0.0 collective-permute-done.1
  55.7 0.0 all-to-all-done.1.refs_0_
  55.7 0.0 copy-start.2
  55.7 0.8 collective-permute-start.5
  56.5 1.4 %convert_add_fusion.1 = f32[64,4096]{1,0:T(8,128)S(1)} fusion(f32[64,4096]{1,0:T(8,128)} %get-tuple-element.34, bf16[64,4096]{1,0:T(8,128)(2,1)S(1)} %collective-permute-done), kind=kLoop, calls=%fused_computation.5 | loop fusion | flops 524288 | bytes 2621440 | tf_op jit(solution)/shard_map/add | solution.py:363
  57.9 0.1 copy-done.5
  58.1 0.1 convert_add_fusion
  58.3 0.0 collective-permute-done.2.second
  58.3 0.0 collective-permute-done.3.first
  58.3 1.3 collective-permute-done.4.second
  59.5 2.5 %collective-permute-start.7 = (bf16[32,4096]{1,0:T(8,128)(2,1)S(1)}, bf16[32,4096]{1,0:T(8,128)(2,1)S(1)}, u32[]{:S(2)}, u32[]{:S(2)}) collective-permute-start(bf16[32,4096]{1,0:T(8,128)(2,1)S(1)} %fusion.3), channel_id=1, source_target_pairs={{0,128},{8,136},{128,0},{136,8},{1,129},{9,137},{129,1},{137,9},{2... | collective-permute-start | bytes 786440 | tf_op jit(solution)/shard_map/ppermute | solution.py:371
  62.0 0.9 collective-permute-start.8
  62.9 0.0 collective-permute-start.9
  62.9 0.0 collective-permute-done.5.refs_1_
  62.9 1.0 copy-done.4
  64.0 6.7 %up.5.after = bf16[8,64,256]{2,1,0:T(8,128)(2,1)} custom-call(s32[5]{0:T(128)} %stack.23.idx, bf16[160,16384]{1,0:T(8,128)(2,1)} %tokens.3, bf16[4,16,64,128]{3,2,1,0:T(8,128)(2,1)} %copy-done.2, bf16[4,16,64,128]{3,2,1,0:T(8,128)(2,1)} %copy-done.4, bf16[160,512]{1,0:T(8,128)(2,1)} %get-tuple-element.40.refs_2_.first), custom_call_target="tpu_custom_call" | custom-call | flops 1 | bytes 1 | tf_op jit(solution)/shard_map/up/pallas_call | solution.py:212
  70.7 6.1 %all-to-all-start.2 = ((bf16[8,64,256]{2,1,0:T(8,128)(2,1)}), bf16[8,64,256]{2,1,0:T(8,128)(2,1)S(1)}, u32[]{:S(2)}, u32[]{:S(2)}) async-start(bf16[8,64,256]{2,1,0:T(8,128)(2,1)} %up.5.after), calls=%async_computation.2 | async-start | bytes 524288 | tf_op jit(solution)/shard_map/all_to_all | solution.py:385
  76.8 5.7 %blocks.2 = (bf16[160,4096]{1,0:T(8,128)(2,1)}, bf16[160,4096]{1,0:T(8,128)(2,1)}) custom-call(bf16[160,512]{1,0:T(8,128)(2,1)} %collective-permute-done.3.first, bf16[160,512]{1,0:T(8,128)(2,1)} %collective-permute-done.4.second, bf16[4096,512]{1,0:T(8,128)(2,1)} %all-gather.2.cloned.1.call-done.weight, bf16[8,64,256]{2,1,0:T(8,128)(2,1)} %up.5.after), custom_call_target="tpu_custom_call" | custom-call | flops 1 | bytes 1 | tf_op jit(solution)/shard_map/blocks/pallas_call | solution.py:257
  82.5 0.0 collective-permute-done.8
  82.5 0.0 collective-permute-done.9
  82.5 0.7 all-to-all-done.2
  83.2 1.1 fusion.2
  84.4 0.7 fusion.19
  85.1 3.3 %collective-permute-start.12 = (bf16[8,4608]{1,0:T(8,128)(2,1)}, bf16[8,4608]{1,0:T(8,128)(2,1)S(1)}, u32[]{:S(2)}, u32[]{:S(2)}) collective-permute-start(bf16[8,4608]{1,0:T(8,128)(2,1)} %get-tuple-element.63), channel_id=1, source_target_pairs={{0,64},{32,96},{64,0},{96,32},{1,65},{33,97},{65,1},{97,33},{2,66}... | collective-permute-start | bytes 221192 | tf_op jit(solution)/shard_map/ppermute | solution.py:393
  88.3 0.9 collective-permute-start.11
  89.2 0.6 collective-permute-start.10
  89.8 1.4 collective-permute-start.14
  91.2 2.3 %collective-permute-start.6 = (bf16[160,4096]{1,0:T(8,128)(2,1)}, bf16[160,4096]{1,0:T(8,128)(2,1)S(1)}, u32[]{:S(2)}, u32[]{:S(2)}) collective-permute-start(bf16[160,4096]{1,0:T(8,128)(2,1)} %get-tuple-element.45), channel_id=1, source_target_pairs={{152,0},{8,16},{16,8},{128,24},{24,128},{136,144},{144,136},{0,152... | collective-permute-start | bytes 3932168 | tf_op jit(solution)/shard_map/ppermute | solution.py:382
  93.5 5.8 %blocks.3 = (bf16[160,4096]{1,0:T(8,128)(2,1)}, bf16[160,4096]{1,0:T(8,128)(2,1)}) custom-call(bf16[160,512]{1,0:T(8,128)(2,1)} %get-tuple-element.40.refs_2_.first, bf16[160,512]{1,0:T(8,128)(2,1)} %copy-done.8, bf16[4096,512]{1,0:T(8,128)(2,1)} %all-gather.2.cloned.1.call-done.weight, bf16[160,4096]{1,0:T(8,128)(2,1)} %get-tuple-element.49.after), custom_call_target="tpu_custom_call" | custom-call | flops 1 | bytes 1 | tf_op jit(solution)/shard_map/blocks/pallas_call | solution.py:257
  99.3 0.5 collective-permute-start.13
  99.8 0.0 collective-permute-done.11
  99.8 0.0 collective-permute-done.10
  99.9 11.9 %all_to_all.26 = bf16[8,16,512]{2,1,0:T(8,128)(2,1)S(1)} all-to-all(bf16[8,16,512]{2,1,0:T(8,128)(2,1)S(1)} %pad_maximum_fusion), channel_id=1, replica_groups=mesh['xh'=2,'y'=4,'c'=2,'xl'=2,'z'=8] {'z'}, dimensions={0} | all-to-all | bytes 262144 | tf_op jit(solution)/shard_map/all_to_all | solution.py:400
  111.8 0.0 collective-permute-done.14.refs_2_
  111.8 0.7 broadcast_in_dim.11
  112.6 6.6 %all-to-all-start.4 = ((bf16[16,16,512]{2,1,0:T(8,128)(2,1)}), bf16[16,16,512]{2,1,0:T(8,128)(2,1)S(1)}, u32[]{:S(2)}, u32[]{:S(2)}) async-start(bf16[16,16,512]{2,1,0:T(8,128)(2,1)} %broadcast_in_dim.11), calls=%async_computation.4 | async-start | bytes 524288 | tf_op jit(solution)/shard_map/all_to_all | solution.py:404
  119.2 0.0 collective-permute-done.13.refs_1_
  119.2 1.3 copy-done
  120.5 3.4 %assemble.2.refs_1_ = bf16[160,16384]{1,0:T(8,128)(2,1)} custom-call(s32[5]{0:T(128)S(1)} %copy-done.1, bf16[160,4096]{1,0:T(8,128)(2,1)S(1)} %copy-done, bf16[160,4096]{1,0:T(8,128)(2,1)} %collective-permute-done.13.refs_1_, bf16[160,4096]{1,0:T(8,128)(2,1)S(1)} %collective-permute-done.14.refs_2_), custom_call_target="tpu_custom_call" | custom-call | flops 1 | bytes 1 | tf_op jit(solution)/shard_map/assemble/pallas_call | solution.py:297
  124.0 0.4 collective-permute-done.6.refs_0_
  124.4 1.7 %assemble.3 = bf16[160,16384]{1,0:T(8,128)(2,1)} custom-call(s32[5]{0:T(128)S(1)} %copy-done.1, bf16[160,4096]{1,0:T(8,128)(2,1)S(1)} %collective-permute-done.6.refs_0_, bf16[160,16384]{1,0:T(8,128)(2,1)} %assemble.2.refs_1_), custom_call_target="tpu_custom_call", output_to_operand_aliasing={{}: (2, {})} | custom-call | flops 1 | bytes 1 | tf_op jit(solution)/shard_map/assemble/pallas_call | solution.py:297
  126.0 1.8 %all-to-all-done.4 = bf16[16,16,512]{2,1,0:T(8,128)(2,1)S(1)} async-done(((bf16[16,16,512]{2,1,0:T(8,128)(2,1)}), bf16[16,16,512]{2,1,0:T(8,128)(2,1)S(1)}, u32[]{:S(2)}, u32[]{:S(2)}) %all-to-all-start.4) | async-done | bytes 262176 | tf_op jit(solution)/shard_map/all_to_all | solution.py:404
  127.9 0.1 convert_multiply_fusion
  127.9 0.7 slice.23
  128.7 0.1 copy.14
  128.8 0.7 copy.15
  (34 shorter events, 0.3 us)
Async XLA Ops:
  7.2 69.6 %all-gather.2.cloned.1.call-start = ((), (), s32[]{:S(2)}) async-start(), calls=%async_computation.5 | async-start | bytes 4718592 | tf_op jit(solution)/shard_map/all_gather | solution.py:337
  32.1 1.3 copy-start.3
  33.3 4.3 %copy-start.9 = (s32[1,160]{1,0:T(1,128)S(1)}, s32[1,160]{1,0:T(1,128)}, u32[]{:S(2)}) copy-start(s32[1,160]{1,0:T(1,128)} %param.10) | copy-start | bytes 1924
  33.3 22.3 %all-to-all-start.1 = ((bf16[4,16,64,128]{3,2,1,0:T(8,128)(2,1)}), bf16[4,16,64,128]{3,2,1,0:T(8,128)(2,1)S(1)}, u32[]{:S(2)}, u32[]{:S(2)}) async-start(bf16[4,16,64,128]{3,2,1,0:T(8,128)(2,1)} %broadcast_in_dim.9), calls=%async_computation.1 | async-start | bytes 2097152 | tf_op jit(solution)/shard_map/all_to_all | solution.py:359
  42.2 10.6 %copy-start.6 = (bf16[160,512]{1,0:T(8,128)(2,1)S(1)}, bf16[160,512]{1,0:T(8,128)(2,1)}, u32[]{:S(2)}) copy-start(bf16[160,512]{1,0:T(8,128)(2,1)} %get-tuple-element.40.refs_2_.first) | copy-start | bytes 491524
  47.8 7.9 %collective-permute-start = (bf16[64,4096]{1,0:T(8,128)(2,1)}, bf16[64,4096]{1,0:T(8,128)(2,1)S(1)}, u32[]{:S(2)}, u32[]{:S(2)}) collective-permute-start(bf16[64,4096]{1,0:T(8,128)(2,1)} %get-tuple-element.35), channel_id=1, source_target_pairs={{0,16},{16,0},{1,17},{17,1},{2,18},{18,2},{3,19},{19,3},{4,20},{20... | collective-permute-start | bytes 1572872 | tf_op jit(solution)/shard_map/ppermute | solution.py:356
  52.6 3.0 %collective-permute-start.1 = (bf16[64,4096]{1,0:T(8,128)(2,1)}, bf16[64,4096]{1,0:T(8,128)(2,1)S(1)}, u32[]{:S(2)}, u32[]{:S(2)}) collective-permute-start(bf16[64,4096]{1,0:T(8,128)(2,1)} %get-tuple-element.36), channel_id=1, source_target_pairs={{0,16},{16,0},{1,17},{17,1},{2,18},{18,2},{3,19},{19,3},{4,20},{20... | collective-permute-start | bytes 1572872 | tf_op jit(solution)/shard_map/ppermute | solution.py:356
  52.7 5.5 %collective-permute-start.2 = (bf16[160,512]{1,0:T(8,128)(2,1)S(1)}, bf16[160,512]{1,0:T(8,128)(2,1)S(1)}, u32[]{:S(2)}, u32[]{:S(2)}) collective-permute-start(bf16[160,512]{1,0:T(8,128)(2,1)S(1)} %copy-done.6), channel_id=1, source_target_pairs={{0,16},{16,0},{1,17},{17,1},{2,18},{18,2},{3,19},{19,3},{4,20},{20... | collective-permute-start | bytes 491528 | tf_op jit(solution)/shard_map/ppermute | solution.py:349
  53.2 5.1 %collective-permute-start.3 = (bf16[160,512]{1,0:T(8,128)(2,1)S(1)}, bf16[160,512]{1,0:T(8,128)(2,1)}, u32[]{:S(2)}, u32[]{:S(2)}) collective-permute-start(bf16[160,512]{1,0:T(8,128)(2,1)S(1)} %copy-done.6), channel_id=1, source_target_pairs={{0,8},{16,152},{8,128},{24,16},{128,136},{144,24},{136,0},{152,144... | collective-permute-start | bytes 491528 | tf_op jit(solution)/shard_map/ppermute | solution.py:350
  54.4 5.1 %collective-permute-start.4 = (bf16[160,512]{1,0:T(8,128)(2,1)S(1)}, bf16[160,512]{1,0:T(8,128)(2,1)}, u32[]{:S(2)}, u32[]{:S(2)}) collective-permute-start(bf16[160,512]{1,0:T(8,128)(2,1)S(1)} %copy-done.6), channel_id=1, source_target_pairs={{0,152},{16,8},{8,16},{24,128},{128,24},{144,136},{136,144},{152,0... | collective-permute-start | bytes 491528 | tf_op jit(solution)/shard_map/ppermute | solution.py:351
  55.7 2.3 %copy-start.2 = (bf16[4,16,64,128]{3,2,1,0:T(8,128)(2,1)}, bf16[4,16,64,128]{3,2,1,0:T(8,128)(2,1)S(1)}, u32[]{:S(2)}) copy-start(bf16[4,16,64,128]{3,2,1,0:T(8,128)(2,1)S(1)} %all-to-all-done.1.refs_0_) | copy-start | bytes 3145732
  55.7 7.3 %collective-permute-start.5 = (bf16[4,16,64,128]{3,2,1,0:T(8,128)(2,1)S(1)}, bf16[4,16,64,128]{3,2,1,0:T(8,128)(2,1)S(1)}, u32[]{:S(2)}, u32[]{:S(2)}) collective-permute-start(bf16[4,16,64,128]{3,2,1,0:T(8,128)(2,1)S(1)} %all-to-all-done.1.refs_0_), channel_id=1, source_target_pairs={{0,16},{16,0},{1,17},{17,1},{2,18},{18,2},{3,19},{19,3},{4,20},{20... | collective-permute-start | bytes 3145736 | tf_op jit(solution)/shard_map/ppermute | solution.py:361
  56.5 1.6 %copy-start.5 = (f32[64,4096]{1,0:T(8,128)S(1)}, f32[64,4096]{1,0:T(8,128)}, u32[]{:S(2)}) copy-start(f32[64,4096]{1,0:T(8,128)} %get-tuple-element.38) | copy-start | bytes 3145732
  58.3 1.3 copy-start.8
  59.5 22.9 %collective-permute-start.7 = (bf16[32,4096]{1,0:T(8,128)(2,1)S(1)}, bf16[32,4096]{1,0:T(8,128)(2,1)S(1)}, u32[]{:S(2)}, u32[]{:S(2)}) collective-permute-start(bf16[32,4096]{1,0:T(8,128)(2,1)S(1)} %fusion.3), channel_id=1, source_target_pairs={{0,128},{8,136},{128,0},{136,8},{1,129},{9,137},{129,1},{137,9},{2... | collective-permute-start | bytes 786440 | tf_op jit(solution)/shard_map/ppermute | solution.py:371
  62.0 20.4 %collective-permute-start.8 = (bf16[32,4096]{1,0:T(8,128)(2,1)S(1)}, bf16[32,4096]{1,0:T(8,128)(2,1)S(1)}, u32[]{:S(2)}, u32[]{:S(2)}) collective-permute-start(bf16[32,4096]{1,0:T(8,128)(2,1)S(1)} %get-tuple-element.47), channel_id=1, source_target_pairs={{0,8},{8,0},{128,136},{136,128},{1,9},{9,1},{129,137},{137,129},{2... | collective-permute-start | bytes 786440 | tf_op jit(solution)/shard_map/ppermute | solution.py:371
  62.9 19.6 %collective-permute-start.9 = (bf16[32,4096]{1,0:T(8,128)(2,1)S(1)}, bf16[32,4096]{1,0:T(8,128)(2,1)}, u32[]{:S(2)}, u32[]{:S(2)}) collective-permute-start(bf16[32,4096]{1,0:T(8,128)(2,1)S(1)} %get-tuple-element.48), channel_id=1, source_target_pairs={{0,136},{8,128},{128,8},{136,0},{1,137},{9,129},{129,9},{137,1},{2... | collective-permute-start | bytes 786440 | tf_op jit(solution)/shard_map/ppermute | solution.py:371
  62.9 1.0 copy-start.4
  70.7 12.5 %all-to-all-start.2 = ((bf16[8,64,256]{2,1,0:T(8,128)(2,1)}), bf16[8,64,256]{2,1,0:T(8,128)(2,1)S(1)}, u32[]{:S(2)}, u32[]{:S(2)}) async-start(bf16[8,64,256]{2,1,0:T(8,128)(2,1)} %up.5.after), calls=%async_computation.2 | async-start | bytes 524288 | tf_op jit(solution)/shard_map/all_to_all | solution.py:385
  82.5 0.7 copy-start.7
  85.1 14.2 %collective-permute-start.12 = (bf16[8,4608]{1,0:T(8,128)(2,1)}, bf16[8,4608]{1,0:T(8,128)(2,1)S(1)}, u32[]{:S(2)}, u32[]{:S(2)}) collective-permute-start(bf16[8,4608]{1,0:T(8,128)(2,1)} %get-tuple-element.63), channel_id=1, source_target_pairs={{0,64},{32,96},{64,0},{96,32},{1,65},{33,97},{65,1},{97,33},{2,66}... | collective-permute-start | bytes 221192 | tf_op jit(solution)/shard_map/ppermute | solution.py:393
  88.3 11.4 %collective-permute-start.11 = (bf16[8,4608]{1,0:T(8,128)(2,1)}, bf16[8,4608]{1,0:T(8,128)(2,1)S(1)}, u32[]{:S(2)}, u32[]{:S(2)}) collective-permute-start(bf16[8,4608]{1,0:T(8,128)(2,1)} %get-tuple-element.62), channel_id=1, source_target_pairs={{0,96},{32,0},{64,32},{96,64},{1,97},{33,1},{65,33},{97,65},{2,98}... | collective-permute-start | bytes 221192 | tf_op jit(solution)/shard_map/ppermute | solution.py:393
  89.2 10.6 %collective-permute-start.10 = (bf16[8,4608]{1,0:T(8,128)(2,1)S(1)}, bf16[8,4608]{1,0:T(8,128)(2,1)S(1)}, u32[]{:S(2)}, u32[]{:S(2)}) collective-permute-start(bf16[8,4608]{1,0:T(8,128)(2,1)S(1)} %get-tuple-element.61), channel_id=1, source_target_pairs={{0,32},{32,64},{64,96},{96,0},{1,33},{33,65},{65,97},{97,1},{2,34}... | collective-permute-start | bytes 221192 | tf_op jit(solution)/shard_map/ppermute | solution.py:393
  89.8 22.0 %collective-permute-start.14 = (bf16[160,4096]{1,0:T(8,128)(2,1)}, bf16[160,4096]{1,0:T(8,128)(2,1)S(1)}, u32[]{:S(2)}, u32[]{:S(2)}) collective-permute-start(bf16[160,4096]{1,0:T(8,128)(2,1)} %get-tuple-element.49.after), channel_id=1, source_target_pairs={{8,0},{152,16},{128,8},{16,24},{136,128},{24,144},{0,136},{144,152... | collective-permute-start | bytes 3932168 | tf_op jit(solution)/shard_map/ppermute | solution.py:381
  91.2 33.2 %collective-permute-start.6 = (bf16[160,4096]{1,0:T(8,128)(2,1)}, bf16[160,4096]{1,0:T(8,128)(2,1)S(1)}, u32[]{:S(2)}, u32[]{:S(2)}) collective-permute-start(bf16[160,4096]{1,0:T(8,128)(2,1)} %get-tuple-element.45), channel_id=1, source_target_pairs={{152,0},{8,16},{16,8},{128,24},{24,128},{136,144},{144,136},{0,152... | collective-permute-start | bytes 3932168 | tf_op jit(solution)/shard_map/ppermute | solution.py:382
  99.2 20.0 %copy-start.1 = (s32[5]{0:T(128)S(1)}, s32[5]{0:T(128)}, u32[]{:S(2)}) copy-start(s32[5]{0:T(128)} %stack.23.idx) | copy-start | bytes 64
  99.3 19.9 %collective-permute-start.13 = (bf16[160,4096]{1,0:T(8,128)(2,1)}, bf16[160,4096]{1,0:T(8,128)(2,1)}, u32[]{:S(2)}, u32[]{:S(2)}) collective-permute-start(bf16[160,4096]{1,0:T(8,128)(2,1)} %get-tuple-element.57), channel_id=1, source_target_pairs={{0,16},{16,0},{1,17},{17,1},{2,18},{18,2},{3,19},{19,3},{4,20},{20... | collective-permute-start | bytes 3932168 | tf_op jit(solution)/shard_map/ppermute | solution.py:380
  112.6 15.3 %all-to-all-start.4 = ((bf16[16,16,512]{2,1,0:T(8,128)(2,1)}), bf16[16,16,512]{2,1,0:T(8,128)(2,1)S(1)}, u32[]{:S(2)}, u32[]{:S(2)}) async-start(bf16[16,16,512]{2,1,0:T(8,128)(2,1)} %broadcast_in_dim.11), calls=%async_computation.4 | async-start | bytes 524288 | tf_op jit(solution)/shard_map/all_to_all | solution.py:404
  119.2 1.3 copy-start
Sparse Core Ops, SparseCore 0:
  12.4 60.8 all-gather.1
